TPU v7x, 32 devices: a whole 2x2x4 slice. The times are simulated.
32 devices in a mesh: dp: 16 (over z, y, x), tensor: 2 (over core).
Axes of the slice: x: 2, y: 2, z: 4, core: 2. Of those that a mesh axis runs over, the one named last changes fastest.
Arguments:
- tokens: bfloat16 [4096, 2048], P('dp', 'tensor'), may hold values from -6 to 6
- cotangent: bfloat16 [4096, 2048], P('dp', 'tensor'), may hold values from -6 to 6
- lengths: int32 [32], replicated, may hold values from 64 to 192, as said below
- order: int32 [32], replicated, may hold values from 0 to 31, as said below
- attn_gain: bfloat16 [2048], P('tensor'), may hold values from 0.5 to 1.5
- w_query: bfloat16 [2048, 2048], P('dp', 'tensor'), may hold values from -0.125 to 0.125
- w_key: bfloat16 [2048, 1024], P('dp', 'tensor'), may hold values from -0.125 to 0.125
- w_value: bfloat16 [2048, 1024], P('dp', 'tensor'), may hold values from -0.125 to 0.125
- w_output: bfloat16 [2048, 2048], P('tensor', 'dp'), may hold values from -0.75 to 0.75
- ffn_gain: bfloat16 [2048], P('tensor'), may hold values from 0.5 to 1.5
- w_gate: bfloat16 [2048, 8192], P('dp', 'tensor'), may hold values from -0.125 to 0.125
- w_up: bfloat16 [2048, 8192], P('dp', 'tensor'), may hold values from -0.125 to 0.125
- w_down: bfloat16 [8192, 2048], P('tensor', 'dp'), may hold values from -0.0625 to 0.0625
Outputs:
- output: bfloat16 [4096, 2048], P('dp', 'tensor')
- tokens_grad: bfloat16 [4096, 2048], P('dp', 'tensor')
- attn_gain_grad: float32 [2, 1024], P('tensor', 'dp')
- query_grad: float32 [2048, 2048], P('dp', 'tensor')
- key_grad: float32 [2048, 1024], P('dp', 'tensor')
- value_grad: float32 [2048, 1024], P('dp', 'tensor')
- out_proj_grad: float32 [2048, 2048], P('tensor', 'dp')
- ffn_gain_grad: float32 [2, 1024], P('tensor', 'dp')
- gate_grad: float32 [2048, 8192], P('dp', 'tensor')
- up_grad: float32 [2048, 8192], P('dp', 'tensor')
- down_grad: float32 [8192, 2048], P('tensor', 'dp')
Inputs may be any that keep to these rules, and one draw needn't show every extreme that they name: `lengths`: sequences order[2g] and order[2g+1] form data group g and have 256 tokens together; sequences lie in input order, each after the one before it. `order`: A permutation of the 32 sequence numbers.
All inputs are finite; a program needn't handle non-finite values.
Results may differ from a plain program's by a relative error of at most 0.015.
Values may be sent and summed in bfloat16 or wider, within the bound.
A program may use at most 320 MiB of HBM per device.

v0:
```python
import jax
import jax.numpy as jnp
from jax import lax
from jax.sharding import PartitionSpec as P

HD = 256


EPSILON = 1e-06
ROPE_BASE = 1000042.0


def matmul(left, right):
    return jnp.dot(left, right, preferred_element_type=jnp.float32)


def matmul_t(left, right):
    return lax.dot_general(
        left, right, (((1,), (1,)), ((), ())), preferred_element_type=jnp.float32
    )


def t_matmul(left, right):
    return lax.dot_general(
        left, right, (((0,), (0,)), ((), ())), preferred_element_type=jnp.float32
    )


def rotary_tables(positions):
    exponents = jnp.arange(0, HD, 2).astype(jnp.float32) / HD
    inverse = jnp.power(jnp.float32(ROPE_BASE), -exponents)
    angles = positions.astype(jnp.float32)[:, None] * inverse[None, :]
    angles = jnp.concatenate([angles, angles], axis=1)
    return (jnp.cos(angles), jnp.sin(angles))


def rotate(vectors, cosine, sine):
    middle = vectors.shape[-1] // 2
    turned = jnp.concatenate([-vectors[..., middle:], vectors[..., :middle]], axis=-1)
    return vectors * cosine + turned * sine


def rotate_back(grads, cosine, sine):
    middle = grads.shape[-1] // 2
    scaled = grads * sine
    turned = jnp.concatenate([scaled[..., middle:], -scaled[..., :middle]], axis=-1)
    return grads * cosine + turned


def masked_scores(queries_rot, keys_rot, allowed):
    raw = jnp.einsum(
        "qgrd,kgd->grqk", queries_rot, keys_rot, preferred_element_type=jnp.float32
    ) * HD ** (-0.5)
    return jnp.where(allowed[None, None], raw, -1e30)


def on_device(
    tokens,
    cotangent,
    lengths,
    order,
    attn_gain,
    w_query,
    w_key,
    w_value,
    w_output,
    ffn_gain,
    w_gate,
    w_up,
    w_down,
):
    group_index = lax.axis_index("dp")
    half_index = lax.axis_index("tensor")
    tensor_count = lax.axis_size("tensor")
    tok_group = tokens.shape[0]
    half_width = tokens.shape[1]
    width = half_width * tensor_count
    seq_count = lengths.shape[0]
    group_count = seq_count // 2
    seq_ids = jnp.arange(seq_count)
    in_start = jnp.cumsum(lengths) - lengths
    matches = order[:, None] == seq_ids[None, :]
    work_len = jnp.sum(jnp.where(matches, lengths[None, :], 0), axis=1)
    work_src = jnp.sum(jnp.where(matches, in_start[None, :], 0), axis=1)
    pair_len = work_len.reshape(group_count, 2)
    pair_start = jnp.cumsum(pair_len, axis=1) - pair_len
    pair_src = work_src.reshape(group_count, 2)
    mine = jnp.arange(group_count)[:, None] == group_index
    my_start = jnp.sum(jnp.where(mine, pair_start, 0), axis=0)
    my_src = jnp.sum(jnp.where(mine, pair_src, 0), axis=0)
    row_ids = jnp.arange(tok_group)
    slot_ids = jnp.sum((row_ids[:, None] >= my_start[None, :]).astype(jnp.int32), axis=1) - 1
    chosen = slot_ids[:, None] == jnp.arange(2)[None, :]
    positions = row_ids - jnp.sum(jnp.where(chosen, my_start[None, :], 0), axis=1)
    sources = jnp.sum(jnp.where(chosen, my_src[None, :], 0), axis=1) + positions
    global_rows = group_index * tok_group + row_ids
    seq_of_row = jnp.sum((global_rows[:, None] >= in_start[None, :]).astype(jnp.int32), axis=1) - 1
    slot_global = seq_ids // 2 * tok_group + pair_start.reshape(-1)
    seq_global = jnp.sum(jnp.where(matches, slot_global[:, None], 0), axis=0)
    shift_table = seq_global - in_start
    onehot_seq = seq_of_row[:, None] == seq_ids[None, :]
    targets = global_rows + jnp.sum(jnp.where(onehot_seq, shift_table[None, :], 0), axis=1)
    empty = jnp.zeros((tok_group, half_width), jnp.bfloat16)
    totals = (empty, empty)
    piece_tokens = lax.all_gather(tokens, "dp", axis=0, tiled=True)
    piece_cot = lax.all_gather(cotangent, "dp", axis=0, tiled=True)
    local = sources
    inside = (local >= 0) & (local < piece_tokens.shape[0])
    safe = jnp.clip(local, 0, piece_tokens.shape[0] - 1)
    tokens_half = jnp.where(inside[:, None], piece_tokens[safe], totals[0])
    cot_half = jnp.where(inside[:, None], piece_cot[safe], totals[1])
    tokens_full, cot_full, gain_one, gain_two = (
        lax.all_gather(tokens_half, "tensor", axis=1, tiled=True),
        lax.all_gather(cot_half, "tensor", axis=1, tiled=True),
        lax.all_gather(attn_gain, "tensor", axis=0, tiled=True),
        lax.all_gather(ffn_gain, "tensor", axis=0, tiled=True),
    )
    gain_one = gain_one.astype(jnp.float32)
    gain_two = gain_two.astype(jnp.float32)
    tokens_wide = tokens_full.astype(jnp.float32)
    rms_one = lax.rsqrt(jnp.mean(tokens_wide * tokens_wide, axis=-1, keepdims=True) + EPSILON)
    normed_attn = (tokens_wide * rms_one * gain_one).astype(jnp.bfloat16)
    attn_fwd = (
        lax.all_gather(w_query, "dp", axis=0, tiled=True),
        lax.all_gather(w_key, "dp", axis=0, tiled=True),
        lax.all_gather(w_value, "dp", axis=0, tiled=True),
        lax.all_gather(w_output, "dp", axis=1, tiled=True),
    )
    query_full, key_full, value_full, output_full = attn_fwd
    kv_local = key_full.shape[1] // HD
    repeats = query_full.shape[1] // key_full.shape[1]
    cosine, sine = rotary_tables(positions)
    cos_four = cosine[:, None, None, :]
    sin_four = sine[:, None, None, :]
    cos_three = cosine[:, None, :]
    sin_three = sine[:, None, :]
    queries = matmul(normed_attn, query_full).reshape(tok_group, kv_local, repeats, HD)
    keys = matmul(normed_attn, key_full).reshape(tok_group, kv_local, HD)
    queries_rot = rotate(queries, cos_four, sin_four).astype(jnp.bfloat16)
    keys_rot = rotate(keys, cos_three, sin_three).astype(jnp.bfloat16)
    values = matmul(normed_attn, value_full).astype(jnp.bfloat16).reshape(tok_group, kv_local, HD)
    allowed = (slot_ids[:, None] == slot_ids[None, :]) & (row_ids[:, None] >= row_ids[None, :])
    scores = masked_scores(queries_rot, keys_rot, allowed)
    highest = jnp.max(scores, axis=-1, keepdims=True)
    log_total = highest + jnp.log(jnp.sum(jnp.exp(scores - highest), axis=-1, keepdims=True))
    probs_low = jnp.exp(scores - log_total).astype(jnp.bfloat16)
    attended = jnp.einsum("grqk,kgd->qgrd", probs_low, values, preferred_element_type=jnp.float32)
    attended = attended.astype(jnp.bfloat16).reshape(tok_group, kv_local * repeats * HD)
    attn_out = lax.psum(matmul(attended, output_full), "tensor")
    mixed = tokens_wide + attn_out
    rms_two = lax.rsqrt(jnp.mean(mixed * mixed, axis=-1, keepdims=True) + EPSILON)
    normed_ffn = (mixed * rms_two * gain_two).astype(jnp.bfloat16)
    ffn_fwd = (
        lax.all_gather(w_gate, "dp", axis=0, tiled=True),
        lax.all_gather(w_up, "dp", axis=0, tiled=True),
        lax.all_gather(w_down, "dp", axis=1, tiled=True),
    )
    gate_full, up_full, down_full = ffn_fwd
    gate = matmul(normed_ffn, gate_full)
    upward = matmul(normed_ffn, up_full)
    sigmoid = jax.nn.sigmoid(gate)
    silu_gate = gate * sigmoid
    hidden = (silu_gate * upward).astype(jnp.bfloat16)
    ffn_half = lax.psum_scatter(
        matmul(hidden, down_full).astype(jnp.bfloat16), "tensor", scatter_dimension=1, tiled=True
    ).astype(jnp.float32)
    mixed_half = lax.dynamic_slice_in_dim(mixed, half_index * half_width, half_width, 1)
    output_work = (mixed_half + ffn_half).astype(jnp.bfloat16)
    gate_back, up_back, down_back = (
        lax.all_gather(w_gate, "dp", axis=0, tiled=True),
        lax.all_gather(w_up, "dp", axis=0, tiled=True),
        lax.all_gather(w_down, "dp", axis=1, tiled=True),
    )
    cot_wide = cot_full.astype(jnp.float32)
    hidden_grad = matmul_t(cot_full, down_back)
    gate_act_grad = (hidden_grad * upward * sigmoid * (1.0 + gate * (1.0 - sigmoid))).astype(
        jnp.bfloat16
    )
    up_act_grad = (hidden_grad * silu_gate).astype(jnp.bfloat16)
    down_local = t_matmul(hidden, cot_full)
    gate_local = t_matmul(normed_ffn, gate_act_grad)
    up_local = t_matmul(normed_ffn, up_act_grad)
    normed_ffn_grad = lax.psum(
        matmul_t(gate_act_grad, gate_back) + matmul_t(up_act_grad, up_back), "tensor"
    )
    ffn_gain_local = jnp.sum(normed_ffn_grad * mixed * rms_two, axis=0)
    inner_two = jnp.sum(normed_ffn_grad * gain_two * mixed, axis=-1, keepdims=True)
    mixed_grad = (
        cot_wide
        + rms_two * gain_two * normed_ffn_grad
        - mixed * rms_two * rms_two * rms_two * inner_two / width
    )
    ffn_gain_half = lax.dynamic_slice_in_dim(
        ffn_gain_local, half_index * half_width, half_width, 0
    ).reshape(1, half_width)
    gate_grad, up_grad, down_grad, ffn_gain_grad = (
        lax.psum_scatter(gate_local, "dp", scatter_dimension=0, tiled=True),
        lax.psum_scatter(up_local, "dp", scatter_dimension=0, tiled=True),
        lax.psum_scatter(down_local, "dp", scatter_dimension=1, tiled=True),
        lax.psum_scatter(ffn_gain_half, "dp", scatter_dimension=1, tiled=True),
    )
    query_back, key_back, value_back, output_back = (
        lax.all_gather(w_query, "dp", axis=0, tiled=True),
        lax.all_gather(w_key, "dp", axis=0, tiled=True),
        lax.all_gather(w_value, "dp", axis=0, tiled=True),
        lax.all_gather(w_output, "dp", axis=1, tiled=True),
    )
    attn_out_grad = mixed_grad.astype(jnp.bfloat16)
    out_local = t_matmul(attended, attn_out_grad)
    attended_grad = (
        matmul_t(attn_out_grad, output_back)
        .astype(jnp.bfloat16)
        .reshape(tok_group, kv_local, repeats, HD)
    )
    scores_again = masked_scores(queries_rot, keys_rot, allowed)
    probs = jnp.exp(scores_again - log_total)
    probs_again = probs.astype(jnp.bfloat16)
    values_grad = jnp.einsum(
        "grqk,qgrd->kgd", probs_again, attended_grad, preferred_element_type=jnp.float32
    )
    values_grad = values_grad.astype(jnp.bfloat16).reshape(tok_group, kv_local * HD)
    probs_grad = jnp.einsum(
        "qgrd,kgd->grqk", attended_grad, values, preferred_element_type=jnp.float32
    )
    scores_grad = (
        probs * (probs_grad - jnp.sum(probs * probs_grad, axis=-1, keepdims=True))
    ).astype(jnp.bfloat16)
    rot_q_grad = jnp.einsum(
        "grqk,kgd->qgrd", scores_grad, keys_rot, preferred_element_type=jnp.float32
    ) * HD ** (-0.5)
    rot_k_grad = jnp.einsum(
        "grqk,qgrd->kgd", scores_grad, queries_rot, preferred_element_type=jnp.float32
    ) * HD ** (-0.5)
    queries_grad = (
        rotate_back(rot_q_grad, cos_four, sin_four)
        .astype(jnp.bfloat16)
        .reshape(tok_group, kv_local * repeats * HD)
    )
    keys_grad = (
        rotate_back(rot_k_grad, cos_three, sin_three)
        .astype(jnp.bfloat16)
        .reshape(tok_group, kv_local * HD)
    )
    query_local = t_matmul(normed_attn, queries_grad)
    key_local = t_matmul(normed_attn, keys_grad)
    value_local = t_matmul(normed_attn, values_grad)
    normed_attn_grad = lax.psum(
        (
            matmul_t(queries_grad, query_back)
            + matmul_t(keys_grad, key_back)
            + matmul_t(values_grad, value_back)
        ).astype(jnp.bfloat16),
        "tensor",
    ).astype(jnp.float32)
    attn_gain_local = jnp.sum(normed_attn_grad * tokens_wide * rms_one, axis=0)
    inner_one = jnp.sum(normed_attn_grad * gain_one * tokens_wide, axis=-1, keepdims=True)
    work_grad = (
        mixed_grad
        + rms_one * gain_one * normed_attn_grad
        - tokens_wide * rms_one * rms_one * rms_one * inner_one / width
    )
    grad_work = lax.dynamic_slice_in_dim(work_grad, half_index * half_width, half_width, 1).astype(
        jnp.bfloat16
    )
    attn_gain_half = lax.dynamic_slice_in_dim(
        attn_gain_local, half_index * half_width, half_width, 0
    ).reshape(1, half_width)
    query_grad, key_grad, value_grad, out_proj_grad, attn_gain_grad = (
        lax.psum_scatter(query_local, "dp", scatter_dimension=0, tiled=True),
        lax.psum_scatter(key_local, "dp", scatter_dimension=0, tiled=True),
        lax.psum_scatter(value_local, "dp", scatter_dimension=0, tiled=True),
        lax.psum_scatter(out_local, "dp", scatter_dimension=1, tiled=True),
        lax.psum_scatter(attn_gain_half, "dp", scatter_dimension=1, tiled=True),
    )
    totals = (empty, empty)
    piece_out = lax.all_gather(output_work, "dp", axis=0, tiled=True)
    piece_grad = lax.all_gather(grad_work, "dp", axis=0, tiled=True)
    local = targets
    inside = (local >= 0) & (local < piece_out.shape[0])
    safe = jnp.clip(local, 0, piece_out.shape[0] - 1)
    output = jnp.where(inside[:, None], piece_out[safe], totals[0])
    tokens_grad = jnp.where(inside[:, None], piece_grad[safe], totals[1])
    return (
        output,
        tokens_grad,
        attn_gain_grad,
        query_grad,
        key_grad,
        value_grad,
        out_proj_grad,
        ffn_gain_grad,
        gate_grad,
        up_grad,
        down_grad,
    )


def solution(mesh):
    return jax.shard_map(
        on_device,
        mesh=mesh,
        in_specs=(
            P("dp", "tensor"),
            P("dp", "tensor"),
            P(),
            P(),
            P("tensor"),
            P("dp", "tensor"),
            P("dp", "tensor"),
            P("dp", "tensor"),
            P("tensor", "dp"),
            P("tensor"),
            P("dp", "tensor"),
            P("dp", "tensor"),
            P("tensor", "dp"),
        ),
        out_specs=(
            P("dp", "tensor"),
            P("dp", "tensor"),
            P("tensor", "dp"),
            P("dp", "tensor"),
            P("dp", "tensor"),
            P("dp", "tensor"),
            P("tensor", "dp"),
            P("tensor", "dp"),
            P("dp", "tensor"),
            P("dp", "tensor"),
            P("tensor", "dp"),
        ),
        check_vma=False,
    )
```

profile of v0, /device:TPU:2, one launch (start us, length us, event | category | flops | bytes accessed | tf_op | source)
XLA Modules:
  0.0 4357.5 jit_solution(5426914320081235344)
XLA Ops:
  13.6 111.1 %all-gather.34.cloned.1.call-done = bf16[4096,1024]{1,0:T(8,128)(2,1)} async-done(((bf16[256,1024]{1,0:T(8,128)(2,1)}), bf16[4096,1024]{1,0:T(8,128)(2,1)}) %all-gather.34.cloned.1.call-update) | async-done | bytes 8388624 | tf_op jit(solution)/shard_map/all_gather | solution.py:106
  130.7 107.8 %all-gather.14.cloned.1.call-done = bf16[4096,1024]{1,0:T(8,128)(2,1)} async-done(((bf16[256,1024]{1,0:T(8,128)(2,1)}), bf16[4096,1024]{1,0:T(8,128)(2,1)}) %all-gather.14.cloned.1.call-update) | async-done | bytes 8388624 | tf_op jit(solution)/shard_map/all_gather | solution.py:105
  255.0 62.6 %all-gather.18.cloned.1.call-done = bf16[2048,512]{1,0:T(8,128)(2,1)} async-done(((bf16[128,512]{1,0:T(8,128)(2,1)}), bf16[2048,512]{1,0:T(8,128)(2,1)}) %all-gather.18.cloned.1.call-update) | async-done | bytes 2097168 | tf_op jit(solution)/shard_map/all_gather | solution.py:126
  320.4 59.2 %all-gather.20.cloned.1.call-done = bf16[2048,512]{1,0:T(8,128)(2,1)} async-done(((bf16[128,512]{1,0:T(8,128)(2,1)}), bf16[2048,512]{1,0:T(8,128)(2,1)}) %all-gather.20.cloned.1.call-update) | async-done | bytes 2097168 | tf_op jit(solution)/shard_map/all_gather | solution.py:125
  382.4 74.8 %all-gather.22.cloned.1.call-done = bf16[2048,1024]{1,0:T(8,128)(2,1)} async-done(((bf16[128,1024]{1,0:T(8,128)(2,1)}), bf16[2048,1024]{1,0:T(8,128)(2,1)}) %all-gather.22.cloned.1.call-update) | async-done | bytes 4194320 | tf_op jit(solution)/shard_map/all_gather | solution.py:124
  464.0 83.7 %all-gather.24.cloned.1.call-done = bf16[1024,2048]{1,0:T(8,128)(2,1)} async-done(((bf16[1024,128]{1,0:T(8,128)(2,1)}), bf16[1024,2048]{1,0:T(8,128)(2,1)}) %all-gather.24.cloned.1.call-update) | async-done | bytes 4194320 | tf_op jit(solution)/shard_map/all_gather | solution.py:127
  557.2 15.2 all-reduce.4.cloned.1.call-done
  575.5 192.5 %all-gather.26.cloned.1.call-done = bf16[2048,4096]{1,0:T(8,128)(2,1)} async-done(((bf16[128,4096]{1,0:T(8,128)(2,1)}), bf16[2048,4096]{1,0:T(8,128)(2,1)}) %all-gather.26.cloned.1.call-update) | async-done | bytes 16777232 | tf_op jit(solution)/shard_map/all_gather | solution.py:154
  768.0 12.5 fusion.45
  780.6 180.3 %all-gather.28.cloned.1.call-done = bf16[2048,4096]{1,0:T(8,128)(2,1)} async-done(((bf16[128,4096]{1,0:T(8,128)(2,1)}), bf16[2048,4096]{1,0:T(8,128)(2,1)}) %all-gather.28.cloned.1.call-update) | async-done | bytes 16777232 | tf_op jit(solution)/shard_map/all_gather | solution.py:155
  960.9 12.6 fusion.46
  973.4 250.6 %all-gather.30.cloned.1.call-done = bf16[4096,2048]{1,0:T(8,128)(2,1)} async-done(((bf16[4096,128]{1,0:T(8,128)(2,1)}), bf16[4096,2048]{1,0:T(8,128)(2,1)}) %all-gather.30.cloned.1.call-update) | async-done | bytes 16777232 | tf_op jit(solution)/shard_map/all_gather | solution.py:156
  1224.1 13.7 multiply_convert_fusion
  1237.8 12.2 fusion.47
  1250.0 12.8 convolution_add_fusion.2
  1263.1 19.6 all-reduce.6.cloned.1.call-done
  1304.1 11.9 convolution_convert_fusion
  1317.3 7.7 all-reduce.8.cloned.1.call-done
  1329.6 7.3 reduce-scatter.15.cloned.1.call-done
  1363.2 13.2 fusion.49
  1378.0 13.2 fusion.50
  1393.1 13.3 fusion.51
  1413.4 73.7 %reduce-scatter.31.cloned.1.call-done = f32[64,1]{1,0:T(8,128)} async-done(((f32[1024,1]{1,0:T(8,128)}), f32[64,1]{1,0:T(8,128)}) %reduce-scatter.31.cloned.1.call-update) | async-done | bytes 272
  1488.5 115.3 %all-gather.32.cloned.1.call-done = bf16[4096,1024]{1,0:T(8,128)(2,1)} async-done(((bf16[256,1024]{1,0:T(8,128)(2,1)}), bf16[4096,1024]{1,0:T(8,128)(2,1)}) %all-gather.32.cloned.1.call-update) | async-done | bytes 8388624 | tf_op jit(solution)/shard_map/all_gather | solution.py:276
  1609.8 108.4 %all-gather.38.cloned.1.call-done = bf16[4096,1024]{1,0:T(8,128)(2,1)} async-done(((bf16[256,1024]{1,0:T(8,128)(2,1)}), bf16[4096,1024]{1,0:T(8,128)(2,1)}) %all-gather.38.cloned.1.call-update) | async-done | bytes 8388624 | tf_op jit(solution)/shard_map/all_gather | solution.py:277
  1725.3 87.2 %reduce-scatter.19.cloned.1.call-done = f32[128,512]{1,0:T(8,128)} async-done(((f32[2048,512]{1,0:T(8,128)}), f32[128,512]{1,0:T(8,128)}) %reduce-scatter.19.cloned.1.call-update) | async-done | bytes 262160 | tf_op jit(solution)/shard_map/reduce_scatter | solution.py:270
  1812.5 97.6 %reduce-scatter.21.cloned.1.call-done = f32[128,512]{1,0:T(8,128)} async-done(((f32[2048,512]{1,0:T(8,128)}), f32[128,512]{1,0:T(8,128)}) %reduce-scatter.21.cloned.1.call-update) | async-done | bytes 262160 | tf_op jit(solution)/shard_map/reduce_scatter | solution.py:271
  1910.1 182.1 %reduce-scatter.17.cloned.1.call-done = f32[128,1024]{1,0:T(8,128)} async-done(((f32[2048,1024]{1,0:T(8,128)}), f32[128,1024]{1,0:T(8,128)}) %reduce-scatter.17.cloned.1.call-update) | async-done | bytes 524304 | tf_op jit(solution)/shard_map/reduce_scatter | solution.py:269
  2092.2 183.1 %reduce-scatter.23.cloned.1.call-done = f32[1024,128]{1,0:T(8,128)} async-done(((f32[1024,2048]{1,0:T(8,128)}), f32[1024,128]{1,0:T(8,128)}) %reduce-scatter.23.cloned.1.call-update) | async-done | bytes 524304 | tf_op jit(solution)/shard_map/reduce_scatter | solution.py:272
  2275.3 691.5 %reduce-scatter.25.cloned.1.call-done = f32[128,4096]{1,0:T(8,128)} async-done(((f32[2048,4096]{1,0:T(8,128)}), f32[128,4096]{1,0:T(8,128)}) %reduce-scatter.25.cloned.1.call-update) | async-done | bytes 2097168 | tf_op jit(solution)/shard_map/reduce_scatter | solution.py:197
  2966.8 692.0 %reduce-scatter.27.cloned.1.call-done = f32[128,4096]{1,0:T(8,128)} async-done(((f32[2048,4096]{1,0:T(8,128)}), f32[128,4096]{1,0:T(8,128)}) %reduce-scatter.27.cloned.1.call-update) | async-done | bytes 2097168 | tf_op jit(solution)/shard_map/reduce_scatter | solution.py:198
  3658.9 691.9 %reduce-scatter.29.cloned.1.call-done = f32[4096,128]{1,0:T(8,128)} async-done(((f32[4096,2048]{1,0:T(8,128)}), f32[4096,128]{1,0:T(8,128)}) %reduce-scatter.29.cloned.1.call-update) | async-done | bytes 2097168 | tf_op jit(solution)/shard_map/reduce_scatter | solution.py:199
  (211 shorter events, 131.9 us)
Async XLA Ops:
  7.2 117.5 %all-gather.34.cloned.1.call-start = ((), (), s32[]{:S(2)}) async-start(), calls=%async_computation.22 | async-start | bytes 8912896 | tf_op jit(solution)/shard_map/all_gather | solution.py:106
  7.9 230.6 %all-gather.14.cloned.1.call-start = ((), (), s32[]{:S(2)}) async-start(), calls=%async_computation.10 | async-start | bytes 8912896 | tf_op jit(solution)/shard_map/all_gather | solution.py:105
  8.7 244.8 %all-gather.16.cloned.1.call-start = ((), (), s32[]{:S(2)}) async-start(), calls=%async_computation.11 | async-start | bytes 1572864 | tf_op jit(solution)/shard_map/all_gather | solution.py:113
  244.5 3.7 copy-start.29
  245.7 71.9 %all-gather.18.cloned.1.call-start = ((), (), s32[]{:S(2)}) async-start(), calls=%async_computation.12 | async-start | bytes 2228224 | tf_op jit(solution)/shard_map/all_gather | solution.py:126
  246.2 133.4 %all-gather.20.cloned.1.call-start = ((), (), s32[]{:S(2)}) async-start(), calls=%async_computation.13 | async-start | bytes 2228224 | tf_op jit(solution)/shard_map/all_gather | solution.py:125
  246.8 210.4 %all-gather.22.cloned.1.call-start = ((), (), s32[]{:S(2)}) async-start(), calls=%async_computation.14 | async-start | bytes 4456448 | tf_op jit(solution)/shard_map/all_gather | solution.py:124
  247.4 300.3 %all-gather.24.cloned.1.call-start = ((), (), s32[]{:S(2)}) async-start(), calls=%async_computation.15 | async-start | bytes 4456448 | tf_op jit(solution)/shard_map/all_gather | solution.py:127
  248.2 324.2 %all-reduce.4.cloned.1.call-start = ((), (), s32[]{:S(2)}) async-start(), calls=%async_computation.16 | async-start | bytes 4194304 | tf_op jit(solution)/shard_map/psum | solution.py:149
  255.0 124.6 %copy-start = (bf16[256,2048]{1,0:T(8,128)(2,1)S(1)}, bf16[256,2048]{1,0:T(8,128)(2,1)}, u32[]{:S(2)}) copy-start(bf16[256,2048]{1,0:T(8,128)(2,1)} %all-gather.16.cloned.1.call-done) | copy-start | bytes 3145732
  320.4 142.5 %copy-start.17 = (bf16[256,2,256]{2,1,0:T(2,128)(2,1)}, bf16[256,2,256]{2,1,0:T(2,128)(2,1)S(1)}, u32[]{:S(2)}) copy-start(bf16[256,2,256]{2,1,0:T(2,128)(2,1)S(1)} %reshape.389) | copy-start | bytes 786436
  382.4 79.1 %copy-start.15 = (bf16[256,2,256,1]{0,2,3,1:T(8,128)(2,1)}, bf16[256,2,256,1]{0,2,3,1:T(8,128)(2,1)S(1)}, u32[]{:S(2)}) copy-start(bf16[256,2,256,1]{0,2,3,1:T(8,128)(2,1)S(1)} %fusion.24) | copy-start | bytes 786436
  464.0 88.4 %copy-start.13 = (bf16[2,256,2,256]{3,1,2,0:T(8,128)(2,1)}, bf16[2,256,2,256]{3,1,2,0:T(8,128)(2,1)S(1)}, u32[]{:S(2)}) copy-start(bf16[2,256,2,256]{3,1,2,0:T(8,128)(2,1)S(1)} %convolution_convert_fusion.1) | copy-start | bytes 1572868
  552.5 215.5 %all-gather.26.cloned.1.call-start = ((), (), s32[]{:S(2)}) async-start(), calls=%async_computation.17 | async-start | bytes 17825792 | tf_op jit(solution)/shard_map/all_gather | solution.py:154
  553.2 407.6 %all-gather.28.cloned.1.call-start = ((), (), s32[]{:S(2)}) async-start(), calls=%async_computation.18 | async-start | bytes 17825792 | tf_op jit(solution)/shard_map/all_gather | solution.py:155
  553.8 419.6 %all-gather.36.cloned.1.call-start = ((), (), s32[]{:S(2)}) async-start(), calls=%async_computation.23 | async-start | bytes 1572864 | tf_op jit(solution)/shard_map/all_gather | solution.py:114
  554.6 669.5 %all-gather.30.cloned.1.call-start = ((), (), s32[]{:S(2)}) async-start(), calls=%async_computation.19 | async-start | bytes 17825792 | tf_op jit(solution)/shard_map/all_gather | solution.py:156
  555.1 727.6 %all-reduce.6.cloned.1.call-start = ((), (), s32[]{:S(2)}) async-start(), calls=%async_computation.24 | async-start | bytes 4194304 | tf_op jit(solution)/shard_map/psum | solution.py:183
  1262.8 62.2 %all-reduce.8.cloned.1.call-start = ((), (), s32[]{:S(2)}) async-start(), calls=%async_computation.25 | async-start | bytes 2097152 | tf_op jit(solution)/shard_map/psum | solution.py:247
  1296.2 5.3 copy-start.19
  1304.1 32.8 reduce-scatter.15.cloned.1.call-start
  1316.0 96.0 %reduce-scatter.33.cloned.1.call-start = ((), (), s32[]{:S(2)}) async-start(), calls=%async_computation.35 | async-start | bytes 557056
  1317.2 169.9 %reduce-scatter.31.cloned.1.call-start = ((), (), s32[]{:S(2)}) async-start(), calls=%async_computation.34 | async-start | bytes 557056
  1329.4 274.4 %all-gather.32.cloned.1.call-start = ((), (), s32[]{:S(2)}) async-start(), calls=%async_computation.21 | async-start | bytes 8912896 | tf_op jit(solution)/shard_map/all_gather | solution.py:276
  1338.9 379.3 %all-gather.38.cloned.1.call-start = ((), (), s32[]{:S(2)}) async-start(), calls=%async_computation.26 | async-start | bytes 8912896 | tf_op jit(solution)/shard_map/all_gather | solution.py:277
  1343.3 469.2 %reduce-scatter.19.cloned.1.call-start = ((), (), s32[]{:S(2)}) async-start(), calls=%async_computation.28 | async-start | bytes 4456448 | tf_op jit(solution)/shard_map/reduce_scatter | solution.py:270
  1346.2 564.0 %reduce-scatter.21.cloned.1.call-start = ((), (), s32[]{:S(2)}) async-start(), calls=%async_computation.29 | async-start | bytes 4456448 | tf_op jit(solution)/shard_map/reduce_scatter | solution.py:271
  1350.0 742.2 %reduce-scatter.17.cloned.1.call-start = ((), (), s32[]{:S(2)}) async-start(), calls=%async_computation.27 | async-start | bytes 8912896 | tf_op jit(solution)/shard_map/reduce_scatter | solution.py:269
  1355.8 919.5 %reduce-scatter.23.cloned.1.call-start = ((), (), s32[]{:S(2)}) async-start(), calls=%async_computation.30 | async-start | bytes 8912896 | tf_op jit(solution)/shard_map/reduce_scatter | solution.py:272
  1361.3 1605.5 %reduce-scatter.25.cloned.1.call-start = ((), (), s32[]{:S(2)}) async-start(), calls=%async_computation.31 | async-start | bytes 35651584 | tf_op jit(solution)/shard_map/reduce_scatter | solution.py:197
  1376.4 2282.5 %reduce-scatter.27.cloned.1.call-start = ((), (), s32[]{:S(2)}) async-start(), calls=%async_computation.32 | async-start | bytes 35651584 | tf_op jit(solution)/shard_map/reduce_scatter | solution.py:198
  1391.2 2959.6 %reduce-scatter.29.cloned.1.call-start = ((), (), s32[]{:S(2)}) async-start(), calls=%async_computation.33 | async-start | bytes 35651584 | tf_op jit(solution)/shard_map/reduce_scatter | solution.py:199
  (27 other events, 43.9 us)
Sparse Core Ops, SparseCore 0:
  10.8 113.8 all-gather.33
  127.4 111.0 all-gather.13
  245.8 7.6 all-gather.15
  256.1 61.4 all-gather.17
  320.2 59.3 all-gather.19
  382.2 74.8 all-gather.21
  459.9 87.7 all-gather.23
  552.6 19.6 all-reduce.3
  575.5 192.4 all-gather.25
  771.0 189.7 all-gather.27
  963.1 7.4 all-gather.35
  973.5 250.4 all-gather.29
  1263.0 19.7 all-reduce.5
  1304.2 20.7 all-reduce.7
  1327.2 9.6 reduce-scatter.14
  1339.0 72.9 reduce-scatter.32
  1414.2 72.8 reduce-scatter.30
  1490.3 113.4 all-gather.31
  1607.2 111.0 all-gather.37
  1720.9 91.5 reduce-scatter.18
  1815.4 94.6 reduce-scatter.20
  1913.0 179.1 reduce-scatter.16
  2095.1 180.2 reduce-scatter.22
  2278.1 688.6 reduce-scatter.24
  2969.8 689.0 reduce-scatter.26
  3661.7 689.0 reduce-scatter.28
where the time goes:
time: 4370 us; the launch traced here: 4360 us
  waiting for transfers between devices  4110 us (94%)
  matrix products  155 us (4%)
  local copies, waits for them, and re-layouts  47.9 us (1%)
    reduce_scatter x1, waiting for transfers between devices, on_device(): lax.psum_scatter(up_local, 'dp', scatter_dimension=0, tiled=True)  692 us
    reduce_scatter x1, waiting for transfers between devices, on_device(): lax.psum_scatter(down_local, 'dp', scatter_dimension=1, tiled=True)  692 us
    reduce_scatter x1, waiting for transfers between devices, on_device(): lax.psum_scatter(gate_local, 'dp', scatter_dimension=0, tiled=True)  692 us
    all_gather x1, waiting for transfers between devices, on_device(): lax.all_gather(w_down, 'dp', axis=1, tiled=True)  251 us
    all_gather x1, waiting for transfers between devices, on_device(): lax.all_gather(w_gate, 'dp', axis=0, tiled=True)  193 us
    reduce_scatter x1, waiting for transfers between devices, on_device(): lax.psum_scatter(out_local, 'dp', scatter_dimension=1, tiled=True)  183 us
    reduce_scatter x1, waiting for transfers between devices, on_device(): lax.psum_scatter(query_local, 'dp', scatter_dimension=0, tiled=True)  182 us
    all_gather x1, waiting for transfers between devices, on_device(): lax.all_gather(w_up, 'dp', axis=0, tiled=True)  180 us
  transfers between devices with their start and end apart: 26, of which 25 were waited for; matrix products, arithmetic and copies ran while one was open for 3% of the time, Pallas kernels for 0%

commit v1 on v0

v1 whole, which is shorter than its diff:
```python
import jax
import jax.numpy as jnp
from jax import lax
from jax.sharding import PartitionSpec as P

HD = 256
HALO = 192
LINE = 4

EPSILON = 1e-06
ROPE_BASE = 1000042.0
BF16 = jnp.bfloat16
F32 = jnp.float32


def matmul(left, right):
    return jnp.dot(left, right, preferred_element_type=F32)


def matmul_t(left, right):
    return lax.dot_general(left, right, (((1,), (1,)), ((), ())), preferred_element_type=F32)


def t_matmul(left, right):
    return lax.dot_general(left, right, (((0,), (0,)), ((), ())), preferred_element_type=F32)


def rotary_tables(positions):
    exponents = jnp.arange(0, HD, 2).astype(F32) / HD
    inverse = jnp.power(F32(ROPE_BASE), -exponents)
    angles = positions.astype(F32)[:, None] * inverse[None, :]
    angles = jnp.concatenate([angles, angles], axis=1)
    return (jnp.cos(angles), jnp.sin(angles))


def rotate(vectors, cosine, sine):
    middle = vectors.shape[-1] // 2
    turned = jnp.concatenate([-vectors[..., middle:], vectors[..., :middle]], axis=-1)
    return vectors * cosine + turned * sine


def rotate_back(grads, cosine, sine):
    middle = grads.shape[-1] // 2
    scaled = grads * sine
    turned = jnp.concatenate([scaled[..., middle:], -scaled[..., :middle]], axis=-1)
    return grads * cosine + turned


class Links:
    def __init__(self):
        self.count = lax.axis_size("dp")
        self.plane = self.count // LINE
        self.index = lax.axis_index("dp")
        self.line, self.place = self.index // self.plane, self.index % self.plane
        self.half = lax.axis_index("tensor")
        self.bits = [1 << b for b in range(self.plane.bit_length() - 1)]

    def step(self, x, k):
        n, shift = self.count, k * self.plane
        return lax.ppermute(x, "dp", [(d, (d + shift) % n) for d in range(n)])

    def cross(self, x, bit):
        return lax.ppermute(x, "dp", [(d, d ^ bit) for d in range(self.count)])

    def swap(self, x):
        return lax.ppermute(x, "tensor", [(0, 1), (1, 0)])

    def both(self, x):
        other = self.swap(x)
        first = self.half == 0
        return jnp.concatenate([jnp.where(first, x, other), jnp.where(first, other, x)], axis=1)

    def halves(self, x):
        width = x.shape[1] // 2
        mine = lax.dynamic_slice_in_dim(x, self.half * width, width, 1)
        theirs = lax.dynamic_slice_in_dim(x, (1 - self.half) * width, width, 1)
        return mine, theirs

    def order(self, turn):
        return self.bits[turn % len(self.bits):] + self.bits[: turn % len(self.bits)]

    def spread(self, x, turn):
        held = {0: x}
        for bit in self.order(turn):
            held |= {key | bit: self.cross(part, bit) for key, part in held.items()}
        return held

    def fold(self, held, turn):
        for bit in self.order(turn):
            kept = {key: part for key, part in held.items() if not key & bit}
            for key in kept:
                got = self.cross(held[key | bit].astype(BF16), bit)
                kept[key] = kept[key].astype(F32) + got.astype(F32)
            held = kept
        return held[0]


def gather_pieces(links, pieces, rows):
    columns = pieces[0].shape[1]
    whole = jnp.zeros((LINE, links.plane, rows, columns), BF16)
    for k, piece in enumerate(pieces):
        origin = (links.line - k) % LINE
        for key, part in links.spread(piece, k).items():
            whole = lax.dynamic_update_slice(
                whole, part[None, None], (origin, links.place ^ key, 0, 0)
            )
    return whole.reshape(-1, columns)


def fold_plane(links, grads, rows):
    columns = grads.shape[1]
    parts = grads.reshape(LINE, links.plane, rows, columns)
    out = []
    for turn in range(2):
        half = parts[turn * 2 : turn * 2 + 2]
        held = {
            key: lax.dynamic_slice_in_dim(half, links.place ^ key, 1, 1)[:, 0]
            for key in range(links.plane)
        }
        out.append(links.fold(held, turn))
    return jnp.concatenate(out, axis=0)


def on_device(
    tokens,
    cotangent,
    lengths,
    order,
    attn_gain,
    w_query,
    w_key,
    w_value,
    w_output,
    ffn_gain,
    w_gate,
    w_up,
    w_down,
):
    links = Links()
    half_index = links.half
    count, half_width = tokens.shape
    width = 2 * half_width
    rows = w_query.shape[0]
    ff_half = w_gate.shape[1]
    chunk = ff_half // LINE

    attn_mine = jnp.concatenate([w_query, w_key, w_value, w_output.T], axis=1)
    attn_all = gather_pieces(
        links, [attn_mine] + [links.step(attn_mine, k) for k in range(1, LINE)], rows
    )
    ffn_mine = jnp.stack(
        [w_gate.reshape(rows, LINE, chunk), w_up.reshape(rows, LINE, chunk), w_down.T.reshape(rows, LINE, chunk)],
        axis=2,
    ).reshape(rows, LINE, 3 * chunk)

    def for_line(k):
        target = (links.line + k) % LINE
        return lax.dynamic_slice_in_dim(ffn_mine, target, 1, 1)[:, 0]

    ffn_all = gather_pieces(
        links, [for_line(0)] + [links.step(for_line(k), k) for k in range(1, LINE)], rows
    )
    w_gate_up, w_down_t = ffn_all[:, : 2 * chunk], ffn_all[:, 2 * chunk :]

    def line_gather(x):
        return jnp.concatenate([x] + [links.step(x, k) for k in range(1, LINE)], axis=0)

    def line_sum(x):
        parts = x.reshape(LINE, count, half_width)
        total = parts[0].astype(F32)
        for k in range(1, LINE):
            total += links.step(parts[k].astype(BF16), LINE - k).astype(F32)
        return total

    n = links.count
    before = lax.ppermute(tokens[count - HALO :], "dp", [(d, d + 1) for d in range(n - 1)])
    tokens_ext = links.both(jnp.concatenate([before, tokens], axis=0)).astype(F32)
    cot_line = links.both(line_gather(cotangent))

    seq_ids = jnp.arange(lengths.shape[0])
    in_start = jnp.sum(jnp.where(seq_ids[None, :] < seq_ids[:, None], lengths[None, :], 0), axis=1)
    row_ids = links.index * count - HALO + jnp.arange(HALO + count)
    seq_of_row = jnp.sum((row_ids[:, None] >= in_start[None, :]).astype(jnp.int32), axis=1) - 1
    chosen = seq_of_row[:, None] == seq_ids[None, :]
    positions = row_ids - jnp.sum(jnp.where(chosen, in_start[None, :], 0), axis=1)
    cosine, sine = rotary_tables(positions)
    cos_k, sin_k = cosine[:, None, :], sine[:, None, :]
    cos_q, sin_q = cosine[HALO:, None, None, :], sine[HALO:, None, None, :]

    gain_one = links.both(attn_gain[None, :]).astype(F32)
    gain_two = ffn_gain.astype(F32)[None, :]
    rms_one = lax.rsqrt(jnp.mean(tokens_ext * tokens_ext, axis=-1, keepdims=True) + EPSILON)
    normed_attn = (tokens_ext * rms_one * gain_one).astype(BF16)

    q_width, k_width = w_query.shape[1], w_key.shape[1]
    kv_local = k_width // HD
    repeats = q_width // k_width
    ext = HALO + count
    w_q = attn_all[:, :q_width]
    w_kv = attn_all[:, q_width : q_width + 2 * k_width]
    w_out_t = attn_all[:, q_width + 2 * k_width :]
    queries = matmul(normed_attn[HALO:], w_q).reshape(count, kv_local, repeats, HD)
    keys_values = matmul(normed_attn, w_kv)
    keys = keys_values[:, :k_width].reshape(ext, kv_local, HD)
    values = keys_values[:, k_width:].astype(BF16).reshape(ext, kv_local, HD)
    queries_rot = rotate(queries, cos_q, sin_q).astype(BF16)
    keys_rot = rotate(keys, cos_k, sin_k).astype(BF16)
    allowed = (seq_of_row[HALO:, None] == seq_of_row[None, :]) & (
        row_ids[HALO:, None] >= row_ids[None, :]
    )
    scores = jnp.einsum("qgrd,kgd->grqk", queries_rot, keys_rot, preferred_element_type=F32)
    scores = jnp.where(allowed[None, None], scores * HD ** (-0.5), -1e30)
    highest = jnp.max(scores, axis=-1, keepdims=True)
    expo = jnp.exp(scores - highest)
    probs = expo / jnp.sum(expo, axis=-1, keepdims=True)
    probs_low = probs.astype(BF16)
    attended = jnp.einsum("grqk,kgd->qgrd", probs_low, values, preferred_element_type=F32)
    attended = attended.astype(BF16).reshape(count, q_width)
    out_mine, out_theirs = links.halves(matmul_t(attended, w_out_t))
    tokens_half = tokens.astype(F32)
    mixed = tokens_half + (out_mine + links.swap(out_theirs))

    def row_sum(x):
        total = jnp.sum(x, axis=-1)[None, :]
        return (total + links.swap(total)).reshape(count, 1)

    rms_two = lax.rsqrt(row_sum(mixed * mixed) / width + EPSILON)
    normed_ffn = links.both(line_gather((mixed * rms_two * gain_two).astype(BF16)))

    gate_up = matmul(normed_ffn, w_gate_up)
    gate, upward = gate_up[:, :chunk], gate_up[:, chunk:]
    sigmoid = jax.nn.sigmoid(gate)
    silu_gate = gate * sigmoid
    hidden = (silu_gate * upward).astype(BF16)
    hidden_grad = matmul(cot_line, w_down_t)
    gate_act_grad = (hidden_grad * upward * sigmoid * (1.0 + gate * (1.0 - sigmoid))).astype(BF16)
    up_act_grad = (hidden_grad * silu_gate).astype(BF16)
    act_grad = jnp.concatenate([gate_act_grad, up_act_grad], axis=1)
    norm_mine, norm_theirs = links.halves(matmul_t(act_grad, w_gate_up))
    normed_ffn_grad = line_sum(norm_mine + links.swap(norm_theirs.astype(BF16)).astype(F32))
    ffn_mine_out, ffn_theirs_out = links.halves(matmul_t(hidden, w_down_t))
    ffn_out = line_sum(ffn_mine_out + links.swap(ffn_theirs_out.astype(BF16)).astype(F32))
    output = (mixed + ffn_out).astype(BF16)

    down_sum = fold_plane(links, t_matmul(cot_line, hidden).astype(BF16), rows)
    gate_up_sum = fold_plane(links, t_matmul(normed_ffn, act_grad).astype(BF16), rows)
    ffn_sum = jnp.concatenate([gate_up_sum, down_sum], axis=2).astype(BF16)
    ffn_grads = jnp.zeros((3, rows, LINE, chunk), F32)
    for k in range(LINE):
        part = lax.dynamic_slice_in_dim(ffn_sum, (links.line + k) % LINE, 1, 0)[0]
        if k:
            part = links.step(part, k)
        part = part.astype(F32).reshape(rows, 3, chunk).transpose(1, 0, 2)
        ffn_grads = lax.dynamic_update_slice(
            ffn_grads, part[:, :, None], (0, 0, (links.line - k) % LINE, 0)
        )
    ffn_grads = ffn_grads.reshape(3, rows, ff_half)

    ffn_gain_local = jnp.sum(normed_ffn_grad * mixed * rms_two, axis=0)
    inner_two = row_sum(normed_ffn_grad * gain_two * mixed)
    mixed_grad = (
        cotangent.astype(F32)
        + rms_two * gain_two * normed_ffn_grad
        - mixed * rms_two * rms_two * rms_two * inner_two / width
    )

    attn_out_grad = links.both(mixed_grad.astype(BF16))
    out_local = t_matmul(attn_out_grad, attended)
    attended_grad = matmul(attn_out_grad, w_out_t).astype(BF16)
    attended_grad = attended_grad.reshape(count, kv_local, repeats, HD)
    values_grad = jnp.einsum("grqk,qgrd->kgd", probs_low, attended_grad, preferred_element_type=F32)
    values_grad = values_grad.astype(BF16).reshape(ext, k_width)
    probs_grad = jnp.einsum("qgrd,kgd->grqk", attended_grad, values, preferred_element_type=F32)
    scores_grad = (
        probs * (probs_grad - jnp.sum(probs * probs_grad, axis=-1, keepdims=True))
    ).astype(BF16)
    rot_q_grad = jnp.einsum(
        "grqk,kgd->qgrd", scores_grad, keys_rot, preferred_element_type=F32
    ) * HD ** (-0.5)
    rot_k_grad = jnp.einsum(
        "grqk,qgrd->kgd", scores_grad, queries_rot, preferred_element_type=F32
    ) * HD ** (-0.5)
    queries_grad = rotate_back(rot_q_grad, cos_q, sin_q).astype(BF16).reshape(count, q_width)
    keys_grad = rotate_back(rot_k_grad, cos_k, sin_k).astype(BF16).reshape(ext, k_width)
    kv_grad = jnp.concatenate([keys_grad, values_grad], axis=1)
    attn_local = jnp.concatenate(
        [t_matmul(normed_attn[HALO:], queries_grad), t_matmul(normed_attn, kv_grad), out_local],
        axis=1,
    )
    attn_sum = fold_plane(links, attn_local.astype(BF16), rows)
    attn_total = lax.dynamic_slice_in_dim(attn_sum, links.line, 1, 0)[0]
    for k in range(1, LINE):
        part = lax.dynamic_slice_in_dim(attn_sum, (links.line + k) % LINE, 1, 0)[0]
        attn_total += links.step(part.astype(BF16), k).astype(F32)

    normed_grad = matmul_t(kv_grad, w_kv)
    normed_grad = normed_grad + jnp.pad(matmul_t(queries_grad, w_q), ((HALO, 0), (0, 0)))
    grad_mine, grad_theirs = links.halves(normed_grad)
    grad_half = grad_mine + links.swap(grad_theirs.astype(BF16)).astype(F32)
    behind = lax.ppermute(grad_half[:HALO].astype(BF16), "dp", [(d + 1, d) for d in range(n - 1)])
    normed_attn_grad = grad_half[HALO:] + jnp.pad(behind.astype(F32), ((count - HALO, 0), (0, 0)))
    rms_mine = rms_one[HALO:]
    gain_mine = attn_gain.astype(F32)[None, :]
    attn_gain_local = jnp.sum(normed_attn_grad * tokens_half * rms_mine, axis=0)
    inner_one = row_sum(normed_attn_grad * gain_mine * tokens_half)
    tokens_grad = (
        mixed_grad
        + rms_mine * gain_mine * normed_attn_grad
        - tokens_half * rms_mine * rms_mine * rms_mine * inner_one / width
    ).astype(BF16)

    gains = jnp.stack([attn_gain_local, ffn_gain_local])
    gains = lax.psum_scatter(gains, "dp", scatter_dimension=1, tiled=True)
    return (
        output,
        tokens_grad,
        gains[:1],
        attn_total[:, :q_width],
        attn_total[:, q_width : q_width + k_width],
        attn_total[:, q_width + k_width : q_width + 2 * k_width],
        attn_total[:, q_width + 2 * k_width :].T,
        gains[1:],
        ffn_grads[0],
        ffn_grads[1],
        ffn_grads[2].T,
    )


def solution(mesh):
    weight = P("dp", "tensor")
    turned = P("tensor", "dp")
    return jax.shard_map(
        on_device,
        mesh=mesh,
        in_specs=(
            weight, weight, P(), P(), P("tensor"), weight, weight, weight, turned,
            P("tensor"), weight, weight, turned,
        ),
        out_specs=(
            weight, weight, turned, weight, weight, weight, turned, turned, weight, weight, turned,
        ),
        check_vma=False,
    )
```

time: 4370 us -> 1040 us (0.24)
  waiting for transfers between devices: 4110 us -> 439 us
  local copies, waits for them, and re-layouts: 47.9 us -> 239 us
  starting transfers between devices: 1.68 us -> 139 us
  other arithmetic: 26.2 us -> 87.6 us
  matrix products: 155 us -> 102 us
    reduce_scatter x8 -> x0, waiting for transfers between devices: 2630 us -> none  [the longest x1 692 us: on_device(): lax.psum_scatter(up_local, 'dp', scatter_dimension=0, tiled=True)]
    all_gather x13 -> x0, waiting for transfers between devices: 1350 us -> none  [the longest x1 251 us: on_device(): lax.all_gather(w_down, 'dp', axis=1, tiled=True)]
    ppermute x0 -> x80, waiting for transfers between devices: none -> 361 us  [the longest x42 259 us: cross(): return lax.ppermute(x, 'dp', [(d, d ^ bit) for d in range(self.count)])]
    ppermute x0 -> x80, starting transfers between devices: none -> 139 us  [the longest x24 81.9 us: step(): return lax.ppermute(x, 'dp', [(d, (d + shift) % n) for d in range(n)])]
    dynamic_slice x3 -> x25, local copies, waits for them, and re-layouts: 0.02 us -> 68.5 us  [the longest x15 57.8 us: fold_plane(): lax.dynamic_slice_in_dim(half, links.place ^ key, 1, 1)[:, 0]]
    dynamic_update_slice x0 -> x34, local copies, waits for them, and re-layouts: none -> 43.9 us  [the longest x31 38.6 us: gather_pieces(): lax.dynamic_update_slice(whole, part[None, None], (origin, links.place ^...]
  transfers between devices with their start and end apart: 26 -> 81, of which waited for: 25 -> 30; matrix products, arithmetic and copies ran while one was open for 3% -> 35% of each run, Pallas kernels for 0% -> 0%
where the time goes in v1:
time: 1040 us; the launch traced here: 1020 us
  waiting for transfers between devices  439 us (42%)
  local copies, waits for them, and re-layouts  239 us (23%)
  starting transfers between devices  139 us (13%)
  matrix products  102 us (10%)
  other arithmetic  87.6 us (8%)
  between operations  15.9 us (2%)
    ppermute x42, waiting for transfers between devices, cross(): return lax.ppermute(x, 'dp', [(d, d ^ bit) for d in range(self.count)])  259 us
    ppermute x24, waiting for transfers between devices, step(): return lax.ppermute(x, 'dp', [(d, (d + shift) % n) for d in range(n)])  102 us
    ppermute x24, starting transfers between devices, step(): return lax.ppermute(x, 'dp', [(d, (d + shift) % n) for d in range(n)])  81.9 us
    unnamed x2, waiting for transfers between devices  77.3 us
    dynamic_slice x15, local copies, waits for them, and re-layouts, fold_plane(): lax.dynamic_slice_in_dim(half, links.place ^ key, 1, 1)[:, 0]  57.8 us
    ppermute x42, starting transfers between devices, cross(): return lax.ppermute(x, 'dp', [(d, d ^ bit) for d in range(self.count)])  50 us
    unnamed x170, local copies, waits for them, and re-layouts  40.2 us
    dynamic_update_slice x31, local copies, waits for them, and re-layouts, gather_pieces(): lax.dynamic_update_slice(whole, part[None, None], (origin, links.place ^...  38.6 us
  transfers between devices with their start and end apart: 81, of which 30 were waited for; matrix products, arithmetic and copies ran while one was open for 35% of the time, Pallas kernels for 0%

profile of v1, /device:TPU:2, one launch (start us, length us, event | category | flops | bytes accessed | tf_op | source)
XLA Modules:
  0.0 1022.8 jit_solution(6018534777604889307)
XLA Ops:
  59.2 7.6 collective-permute-start.6
  79.2 13.2 %collective-permute-done.24 = bf16[128,3072]{1,0:T(8,128)(2,1)S(1)} collective-permute-done((bf16[128,3072]{1,0:T(8,128)(2,1)S(1)}, bf16[128,3072]{1,0:T(8,128)(2,1)S(1)}, u32[]{:S(2)}, u32[]{:S(2)}) %collective-permute-start.24) | collective-permute-done | bytes 786464 | tf_op jit(solution)/shard_map/ppermute | solution.py:63
  94.8 16.6 %collective-permute-done.25 = bf16[128,3072]{1,0:T(8,128)(2,1)S(1)} collective-permute-done((bf16[128,3072]{1,0:T(8,128)(2,1)S(1)}, bf16[128,3072]{1,0:T(8,128)(2,1)S(1)}, u32[]{:S(2)}, u32[]{:S(2)}) %collective-permute-start.25) | collective-permute-done | bytes 786464 | tf_op jit(solution)/shard_map/ppermute | solution.py:63
  115.3 15.8 %collective-permute-done.5 = bf16[128,3072]{1,0:T(8,128)(2,1)S(1)} collective-permute-done((bf16[128,3072]{1,0:T(8,128)(2,1)S(1)}, bf16[128,3072]{1,0:T(8,128)(2,1)S(1)}, u32[]{:S(2)}, u32[]{:S(2)}) %collective-permute-start.5) | collective-permute-done | bytes 786464 | tf_op jit(solution)/shard_map/ppermute | solution.py:63
  140.5 8.3 collective-permute-done.26
  151.8 14.7 %collective-permute-done.7 = bf16[128,3072]{1,0:T(8,128)(2,1)S(1)} collective-permute-done((bf16[128,3072]{1,0:T(8,128)(2,1)S(1)}, bf16[128,3072]{1,0:T(8,128)(2,1)S(1)}, u32[]{:S(2)}, u32[]{:S(2)}) %collective-permute-start.7) | collective-permute-done | bytes 786464 | tf_op jit(solution)/shard_map/ppermute | solution.py:63
  170.7 11.3 %collective-permute-done.28 = bf16[128,3072]{1,0:T(8,128)(2,1)} collective-permute-done((bf16[128,3072]{1,0:T(8,128)(2,1)S(1)}, bf16[128,3072]{1,0:T(8,128)(2,1)}, u32[]{:S(2)}, u32[]{:S(2)}) %collective-permute-start.28) | collective-permute-done | bytes 786464 | tf_op jit(solution)/shard_map/ppermute | solution.py:63
  194.3 10.8 %collective-permute-done.11 = bf16[128,3072]{1,0:T(8,128)(2,1)S(1)} collective-permute-done((bf16[128,3072]{1,0:T(8,128)(2,1)S(1)}, bf16[128,3072]{1,0:T(8,128)(2,1)S(1)}, u32[]{:S(2)}, u32[]{:S(2)}) %collective-permute-start.11) | collective-permute-done | bytes 786464 | tf_op jit(solution)/shard_map/ppermute | solution.py:63
  206.9 8.9 collective-permute-done.9
  231.1 9.6 collective-permute-done.13
  248.2 10.4 %collective-permute-done.32 = bf16[128,3072]{1,0:T(8,128)(2,1)} collective-permute-done((bf16[128,3072]{1,0:T(8,128)(2,1)}, bf16[128,3072]{1,0:T(8,128)(2,1)}, u32[]{:S(2)}, u32[]{:S(2)}) %collective-permute-start.32) | collective-permute-done | bytes 786464 | tf_op jit(solution)/shard_map/ppermute | solution.py:63
  260.1 15.3 %collective-permute-done.17 = bf16[128,3072]{1,0:T(8,128)(2,1)S(1)} collective-permute-done((bf16[128,3072]{1,0:T(8,128)(2,1)S(1)}, bf16[128,3072]{1,0:T(8,128)(2,1)S(1)}, u32[]{:S(2)}, u32[]{:S(2)}) %collective-permute-start.17) | collective-permute-done | bytes 786464 | tf_op jit(solution)/shard_map/ppermute | solution.py:63
  314.8 20.9 %collective-permute-start.20 = (bf16[256,1024]{1,0:T(8,128)(2,1)S(1)}, bf16[256,1024]{1,0:T(8,128)(2,1)S(1)}, u32[]{:S(2)}, u32[]{:S(2)}) collective-permute-start(bf16[256,1024]{1,0:T(8,128)(2,1)S(1)} %multiply_convert_fusion.3), channel_id=1, source_target_pairs={{0,8},{2,10},{4,12},{6,14},{8,16},{10,18},{12,20},{14,22},{16,24},... | collective-permute-start | bytes 1572872 | tf_op jit(solution)/shard_map/ppermute | solution.py:60
  349.7 14.1 %collective-permute-done.21 = bf16[256,1024]{1,0:T(8,128)(2,1)S(1)} collective-permute-done((bf16[256,1024]{1,0:T(8,128)(2,1)S(1)}, bf16[256,1024]{1,0:T(8,128)(2,1)S(1)}, u32[]{:S(2)}, u32[]{:S(2)}) %collective-permute-start.21) | collective-permute-done | bytes 524320 | tf_op jit(solution)/shard_map/ppermute | solution.py:60
  387.8 11.1 %fusion.3 = f32[1024,2048]{1,0:T(8,128)} fusion(bf16[2048,3072]{1,0:T(8,128)(2,1)S(1)} %bitcast.290, bf16[1024,1024]{1,0:T(8,128)(2,1)S(1)} %get-tuple-element.115, bf16[1024,1024]{1,0:T(8,128)(2,1)S(1)} %get-tuple-element.114), kind=kOutput, calls=%fused_computation.13 | convolution fusion | flops 8598323200 | bytes 20971520 | tf_op jit(solution)/shard_map/dot_general | solution.py:17
  398.9 10.1 multiply_convert_fusion.1
  408.9 14.0 %convolution_convert_fusion = bf16[2048,2048]{1,0:T(8,128)(2,1)} fusion(bf16[1024,1024]{1,0:T(8,128)(2,1)} %get-tuple-element.84, bf16[1024,1024]{1,0:T(8,128)(2,1)} %get-tuple-element.83, bf16[1024,1024]{1,0:T(8,128)(2,1)} %copy-done.32, bf16[1024,1024]{1,0:T(8,128)(2,1)S(1)} %get-tuple-element.114), kind=kOutput, calls=%fused_computation.10 | convolution fusion | flops 8610906112 | bytes 16777216 | tf_op jit(solution)/shard_map/dot_general | solution.py:25
  423.0 12.4 %fusion.1 = f32[1024,2048]{1,0:T(8,128)} fusion(bf16[2048,3072]{1,0:T(8,128)(2,1)S(1)} %bitcast.292, bf16[1024,1024]{1,0:T(8,128)(2,1)} %get-tuple-element.84, bf16[1024,1024]{1,0:T(8,128)(2,1)S(1)} %copy-done.69), kind=kOutput, calls=%fused_computation.11 | convolution fusion | flops 8598323200 | bytes 20971520 | tf_op jit(solution)/shard_map/dot_general | solution.py:21
  445.0 7.4 convolution_convert_fusion.4
  456.1 10.5 %fusion.8 = f32[1024,2048]{1,0:T(8,128)} fusion(bf16[1024,1024]{1,0:T(8,128)(2,1)} %get-tuple-element.87, bf16[2048,3072]{1,0:T(8,128)(2,1)} %bitcast.289), kind=kOutput, calls=%fused_computation.35 | convolution fusion | flops 4294967296 | bytes 14680064 | tf_op jit(solution)/shard_map/dot_general | solution.py:21
  535.7 17.1 %collective-permute-done.76 = bf16[2,128,1024]{1,2,0:T(8,128)(2,1)S(1)} collective-permute-done((bf16[2,128,1024]{1,2,0:T(8,128)(2,1)S(1)}, bf16[2,128,1024]{1,2,0:T(8,128)(2,1)S(1)}, u32[]{:S(2)}, u32[]{:S(2)}) %collective-permute-start.76) | collective-permute-done | bytes 524320 | tf_op jit(solution)/shard_map/ppermute | solution.py:63
  556.9 14.6 %collective-permute-start.48 = (bf16[256,1024]{1,0:T(8,128)(2,1)S(1)}, bf16[256,1024]{1,0:T(8,128)(2,1)S(1)}, u32[]{:S(2)}, u32[]{:S(2)}) collective-permute-start(bf16[256,1024]{1,0:T(8,128)(2,1)S(1)} %get-tuple-element.132), channel_id=1, source_target_pairs={{0,24},{2,26},{4,28},{6,30},{8,0},{10,2},{12,4},{14,6},{16,8},{18,... | collective-permute-start | bytes 1572872 | tf_op jit(solution)/shard_map/ppermute | solution.py:60
  574.3 9.5 collective-permute-done.48
  588.1 46.3 %collective-permute-done.49 = bf16[256,1024]{1,0:T(8,128)(2,1)S(1)} collective-permute-done((bf16[256,1024]{1,0:T(8,128)(2,1)S(1)}, bf16[256,1024]{1,0:T(8,128)(2,1)S(1)}, u32[]{:S(2)}, u32[]{:S(2)}) %collective-permute-start.49) | collective-permute-done | bytes 524320 | tf_op jit(solution)/shard_map/ppermute | solution.py:60
  637.2 23.4 %collective-permute-done.41 = bf16[256,1024]{1,0:T(8,128)(2,1)S(1)} collective-permute-done((bf16[256,1024]{1,0:T(8,128)(2,1)S(1)}, bf16[256,1024]{1,0:T(8,128)(2,1)S(1)}, u32[]{:S(2)}, u32[]{:S(2)}) %collective-permute-start.41) | collective-permute-done | bytes 524320 | tf_op jit(solution)/shard_map/ppermute | solution.py:60
  697.6 19.7 %pad_maximum_fusion = bf16[2048,3072]{0,1:T(8,128)(2,1)S(1)} fusion(bf16[2048,1024]{0,1:T(8,128)(2,1)S(1)} %copy-done.1, bf16[2048,1024]{0,1:T(8,128)(2,1)S(1)} %convolution_convert_fusion.1, bf16[2048,1024]{0,1:T(8,128)(2,1)S(1)} %convolution_convert_fusion.3), kind=kLoop, calls=%fused_computation.1 | loop fusion | flops 37748736 | bytes 25165824 | tf_op jit(solution)/shard_map/concatenate | solution.py:286
  722.3 11.0 %slice.222 = bf16[2,4,128,3072]{2,1,0,3:T(4,128)(2,1)} reshape(bf16[1024,3072]{0,1:T(8,128)(2,1)} %get-tuple-element.82) | data formatting | bytes 12582912 | tf_op jit(solution)/shard_map/slice | solution.py:115
  733.3 11.0 %slice.224 = bf16[2,4,128,3072]{2,1,0,3:T(4,128)(2,1)} reshape(bf16[1024,3072]{0,1:T(8,128)(2,1)} %get-tuple-element.81) | data formatting | bytes 12582912 | tf_op jit(solution)/shard_map/slice | solution.py:115
  744.3 34.3 %constant_dynamic-slice_fusion.23 = (bf16[2,1,128,3072]{2,1,0,3:T(2,128)(2,1)}, bf16[2,1,128,3072]{2,1,0,3:T(2,128)(2,1)S(1)}, bf16[2,1,128,3072]{2,1,0,3:T(2,12...) fusion(bf16[2,4,128,3072]{2,1,0,3:T(4,128)(2,1)} %slice.224, ...), kind=kLoop, calls=%fused_computation.267 | loop fusion | bytes 25165840 | tf_op jit(solution)/shard_map/dynamic_slice | solution.py:117
  822.9 14.1 %collective-permute-done.57 = bf16[2,128,3072]{1,2,0:T(8,128)(2,1)S(1)} collective-permute-done((bf16[2,128,3072]{1,2,0:T(8,128)(2,1)S(1)}, bf16[2,128,3072]{1,2,0:T(8,128)(2,1)S(1)}, u32[]{:S(2)}, u32[]{:S(2)}) %collective-permute-start.57) | collective-permute-done | bytes 1572896 | tf_op jit(solution)/shard_map/ppermute | solution.py:63
  854.6 57.1 %collective-permute-done.61 = bf16[2,128,3072]{1,2,0:T(8,128)(2,1)} collective-permute-done((bf16[2,128,3072]{1,2,0:T(8,128)(2,1)}, bf16[2,128,3072]{1,2,0:T(8,128)(2,1)}, u32[]{:S(2)}, u32[]{:S(2)}) %collective-permute-start.61) | collective-permute-done | bytes 1572896 | tf_op jit(solution)/shard_map/ppermute | solution.py:63
  930.0 77.3 %reduce-scatter.4.cloned.1.call-done = f32[64,2]{1,0:T(8,128)} async-done(((f32[1024,2]{1,0:T(8,128)}), f32[64,2]{1,0:T(8,128)}) %reduce-scatter.4.cloned.1.call-update) | async-done | bytes 528
  (491 shorter events, 428.4 us)
Async XLA Ops:
  7.2 1000.1 %reduce-scatter.4.cloned.1.call-start = ((), (), s32[]{:S(2)}) async-start(), calls=%async_computation.1 | async-start | bytes 557056
  7.2 51.9 %collective-permute-start.43 = (bf16[256,1024]{1,0:T(8,128)(2,1)}, bf16[256,1024]{1,0:T(8,128)(2,1)}, u32[]{:S(2)}, u32[]{:S(2)}) collective-permute-start(bf16[256,1024]{1,0:T(8,128)(2,1)} %param.14), channel_id=1, source_target_pairs={{0,8},{2,10},{4,12},{6,14},{8,16},{10,18},{12,20},{14,22},{16,24},... | collective-permute-start | bytes 1572872 | tf_op jit(solution)/shard_map/ppermute | solution.py:60
  8.9 59.8 %collective-permute-start.44 = (bf16[256,1024]{1,0:T(8,128)(2,1)}, bf16[256,1024]{1,0:T(8,128)(2,1)}, u32[]{:S(2)}, u32[]{:S(2)}) collective-permute-start(bf16[256,1024]{1,0:T(8,128)(2,1)} %param.14), channel_id=1, source_target_pairs={{0,16},{2,18},{4,20},{6,22},{8,24},{10,26},{12,28},{14,30},{16,0},... | collective-permute-start | bytes 1572872 | tf_op jit(solution)/shard_map/ppermute | solution.py:60
  11.5 59.2 %collective-permute-start.45 = (bf16[256,1024]{1,0:T(8,128)(2,1)}, bf16[256,1024]{1,0:T(8,128)(2,1)}, u32[]{:S(2)}, u32[]{:S(2)}) collective-permute-start(bf16[256,1024]{1,0:T(8,128)(2,1)} %param.14), channel_id=1, source_target_pairs={{0,24},{2,26},{4,28},{6,30},{8,0},{10,2},{12,4},{14,6},{16,8},{18,... | collective-permute-start | bytes 1572872 | tf_op jit(solution)/shard_map/ppermute | solution.py:60
  59.2 73.1 %collective-permute-start.6 = (bf16[128,3072]{1,0:T(8,128)(2,1)S(1)}, bf16[128,3072]{1,0:T(8,128)(2,1)S(1)}, u32[]{:S(2)}, u32[]{:S(2)}) collective-permute-start(bf16[128,3072]{1,0:T(8,128)(2,1)S(1)} %copy-done.51), channel_id=1, source_target_pairs={{0,8},{2,10},{4,12},{6,14},{8,16},{10,18},{12,20},{14,22},{16,24},... | collective-permute-start | bytes 2359304 | tf_op jit(solution)/shard_map/ppermute | solution.py:60
  68.7 99.1 %collective-permute-start.10 = (bf16[128,3072]{1,0:T(8,128)(2,1)S(1)}, bf16[128,3072]{1,0:T(8,128)(2,1)S(1)}, u32[]{:S(2)}, u32[]{:S(2)}) collective-permute-start(bf16[128,3072]{1,0:T(8,128)(2,1)S(1)} %copy-done.51), channel_id=1, source_target_pairs={{0,16},{2,18},{4,20},{6,22},{8,24},{10,26},{12,28},{14,30},{16,0},... | collective-permute-start | bytes 2359304 | tf_op jit(solution)/shard_map/ppermute | solution.py:60
  75.9 116.6 %collective-permute-start.14 = (bf16[128,3072]{1,0:T(8,128)(2,1)S(1)}, bf16[128,3072]{1,0:T(8,128)(2,1)S(1)}, u32[]{:S(2)}, u32[]{:S(2)}) collective-permute-start(bf16[128,3072]{1,0:T(8,128)(2,1)S(1)} %copy-done.51), channel_id=1, source_target_pairs={{0,24},{2,26},{4,28},{6,30},{8,0},{10,2},{12,4},{14,6},{16,8},{18,... | collective-permute-start | bytes 2359304 | tf_op jit(solution)/shard_map/ppermute | solution.py:60
  132.3 89.1 %collective-permute-start.31 = (bf16[128,3072]{1,0:T(8,128)(2,1)S(1)}, bf16[128,3072]{1,0:T(8,128)(2,1)}, u32[]{:S(2)}, u32[]{:S(2)}) collective-permute-start(bf16[128,3072]{1,0:T(8,128)(2,1)S(1)} %bitcast.329), channel_id=1, source_target_pairs={{0,16},{2,18},{4,20},{6,22},{8,24},{10,26},{12,28},{14,30},{16,0},... | collective-permute-start | bytes 2359304 | tf_op jit(solution)/shard_map/ppermute | solution.py:60
  188.2 57.1 %collective-permute-start.35 = (bf16[128,3072]{1,0:T(8,128)(2,1)S(1)}, bf16[128,3072]{1,0:T(8,128)(2,1)}, u32[]{:S(2)}, u32[]{:S(2)}) collective-permute-start(bf16[128,3072]{1,0:T(8,128)(2,1)S(1)} %bitcast.328), channel_id=1, source_target_pairs={{0,24},{2,26},{4,28},{6,30},{8,0},{10,2},{12,4},{14,6},{16,8},{18,... | collective-permute-start | bytes 2359304 | tf_op jit(solution)/shard_map/ppermute | solution.py:60
  220.5 159.3 %collective-permute-start.46 = (bf16[1024,1024]{1,0:T(8,128)(2,1)}, bf16[1024,1024]{1,0:T(8,128)(2,1)}, u32[]{:S(2)}, u32[]{:S(2)}) collective-permute-start(bf16[1024,1024]{1,0:T(8,128)(2,1)} %constant_dynamic-update-slice_fusion.5), channel_id=1, source_target_pairs={{0,1},{1,0},{2,3},{3,2},{4,5},{5,4},{6,7},{7,6},{8,9},{9,8},{10,11... | collective-permute-start | bytes 6291464 | tf_op jit(solution)/shard_map/ppermute | solution.py:66
  245.3 64.3 %collective-permute-start.33 = (bf16[128,3072]{1,0:T(8,128)(2,1)}, bf16[128,3072]{1,0:T(8,128)(2,1)}, u32[]{:S(2)}, u32[]{:S(2)}) collective-permute-start(bf16[128,3072]{1,0:T(8,128)(2,1)} %collective-permute-done.31), channel_id=1, source_target_pairs={{0,4},{2,6},{4,0},{6,2},{8,12},{10,14},{12,8},{14,10},{16,20},{18,... | collective-permute-start | bytes 2359304 | tf_op jit(solution)/shard_map/ppermute | solution.py:63
  246.4 96.7 %collective-permute-start.36 = (bf16[128,3072]{1,0:T(8,128)(2,1)}, bf16[128,3072]{1,0:T(8,128)(2,1)}, u32[]{:S(2)}, u32[]{:S(2)}) collective-permute-start(bf16[128,3072]{1,0:T(8,128)(2,1)} %collective-permute-done.35), channel_id=1, source_target_pairs={{0,4},{2,6},{4,0},{6,2},{8,12},{10,14},{12,8},{14,10},{16,20},{18,... | collective-permute-start | bytes 2359304 | tf_op jit(solution)/shard_map/ppermute | solution.py:63
  443.3 69.6 %collective-permute-start.66 = (bf16[2,128,2048]{1,2,0:T(8,128)(2,1)}, bf16[2,128,2048]{1,2,0:T(8,128)(2,1)}, u32[]{:S(2)}, u32[]{:S(2)}) collective-permute-start(bf16[2,128,2048]{1,2,0:T(8,128)(2,1)} %bitcast.323), channel_id=1, source_target_pairs={{0,2},{2,0},{4,6},{6,4},{8,10},{10,8},{12,14},{14,12},{16,18},{18,... | collective-permute-start | bytes 3145736 | tf_op jit(solution)/shard_map/ppermute | solution.py:63
  455.7 49.5 %collective-permute-start.72 = (bf16[2,128,1024]{1,2,0:T(8,128)(2,1)}, bf16[2,128,1024]{1,2,0:T(8,128)(2,1)}, u32[]{:S(2)}, u32[]{:S(2)}) collective-permute-start(bf16[2,128,1024]{1,2,0:T(8,128)(2,1)} %bitcast.98), channel_id=1, source_target_pairs={{0,2},{2,0},{4,6},{6,4},{8,10},{10,8},{12,14},{14,12},{16,18},{18,... | collective-permute-start | bytes 1572872 | tf_op jit(solution)/shard_map/ppermute | solution.py:63
  474.1 48.8 %collective-permute-start.69 = (bf16[2,128,2048]{1,2,0:T(8,128)(2,1)}, bf16[2,128,2048]{1,2,0:T(8,128)(2,1)}, u32[]{:S(2)}, u32[]{:S(2)}) collective-permute-start(bf16[2,128,2048]{1,2,0:T(8,128)(2,1)} %bitcast.324), channel_id=1, source_target_pairs={{0,4},{2,6},{4,0},{6,2},{8,12},{10,14},{12,8},{14,10},{16,20},{18,... | collective-permute-start | bytes 3145736 | tf_op jit(solution)/shard_map/ppermute | solution.py:63
  522.9 48.6 %collective-permute-start.39 = (bf16[1024,1024]{1,0:T(8,128)(2,1)}, bf16[1024,1024]{1,0:T(8,128)(2,1)S(1)}, u32[]{:S(2)}, u32[]{:S(2)}) collective-permute-start(bf16[1024,1024]{1,0:T(8,128)(2,1)} %dynamic-slice_convert_fusion.1), channel_id=1, source_target_pairs={{0,1},{1,0},{2,3},{3,2},{4,5},{5,4},{6,7},{7,6},{8,9},{9,8},{10,11... | collective-permute-start | bytes 6291464 | tf_op jit(solution)/shard_map/ppermute | solution.py:66
  552.7 82.3 %collective-permute-start.68 = (bf16[2,128,2048]{1,2,0:T(8,128)(2,1)}, bf16[2,128,2048]{1,2,0:T(8,128)(2,1)}, u32[]{:S(2)}, u32[]{:S(2)}) collective-permute-start(bf16[2,128,2048]{1,2,0:T(8,128)(2,1)} %bitcast.91), channel_id=1, source_target_pairs={{0,4},{2,6},{4,0},{6,2},{8,12},{10,14},{12,8},{14,10},{16,20},{18,... | collective-permute-start | bytes 3145736 | tf_op jit(solution)/shard_map/ppermute | solution.py:63
  553.4 81.8 %collective-permute-start.70 = (bf16[2,128,2048]{1,2,0:T(8,128)(2,1)S(1)}, bf16[2,128,2048]{1,2,0:T(8,128)(2,1)}, u32[]{:S(2)}, u32[]{:S(2)}) collective-permute-start(bf16[2,128,2048]{1,2,0:T(8,128)(2,1)S(1)} %fusion.31), channel_id=1, source_target_pairs={{0,2},{2,0},{4,6},{6,4},{8,10},{10,8},{12,14},{14,12},{16,18},{18,... | collective-permute-start | bytes 3145736 | tf_op jit(solution)/shard_map/ppermute | solution.py:63
  571.4 63.0 %collective-permute-start.49 = (bf16[256,1024]{1,0:T(8,128)(2,1)S(1)}, bf16[256,1024]{1,0:T(8,128)(2,1)S(1)}, u32[]{:S(2)}, u32[]{:S(2)}) collective-permute-start(bf16[256,1024]{1,0:T(8,128)(2,1)S(1)} %get-tuple-element.134), channel_id=1, source_target_pairs={{0,16},{2,18},{4,20},{6,22},{8,24},{10,26},{12,28},{14,30},{16,0},... | collective-permute-start | bytes 1572872 | tf_op jit(solution)/shard_map/ppermute | solution.py:60
  571.4 63.0 %collective-permute-start.50 = (bf16[256,1024]{1,0:T(8,128)(2,1)S(1)}, bf16[256,1024]{1,0:T(8,128)(2,1)S(1)}, u32[]{:S(2)}, u32[]{:S(2)}) collective-permute-start(bf16[256,1024]{1,0:T(8,128)(2,1)S(1)} %get-tuple-element.133), channel_id=1, source_target_pairs={{0,8},{2,10},{4,12},{6,14},{8,16},{10,18},{12,20},{14,22},{16,24},... | collective-permute-start | bytes 1572872 | tf_op jit(solution)/shard_map/ppermute | solution.py:60
  583.8 53.4 %collective-permute-start.40 = (bf16[256,1024]{1,0:T(8,128)(2,1)S(1)}, bf16[256,1024]{1,0:T(8,128)(2,1)S(1)}, u32[]{:S(2)}, u32[]{:S(2)}) collective-permute-start(bf16[256,1024]{1,0:T(8,128)(2,1)S(1)} %get-tuple-element.135), channel_id=1, source_target_pairs={{0,24},{2,26},{4,28},{6,30},{8,0},{10,2},{12,4},{14,6},{16,8},{18,... | collective-permute-start | bytes 1572872 | tf_op jit(solution)/shard_map/ppermute | solution.py:60
  671.7 114.4 %collective-permute-start.77 = (bf16[128,3072]{1,0:T(8,128)(2,1)}, bf16[128,3072]{1,0:T(8,128)(2,1)}, u32[]{:S(2)}, u32[]{:S(2)}) collective-permute-start(bf16[128,3072]{1,0:T(8,128)(2,1)} %bitcast.331), channel_id=1, source_target_pairs={{0,8},{2,10},{4,12},{6,14},{8,16},{10,18},{12,20},{14,22},{16,24},... | collective-permute-start | bytes 2359304 | tf_op jit(solution)/shard_map/ppermute | solution.py:60
  672.9 115.7 %collective-permute-start.78 = (bf16[128,3072]{1,0:T(8,128)(2,1)}, bf16[128,3072]{1,0:T(8,128)(2,1)}, u32[]{:S(2)}, u32[]{:S(2)}) collective-permute-start(bf16[128,3072]{1,0:T(8,128)(2,1)} %bitcast.113), channel_id=1, source_target_pairs={{0,16},{2,18},{4,20},{6,22},{8,24},{10,26},{12,28},{14,30},{16,0},... | collective-permute-start | bytes 2359304 | tf_op jit(solution)/shard_map/ppermute | solution.py:60
  674.6 116.5 %collective-permute-start.79 = (bf16[128,3072]{1,0:T(8,128)(2,1)}, bf16[128,3072]{1,0:T(8,128)(2,1)}, u32[]{:S(2)}, u32[]{:S(2)}) collective-permute-start(bf16[128,3072]{1,0:T(8,128)(2,1)} %bitcast.118), channel_id=1, source_target_pairs={{0,24},{2,26},{4,28},{6,30},{8,0},{10,2},{12,4},{14,6},{16,8},{18,... | collective-permute-start | bytes 2359304 | tf_op jit(solution)/shard_map/ppermute | solution.py:60
  806.1 48.5 %collective-permute-start.59 = (bf16[2,128,3072]{1,2,0:T(8,128)(2,1)}, bf16[2,128,3072]{1,2,0:T(8,128)(2,1)}, u32[]{:S(2)}, u32[]{:S(2)}) collective-permute-start(bf16[2,128,3072]{1,2,0:T(8,128)(2,1)} %bitcast.277), channel_id=1, source_target_pairs={{0,4},{2,6},{4,0},{6,2},{8,12},{10,14},{12,8},{14,10},{16,20},{18,... | collective-permute-start | bytes 4718600 | tf_op jit(solution)/shard_map/ppermute | solution.py:63
  808.6 105.5 %collective-permute-start.56 = (bf16[2,128,3072]{1,2,0:T(8,128)(2,1)}, bf16[2,128,3072]{1,2,0:T(8,128)(2,1)}, u32[]{:S(2)}, u32[]{:S(2)}) collective-permute-start(bf16[2,128,3072]{1,2,0:T(8,128)(2,1)} %bitcast.279), channel_id=1, source_target_pairs={{0,2},{2,0},{4,6},{6,4},{8,10},{10,8},{12,14},{14,12},{16,18},{18,... | collective-permute-start | bytes 4718600 | tf_op jit(solution)/shard_map/ppermute | solution.py:63
  820.4 91.2 %collective-permute-start.61 = (bf16[2,128,3072]{1,2,0:T(8,128)(2,1)}, bf16[2,128,3072]{1,2,0:T(8,128)(2,1)}, u32[]{:S(2)}, u32[]{:S(2)}) collective-permute-start(bf16[2,128,3072]{1,2,0:T(8,128)(2,1)} %fusion.25), channel_id=1, source_target_pairs={{0,2},{2,0},{4,6},{6,4},{8,10},{10,8},{12,14},{14,12},{16,18},{18,... | collective-permute-start | bytes 4718600 | tf_op jit(solution)/shard_map/ppermute | solution.py:63
  838.6 75.5 %collective-permute-start.58 = (bf16[2,128,3072]{1,2,0:T(8,128)(2,1)}, bf16[2,128,3072]{1,2,0:T(8,128)(2,1)}, u32[]{:S(2)}, u32[]{:S(2)}) collective-permute-start(bf16[2,128,3072]{1,2,0:T(8,128)(2,1)} %fusion.27), channel_id=1, source_target_pairs={{0,4},{2,6},{4,0},{6,2},{8,12},{10,14},{12,8},{14,10},{16,20},{18,... | collective-permute-start | bytes 4718600 | tf_op jit(solution)/shard_map/ppermute | solution.py:63
  851.3 72.7 %collective-permute-start.54 = (bf16[192,1024]{1,0:T(8,128)(2,1)S(1)}, bf16[192,1024]{1,0:T(8,128)(2,1)S(1)}, u32[]{:S(2)}, u32[]{:S(2)}) collective-permute-start(bf16[192,1024]{1,0:T(8,128)(2,1)S(1)} %slice.353), channel_id=1, source_target_pairs={{2,0},{4,2},{6,4},{8,6},{10,8},{12,10},{14,12},{16,14},{18,16},{20... | collective-permute-start | bytes 1179656 | tf_op jit(solution)/shard_map/ppermute | solution.py:300
  919.2 90.2 %collective-permute-start.62 = (bf16[128,3072]{0,1:T(8,128)(2,1)}, bf16[128,3072]{0,1:T(8,128)(2,1)}, u32[]{:S(2)}, u32[]{:S(2)}) collective-permute-start(bf16[128,3072]{0,1:T(8,128)(2,1)} %get-tuple-element.91), channel_id=1, source_target_pairs={{0,8},{2,10},{4,12},{6,14},{8,16},{10,18},{12,20},{14,22},{16,24},... | collective-permute-start | bytes 2359304 | tf_op jit(solution)/shard_map/ppermute | solution.py:60
  919.6 89.7 %collective-permute-start.63 = (bf16[128,3072]{0,1:T(8,128)(2,1)}, bf16[128,3072]{0,1:T(8,128)(2,1)}, u32[]{:S(2)}, u32[]{:S(2)}) collective-permute-start(bf16[128,3072]{0,1:T(8,128)(2,1)} %get-tuple-element.92), channel_id=1, source_target_pairs={{0,16},{2,18},{4,20},{6,22},{8,24},{10,26},{12,28},{14,30},{16,0},... | collective-permute-start | bytes 2359304 | tf_op jit(solution)/shard_map/ppermute | solution.py:60
  921.0 88.4 %collective-permute-start.64 = (bf16[128,3072]{0,1:T(8,128)(2,1)}, bf16[128,3072]{0,1:T(8,128)(2,1)}, u32[]{:S(2)}, u32[]{:S(2)}) collective-permute-start(bf16[128,3072]{0,1:T(8,128)(2,1)} %get-tuple-element.93), channel_id=1, source_target_pairs={{0,24},{2,26},{4,28},{6,30},{8,0},{10,2},{12,4},{14,6},{16,8},{18,... | collective-permute-start | bytes 2359304 | tf_op jit(solution)/shard_map/ppermute | solution.py:60
  (123 other events, 2340.9 us)
Sparse Core Ops, SparseCore 0:
  926.1 81.1 reduce-scatter.3

commit v2 on v1

--- a/solution.py
+++ b/solution.py
@@ -1,4 +1,8 @@
+import functools
+
 import jax
+import jax.experimental.pallas as pl
+import jax.experimental.pallas.tpu as pltpu
 import jax.numpy as jnp
 from jax import lax
 from jax.sharding import PartitionSpec as P
@@ -11,6 +15,8 @@
 ROPE_BASE = 1000042.0
 BF16 = jnp.bfloat16
 F32 = jnp.float32
+MESH = pl.DeviceIdType.MESH
+ANY = pl.BlockSpec(memory_space=pl.ANY)
 
 
 def matmul(left, right):
@@ -95,16 +101,506 @@
         return held[0]
 
 
-def gather_pieces(links, pieces, rows):
-    columns = pieces[0].shape[1]
+def flip(place, key):
+    bit = 1
+    while bit <= key:
+        if key & bit:
+            place = place + bit * (1 - 2 * lax.rem(lax.div(place, bit), 2))
+        bit *= 2
+    return place
+
+
+def gather_kernel(plane, wq, wk, wv, wo, wg, wu, wd, tok, attn, ffn, ext,
+                  own_sem, zs, zr, ps, pr, fs, fr, ts, tr):
+    rows, tok_rows, width = wq.shape[0], tok.shape[0], tok.shape[1]
+    count = plane * LINE
+    halo = ext.shape[0] - tok_rows
+    chunk = wd.shape[1] // LINE
+    bits = [1 << b for b in range(plane.bit_length() - 1)]
+    device, half = lax.axis_index("dp"), lax.axis_index("tensor")
+    line, place = lax.div(device, plane), lax.rem(device, plane)
+
+    greet = [lax.rem(line + k, LINE) * plane + place for k in range(1, LINE)]
+    greet += [line * plane + flip(place, bit) for bit in bits]
+    greet += [lax.rem(device + 1, count), lax.rem(device + count - 1, count)]
+    barrier = pltpu.get_barrier_semaphore()
+    for peer in greet:
+        pl.semaphore_signal(barrier, 1, device_id=(peer, half), device_id_type=MESH)
+    pl.semaphore_signal(barrier, 1, device_id=(device, 1 - half), device_id_type=MESH)
+
+    def remote(src, dst, sent, got, peer, core=half):
+        return pltpu.make_async_remote_copy(
+            src_ref=src, dst_ref=dst, send_sem=sent, recv_sem=got,
+            device_id=(peer, core), device_id_type=MESH,
+        )
+
+    mine = pl.ds(pl.multiple_of(device * rows, rows), rows)
+    own, at = [], 0
+    for block in (wq, wk, wv, wo):
+        wide = block.shape[1]
+        own.append(pltpu.make_async_copy(block, attn.at[mine, pl.ds(at, wide)], own_sem.at[len(own)]))
+        at += wide
+    from_line = pl.ds(pl.multiple_of(line * rows, rows), rows)
+
+    def hidden(block, member):
+        return block.at[:, pl.ds(pl.multiple_of(member * chunk, chunk), chunk)]
+
+    for j, block in enumerate((wg, wu, wd)):
+        own.append(
+            pltpu.make_async_copy(
+                hidden(block, line), ffn.at[from_line, pl.ds(j * chunk, chunk)], own_sem.at[len(own)]
+            )
+        )
+    features = pl.ds(pl.multiple_of(half * width, width), width)
+    own.append(pltpu.make_async_copy(tok, ext.at[pl.ds(halo, tok_rows), features], own_sem.at[len(own)]))
+    for copy in own:
+        copy.start()
+    first = pltpu.make_async_copy(
+        tok.at[pl.ds(0, halo)], ext.at[pl.ds(0, halo), features], own_sem.at[len(own)]
+    )
+    pl.semaphore_wait(barrier, len(greet) + 1)
+
+    tok_cross = remote(tok, ext.at[pl.ds(halo, tok_rows), features], ts.at[0], tr.at[0], device, 1 - half)
+    tok_next = remote(
+        tok.at[pl.ds(tok_rows - halo, halo)], ext.at[pl.ds(0, halo), features], ts.at[1], tr.at[1], device + 1
+    )
+    tok_relay = remote(
+        ext.at[pl.ds(0, halo), features], ext.at[pl.ds(0, halo), features], ts.at[2], tr.at[2], device, 1 - half
+    )
+    for copy in own[:4]:
+        copy.wait()
+
+    def line_copy(origin, step):
+        block = attn.at[pl.ds(pl.multiple_of((origin * plane + place) * rows, rows), rows)]
+        return remote(block, block, zs.at[(step + 1) // 2, origin], zr.at[origin], device + step * plane)
+
+    part = rows // 2
+
+    def keys_after(turn, stage):
+        keys = [0]
+        for bit in (bits[turn:] + bits[:turn])[:stage]:
+            keys += [key | bit for key in keys]
+        return keys
+
+    def plane_copy(origin, turn, key, bit):
+        block = attn.at[
+            pl.ds(pl.multiple_of((origin * plane + flip(place, key)) * rows + turn * part, part), part)
+        ]
+        sems = [s.at[origin, turn, key | bit] for s in (ps, pr)]
+        return remote(block, block, *sems, line * plane + flip(place, bit))
+
+    def spread(origin, stage):
+        for turn in range(2):
+            order = bits[turn:] + bits[:turn]
+            if stage:
+                for key in keys_after(turn, stage - 1):
+                    plane_copy(origin, turn, key, order[stage - 1]).wait_recv()
+            if stage < len(bits):
+                for key in keys_after(turn, stage):
+                    plane_copy(origin, turn, key, order[stage]).start()
+
+    def ffn_copies(k):
+        member = lax.rem(line + k, LINE)
+        return [
+            remote(
+                hidden(block, member), ffn.at[from_line, pl.ds(j * chunk, chunk)],
+                fs.at[k - 1, j], fr.at[k - 1, j], member * plane + place,
+            )
+            for j, block in enumerate((wg, wu, wd))
+        ]
+
+    slots = [(line, None, None)]
+    for d in range(1, LINE):
+        slots += [(line - d, line >= d, 1), (line + d, line + d < LINE, -1)]
+
+    def guarded(condition, action):
+        if condition is None:
+            action()
+        else:
+            pl.when(condition)(action)
+
+    def arrive(origin, step):
+        if step is not None:
+            line_copy(origin, step).wait_recv()
+        if step in (None, 1):
+            pl.when(line < LINE - 1)(lambda: line_copy(origin, 1).start())
+        if step in (None, -1):
+            pl.when(line > 0)(lambda: line_copy(origin, -1).start())
+        spread(origin, 0)
+
+    pl.when(device < count - 1)(lambda: tok_next.start())
+    for j in range(len(slots) + len(bits)):
+        if j < len(slots):
+            origin, condition, step = slots[j]
+            guarded(condition, functools.partial(arrive, origin, step))
+        if j == 0:
+            tok_cross.start()
+        if j in (2, 4, 6):
+            for copy in ffn_copies((1, 3, 2)[j // 2 - 1]):
+                copy.start()
+        for stage in range(1, len(bits) + 1):
+            if 0 <= j - stage < len(slots):
+                origin, condition, step = slots[j - stage]
+                guarded(condition, functools.partial(spread, origin, stage))
+        if j == 1:
+            pl.when(device == 0)(lambda: first.start())
+            pl.when(device == 0)(lambda: first.wait())
+            pl.when(device > 0)(lambda: tok_next.wait_recv())
+            tok_relay.start()
+
+    for origin in range(LINE):
+        pl.when((origin <= line) & (line < LINE - 1))(lambda o=origin: line_copy(o, 1).wait_send())
+        pl.when((origin >= line) & (line > 0))(lambda o=origin: line_copy(o, -1).wait_send())
+        for turn in range(2):
+            order = bits[turn:] + bits[:turn]
+            for stage, bit in enumerate(order):
+                for key in keys_after(turn, stage):
+                    plane_copy(origin, turn, key, bit).wait_send()
+    for k in range(1, LINE):
+        for copy in ffn_copies(k):
+            copy.wait()
+    pl.when(device < count - 1)(lambda: tok_next.wait_send())
+    tok_cross.wait()
+    tok_relay.wait()
+    for copy in own[4:]:
+        copy.wait()
+
+
+def gather_start(plane, tokens, wq, wk, wv, wo, wg, wu, wd):
+    rows = wq.shape[0]
+    chunk = wd.shape[1] // LINE
+    columns = sum(w.shape[1] for w in (wq, wk, wv, wo))
+    dma = pltpu.SemaphoreType.DMA
+    return pl.pallas_call(
+        functools.partial(gather_kernel, plane),
+        out_shape=(
+            jax.ShapeDtypeStruct((LINE * plane * rows, columns), BF16),
+            jax.ShapeDtypeStruct((LINE * rows, 3 * chunk), BF16),
+            jax.ShapeDtypeStruct((HALO + tokens.shape[0], 2 * tokens.shape[1]), BF16),
+        ),
+        in_specs=[ANY] * 8,
+        out_specs=[ANY] * 3,
+        scratch_shapes=[
+            dma((9,)), dma((2, LINE)), dma((LINE,)), dma((LINE, 2, plane)), dma((LINE, 2, plane)),
+            dma((LINE - 1, 3)), dma((LINE - 1, 3)), dma((3,)), dma((3,)),
+        ],
+        compiler_params=pltpu.CompilerParams(collective_id=1, has_side_effects=True),
+    )(wq, wk, wv, wo, wg, wu, wd, tokens)
+
+
+def spread_plane(links, own, rows):
+    columns = own.shape[1]
+    own = own.reshape(LINE, rows, columns)
     whole = jnp.zeros((LINE, links.plane, rows, columns), BF16)
-    for k, piece in enumerate(pieces):
-        origin = (links.line - k) % LINE
-        for key, part in links.spread(piece, k).items():
+    for turn in range(2):
+        for key, part in links.spread(own[2 * turn : 2 * turn + 2], turn).items():
             whole = lax.dynamic_update_slice(
-                whole, part[None, None], (origin, links.place ^ key, 0, 0)
+                whole, part[:, None], (2 * turn, flip(links.place, key), 0, 0)
             )
     return whole.reshape(-1, columns)
+
+
+def fold_plan(bits, turn):
+    order, plan, slot = bits[turn:] + bits[:turn], [], 0
+    for stage, bit in enumerate(order):
+        keys = [0]
+        for later in order[stage + 1 :]:
+            keys += [key | later for key in keys]
+        plan.append((bit, keys, slot))
+        slot += len(keys)
+    return plan
+
+
+def finish_kernel(plane, gq, gkv, go, fsum, grad_mine, grad_theirs, mixed_grad, tok, rms, gain, gain_two,
+                  total, fout, tok_grad, gains,
+                  recv, sendbuf, acc, zsend, zrecv, gx, hsend, hrecv, nag, inner, inner_in, gbuf, gin,
+                  own_sem, s0, r0, zs, zr, fs, fr, cs, cr, gs, gr):
+    rows = total.shape[0]
+    segment = gq.shape[1]
+    count = plane * LINE
+    tok_rows, width = tok.shape
+    halo = grad_mine.shape[0] - tok_rows
+    chunk = fsum.shape[2] // 3
+    part = rows // 2
+    bits = [1 << b for b in range(plane.bit_length() - 1)]
+    device, half = lax.axis_index("dp"), lax.axis_index("tensor")
+    line, place = lax.div(device, plane), lax.rem(device, plane)
+
+    greet = [lax.rem(line + k, LINE) * plane + place for k in range(1, LINE)]
+    greet += [line * plane + flip(place, bit) for bit in bits]
+    greet += [lax.rem(device + 1, count), lax.rem(device + count - 1, count)]
+    barrier = pltpu.get_barrier_semaphore()
+    for peer in greet:
+        pl.semaphore_signal(barrier, 1, device_id=(peer, half), device_id_type=MESH)
+    pl.semaphore_signal(barrier, 1, device_id=(device, 1 - half), device_id_type=MESH)
+
+    def remote(src, dst, sent, got, peer, core=half):
+        return pltpu.make_async_remote_copy(
+            src_ref=src, dst_ref=dst, send_sem=sent, recv_sem=got,
+            device_id=(peer, core), device_id_type=MESH,
+        )
+
+    def member(c):
+        return lax.rem(line + c, LINE)
+
+    def hidden(origin):
+        return pl.ds(pl.multiple_of(origin * chunk, chunk), chunk)
+
+    def ffn_copy(c, j):
+        return remote(
+            fsum.at[member(c), :, pl.ds(j * chunk, chunk)], fout.at[j, :, hidden(line)],
+            fs.at[c - 1, j], fr.at[c - 1, j], member(c) * plane + place,
+        )
+
+    own = [
+        pltpu.make_async_copy(fsum.at[line, :, pl.ds(j * chunk, chunk)], fout.at[j, :, hidden(line)], own_sem.at[j])
+        for j in range(3)
+    ]
+    for copy in own:
+        copy.start()
+    pl.semaphore_wait(barrier, len(greet) + 1)
+
+    plans = [fold_plan(bits, turn) for turn in range(2)]
+    stages, later = len(bits), plane // 2
+
+    def raw(ref, c, turn, key):
+        at = (member(c) * plane + flip(place, key)) * rows + turn * part
+        return ref.at[pl.ds(pl.multiple_of(at, part), part)]
+
+    def fold_copies(c, turn, stage):
+        bit, keys, slot = plans[turn][stage]
+        peer = line * plane + flip(place, bit)
+        out = []
+        for j, key in enumerate(keys):
+            sems = (s0.at[c, turn, slot + j], r0.at[c, turn, slot + j])
+            dst = recv.at[c, turn, slot + j]
+            if stage == 0:
+                for g, ref in enumerate((gq, gkv, go)):
+                    out.append(remote(raw(ref, c, turn, key | bit), dst.at[:, pl.ds(g * segment, segment)], *sems, peer))
+            else:
+                out.append(remote(sendbuf.at[c, turn, slot - later + j], dst, *sems, peer))
+        return out
+
+    def fold_wait(c, turn, stage, sent):
+        bit, keys, slot = plans[turn][stage]
+        for j in range(len(keys)):
+            whole = recv.at[c, turn, slot + j]
+            copy = remote(whole, whole, s0.at[c, turn, slot + j], r0.at[c, turn, slot + j], line * plane + flip(place, bit))
+            if sent:
+                copy.wait_send()
+            else:
+                copy.wait_recv()
+
+    step = 16
+
+    def fold_add(c, turn, stage):
+        bit, keys, slot = plans[turn][stage]
+        last = stage == len(plans[turn]) - 1
+        sends = {}
+        if not last:
+            next_bit, next_keys, next_slot = plans[turn][stage + 1]
+            sends = {key | next_bit: next_slot - later + j for j, key in enumerate(next_keys)}
+
+        def body(i, carry):
+            at = pl.ds(pl.multiple_of(i * step, step), step)
+            for j, key in enumerate(keys):
+                for g, ref in enumerate((gq, gkv, go)):
+                    columns = pl.ds(g * segment, segment)
+                    got = recv[c, turn, slot + j, at, columns].astype(F32)
+                    if stage == 0:
+                        had = raw(ref, c, turn, key)[at, :].astype(F32)
+                    else:
+                        had = acc[c, turn, key_slot[key], at, columns]
+                    value = had + got
+                    if last and c:
+                        zsend[c - 1, pl.ds(pl.multiple_of(turn * part + i * step, step), step), columns] = value.astype(BF16)
+                    elif last:
+                        total[pl.ds(pl.multiple_of(turn * part + i * step, step), step), columns] = value
+                    elif key in sends:
+                        sendbuf[c, turn, sends[key], at, columns] = value.astype(BF16)
+                    else:
+                        acc[c, turn, key_slot[key], at, columns] = value
+            return carry
+
+        stay = [key for key in plans[turn][0][1] if not key & plans[turn][min(1, stages - 1)][0]]
+        key_slot = {key: j for j, key in enumerate(stay)}
+        lax.fori_loop(0, part // step, body, 0)
+
+    def z_copy(c, turn):
+        at = pl.ds(turn * part, part)
+        return remote(
+            zsend.at[c - 1, at], zrecv.at[c - 1, at], zs.at[c - 1, turn], zr.at[c - 1, turn], member(c) * plane + place
+        )
+
+    core_copy = remote(grad_theirs, gx, cs.at[0], cr.at[0], device, 1 - half)
+    halo_copy = remote(hsend, hrecv, cs.at[1], cr.at[1], device - 1)
+    inner_copy = remote(inner, inner_in, cs.at[2], cr.at[2], device, 1 - half)
+    core_copy.start()
+
+    turns = (2, 1, 3, 0)
+
+    def start(c, stage):
+        for turn in range(2):
+            for copy in fold_copies(c, turn, stage):
+                copy.start()
+
+    start(turns[0], 0)
+    start(turns[1], 0)
+    for c in range(1, LINE):
+        for j in range(3):
+            ffn_copy(c, j).start()
+
+    core_copy.wait()
+
+    def rows_of(i):
+        return pl.ds(pl.multiple_of(i * step, step), step)
+
+    def add_halo(i, carry):
+        hsend[rows_of(i)] = (grad_mine[rows_of(i)] + gx[rows_of(i)].astype(F32)).astype(BF16)
+        return carry
+
+    def add_own(i, carry):
+        at = pl.ds(pl.multiple_of(halo + i * step, step), step)
+        nag[rows_of(i)] = grad_mine[at] + gx[at].astype(F32)
+        return carry
+
+    def add_behind(i, carry):
+        at = pl.ds(pl.multiple_of(tok_rows - halo + i * step, step), step)
+        nag[at] = nag[at] + hrecv[rows_of(i)].astype(F32)
+        return carry
+
+    def local_sums(i, carry):
+        at = rows_of(i)
+        grad, x = nag[at], tok[at].astype(F32)
+        weighted = jnp.sum(grad * gain[...] * x, axis=1, keepdims=True)
+        inner[at] = jnp.broadcast_to(weighted, (step, inner.shape[1]))
+        product = grad * x * rms[at]
+        return carry + product[:8] + product[8:]
+
+    def last_norm(i, carry):
+        at = rows_of(i)
+        r = rms[at]
+        whole = (inner[at] + inner_in[at])[:, :1]
+        value = mixed_grad[at] + r * gain[...] * nag[at] - tok[at].astype(F32) * (r * r * r * whole / (2 * width))
+        tok_grad[at] = value.astype(BF16)
+        return carry
+
+    def norm_first():
+        lax.fori_loop(0, halo // step, add_halo, 0)
+        pl.when(device > 0)(lambda: halo_copy.start())
+        lax.fori_loop(0, tok_rows // step, add_own, 0)
+
+    def norm_second():
+        @pl.when(device < count - 1)
+        def _():
+            halo_copy.wait_recv()
+            lax.fori_loop(0, halo // step, add_behind, 0)
+
+        sums = lax.fori_loop(0, tok_rows // step, local_sums, jnp.zeros((8, width), F32))
+        gbuf[...] = jnp.concatenate(
+            [jnp.sum(sums, axis=0, keepdims=True), gain_two[...], jnp.zeros((6, width), F32)], axis=0
+        )
+        inner_copy.start()
+
+    def gain_copy(j):
+        peer = line * plane + flip(place, bits[j]) if j < stages else member(j - stages + 1) * plane + place
+        return remote(gbuf, gin.at[j], gs.at[j], gr.at[j], peer)
+
+    def norm_third():
+        inner_copy.wait()
+        lax.fori_loop(0, tok_rows // step, last_norm, 0)
+
+    norm_first()
+
+    pending = []
+    for j in range(len(turns) + stages):
+        if j < len(turns):
+            if j + 2 < len(turns):
+                start(turns[j + 2], 0)
+        for stage in range(stages):
+            if 0 <= j - stage < len(turns):
+                c = turns[j - stage]
+                for turn in range(2):
+                    fold_wait(c, turn, stage, False)
+                    fold_add(c, turn, stage)
+                    if stage + 1 < stages:
+                        for copy in fold_copies(c, turn, stage + 1):
+                            copy.start()
+                    elif c:
+                        z_copy(c, turn).start()
+        if j == 0:
+            norm_second()
+        elif j <= stages:
+            if j > 1:
+                gain_copy(j - 2).wait()
+                gbuf[...] = gbuf[...] + gin[j - 2]
+            gain_copy(j - 1).start()
+            if j == 1:
+                norm_third()
+
+    gain_copy(stages - 1).wait()
+    gbuf[...] = gbuf[...] + gin[stages - 1]
+    for k in range(stages, stages + LINE - 1):
+        gain_copy(k).start()
+    for k in range(stages, stages + LINE - 1):
+        gain_copy(k).wait()
+    gains[...] = gbuf[...] + sum(gin[k] for k in range(stages, stages + LINE - 1))
+
+    for c in range(1, LINE):
+        for turn in range(2):
+            z_copy(c, turn).wait()
+
+    def add_line(i, carry):
+        at = rows_of(i)
+        total[at] = total[at] + sum(zrecv[c, at].astype(F32) for c in range(LINE - 1))
+        return carry
+
+    lax.fori_loop(0, rows // step, add_line, 0)
+    for c in range(LINE):
+        for turn in range(2):
+            for stage in range(stages):
+                fold_wait(c, turn, stage, True)
+    for c in range(1, LINE):
+        for j in range(3):
+            ffn_copy(c, j).wait()
+    pl.when(device > 0)(lambda: halo_copy.wait_send())
+    for copy in own:
+        copy.wait()
+
+
+def finish(plane, gq, gkv, go, fsum, grad_mine, grad_theirs, mixed_grad, tok, rms, gain, gain_two):
+    columns = 3 * gq.shape[1]
+    rows, chunk = fsum.shape[1], fsum.shape[2] // 3
+    part = rows // 2
+    tok_rows, width = tok.shape
+    bits = plane.bit_length() - 1
+    dma, vmem = pltpu.SemaphoreType.DMA, pltpu.VMEM
+    kept = plane - 1
+    inside = pl.BlockSpec(memory_space=pltpu.VMEM)
+    return pl.pallas_call(
+        functools.partial(finish_kernel, plane),
+        out_shape=(
+            jax.ShapeDtypeStruct((rows, columns), F32),
+            jax.ShapeDtypeStruct((3, rows, LINE * chunk), BF16),
+            jax.ShapeDtypeStruct((tok_rows, width), BF16),
+            jax.ShapeDtypeStruct((8, width), F32),
+        ),
+        in_specs=[inside] * 3 + [ANY] + [inside] * 7,
+        out_specs=[inside, ANY, inside, inside],
+        scratch_shapes=[
+            vmem((LINE, 2, kept, part, columns), BF16), vmem((LINE, 2, kept - plane // 2, part, columns), BF16),
+            vmem((LINE, 2, plane // 4, part, columns), F32), vmem((LINE - 1, rows, columns), BF16),
+            vmem((LINE - 1, rows, columns), BF16), vmem(grad_theirs.shape, BF16), vmem((HALO, width), BF16),
+            vmem((HALO, width), BF16), vmem((tok_rows, width), F32), vmem((tok_rows, 128), F32),
+            vmem((tok_rows, 128), F32), vmem((8, width), F32), vmem((bits + LINE - 1, 8, width), F32),
+            dma((3,)), dma((LINE, 2, kept)), dma((LINE, 2, kept)), dma((LINE - 1, 2)), dma((LINE - 1, 2)),
+            dma((LINE - 1, 3)), dma((LINE - 1, 3)), dma((3,)), dma((3,)),
+            dma((bits + LINE - 1,)), dma((bits + LINE - 1,)),
+        ],
+        compiler_params=pltpu.CompilerParams(
+            collective_id=2, has_side_effects=True, vmem_limit_bytes=60 * 2**20
+        ),
+    )(gq, gkv, go, fsum, grad_mine, grad_theirs, mixed_grad, tok, rms, gain, gain_two)
 
 
 def fold_plane(links, grads, rows):
@@ -114,7 +610,7 @@
     for turn in range(2):
         half = parts[turn * 2 : turn * 2 + 2]
         held = {
-            key: lax.dynamic_slice_in_dim(half, links.place ^ key, 1, 1)[:, 0]
+            key: lax.dynamic_slice_in_dim(half, flip(links.place, key), 1, 1)[:, 0]
             for key in range(links.plane)
         }
         out.append(links.fold(held, turn))
@@ -144,22 +640,10 @@
     ff_half = w_gate.shape[1]
     chunk = ff_half // LINE
 
-    attn_mine = jnp.concatenate([w_query, w_key, w_value, w_output.T], axis=1)
-    attn_all = gather_pieces(
-        links, [attn_mine] + [links.step(attn_mine, k) for k in range(1, LINE)], rows
-    )
-    ffn_mine = jnp.stack(
-        [w_gate.reshape(rows, LINE, chunk), w_up.reshape(rows, LINE, chunk), w_down.T.reshape(rows, LINE, chunk)],
-        axis=2,
-    ).reshape(rows, LINE, 3 * chunk)
-
-    def for_line(k):
-        target = (links.line + k) % LINE
-        return lax.dynamic_slice_in_dim(ffn_mine, target, 1, 1)[:, 0]
-
-    ffn_all = gather_pieces(
-        links, [for_line(0)] + [links.step(for_line(k), k) for k in range(1, LINE)], rows
-    )
+    attn_all, ffn_own, tokens_ext = gather_start(
+        links.plane, tokens, w_query, w_key, w_value, w_output.T, w_gate, w_up, w_down.T
+    )
+    ffn_all = spread_plane(links, ffn_own, rows)
     w_gate_up, w_down_t = ffn_all[:, : 2 * chunk], ffn_all[:, 2 * chunk :]
 
     def line_gather(x):
@@ -173,8 +657,7 @@
         return total
 
     n = links.count
-    before = lax.ppermute(tokens[count - HALO :], "dp", [(d, d + 1) for d in range(n - 1)])
-    tokens_ext = links.both(jnp.concatenate([before, tokens], axis=0)).astype(F32)
+    tokens_ext = tokens_ext.astype(F32)
     cot_line = links.both(line_gather(cotangent))
 
     seq_ids = jnp.arange(lengths.shape[0])
@@ -236,7 +719,10 @@
     gate_act_grad = (hidden_grad * upward * sigmoid * (1.0 + gate * (1.0 - sigmoid))).astype(BF16)
     up_act_grad = (hidden_grad * silu_gate).astype(BF16)
     act_grad = jnp.concatenate([gate_act_grad, up_act_grad], axis=1)
-    norm_mine, norm_theirs = links.halves(matmul_t(act_grad, w_gate_up))
+    norm_part, act_grad, hidden = lax.optimization_barrier(
+        (matmul_t(act_grad, w_gate_up), act_grad, hidden)
+    )
+    norm_mine, norm_theirs = links.halves(norm_part)
     normed_ffn_grad = line_sum(norm_mine + links.swap(norm_theirs.astype(BF16)).astype(F32))
     ffn_mine_out, ffn_theirs_out = links.halves(matmul_t(hidden, w_down_t))
     ffn_out = line_sum(ffn_mine_out + links.swap(ffn_theirs_out.astype(BF16)).astype(F32))
@@ -245,17 +731,6 @@
     down_sum = fold_plane(links, t_matmul(cot_line, hidden).astype(BF16), rows)
     gate_up_sum = fold_plane(links, t_matmul(normed_ffn, act_grad).astype(BF16), rows)
     ffn_sum = jnp.concatenate([gate_up_sum, down_sum], axis=2).astype(BF16)
-    ffn_grads = jnp.zeros((3, rows, LINE, chunk), F32)
-    for k in range(LINE):
-        part = lax.dynamic_slice_in_dim(ffn_sum, (links.line + k) % LINE, 1, 0)[0]
-        if k:
-            part = links.step(part, k)
-        part = part.astype(F32).reshape(rows, 3, chunk).transpose(1, 0, 2)
-        ffn_grads = lax.dynamic_update_slice(
-            ffn_grads, part[:, :, None], (0, 0, (links.line - k) % LINE, 0)
-        )
-    ffn_grads = ffn_grads.reshape(3, rows, ff_half)
-
     ffn_gain_local = jnp.sum(normed_ffn_grad * mixed * rms_two, axis=0)
     inner_two = row_sum(normed_ffn_grad * gain_two * mixed)
     mixed_grad = (
@@ -283,34 +758,26 @@
     queries_grad = rotate_back(rot_q_grad, cos_q, sin_q).astype(BF16).reshape(count, q_width)
     keys_grad = rotate_back(rot_k_grad, cos_k, sin_k).astype(BF16).reshape(ext, k_width)
     kv_grad = jnp.concatenate([keys_grad, values_grad], axis=1)
-    attn_local = jnp.concatenate(
-        [t_matmul(normed_attn[HALO:], queries_grad), t_matmul(normed_attn, kv_grad), out_local],
-        axis=1,
-    )
-    attn_sum = fold_plane(links, attn_local.astype(BF16), rows)
-    attn_total = lax.dynamic_slice_in_dim(attn_sum, links.line, 1, 0)[0]
-    for k in range(1, LINE):
-        part = lax.dynamic_slice_in_dim(attn_sum, (links.line + k) % LINE, 1, 0)[0]
-        attn_total += links.step(part.astype(BF16), k).astype(F32)
-
     normed_grad = matmul_t(kv_grad, w_kv)
     normed_grad = normed_grad + jnp.pad(matmul_t(queries_grad, w_q), ((HALO, 0), (0, 0)))
     grad_mine, grad_theirs = links.halves(normed_grad)
-    grad_half = grad_mine + links.swap(grad_theirs.astype(BF16)).astype(F32)
-    behind = lax.ppermute(grad_half[:HALO].astype(BF16), "dp", [(d + 1, d) for d in range(n - 1)])
-    normed_attn_grad = grad_half[HALO:] + jnp.pad(behind.astype(F32), ((count - HALO, 0), (0, 0)))
-    rms_mine = rms_one[HALO:]
-    gain_mine = attn_gain.astype(F32)[None, :]
-    attn_gain_local = jnp.sum(normed_attn_grad * tokens_half * rms_mine, axis=0)
-    inner_one = row_sum(normed_attn_grad * gain_mine * tokens_half)
-    tokens_grad = (
-        mixed_grad
-        + rms_mine * gain_mine * normed_attn_grad
-        - tokens_half * rms_mine * rms_mine * rms_mine * inner_one / width
-    ).astype(BF16)
-
-    gains = jnp.stack([attn_gain_local, ffn_gain_local])
-    gains = lax.psum_scatter(gains, "dp", scatter_dimension=1, tiled=True)
+    attn_total, ffn_bf16, tokens_grad, gains = finish(
+        links.plane,
+        t_matmul(normed_attn[HALO:], queries_grad).astype(BF16),
+        t_matmul(normed_attn, kv_grad).astype(BF16),
+        out_local.astype(BF16),
+        ffn_sum,
+        grad_mine,
+        grad_theirs.astype(BF16),
+        mixed_grad,
+        tokens,
+        rms_one[HALO:],
+        attn_gain.astype(F32)[None, :],
+        ffn_gain_local[None, :],
+    )
+    ffn_grads = ffn_bf16.astype(F32)
+    share = half_width // n
+    gains = lax.dynamic_slice_in_dim(gains[:2], links.index * share, share, 1)
     return (
         output,
         tokens_grad,

time: 1040 us -> 831 us (0.80)
  Pallas kernels: 0 us -> 346 us
  waiting for transfers between devices: 439 us -> 233 us
  local copies, waits for them, and re-layouts: 239 us -> 63.7 us
  starting transfers between devices: 139 us -> 30.2 us
  other arithmetic: 87.6 us -> 47.5 us
  between operations: 15.9 us -> 1.72 us
    pallas_call x0 -> x2, Pallas kernels: none -> 346 us  [the longest x1 178 us: finish(): pl.pallas_call(functools.partial(finish_kernel, plane), out_shape=(jax.Sh...]
    ppermute x42 -> x18, waiting for transfers between devices: 259 us -> 148 us  [cross(): return lax.ppermute(x, 'dp', [(d, d ^ bit) for d in range(self.count)])]
    unnamed x2 -> x0, waiting for transfers between devices: 77.3 us -> none
    ppermute x24 -> x12, starting transfers between devices: 81.9 us -> 12.1 us  [step(): return lax.ppermute(x, 'dp', [(d, (d + shift) % n) for d in range(n)])]
    dynamic_slice x24 -> x2, local copies, waits for them, and re-layouts: 68.4 us -> 1.52 us  [the longest x1 1.45 us: halves(): mine = lax.dynamic_slice_in_dim(x, self.half * width, width, 1)]
    dynamic_update_slice x34 -> x8, local copies, waits for them, and re-layouts: 43.9 us -> 9.09 us  [spread_plane(): lax.dynamic_update_slice(whole, part[:, None], (2 * turn, flip(links.plac...]
    ppermute x42 -> x18, starting transfers between devices: 50 us -> 18 us  [cross(): return lax.ppermute(x, 'dp', [(d, d ^ bit) for d in range(self.count)])]
    slice x5 -> x2, local copies, waits for them, and re-layouts: 31.2 us -> 1.32 us  [fold_plane(): half = parts[turn * 2:turn * 2 + 2]]
  transfers between devices with their start and end apart: 81 -> 39, of which waited for: 30 -> 17; matrix products, arithmetic and copies ran while one was open for 35% -> 13% of each run, Pallas kernels for 0% -> 20%
where the time goes in v2:
time: 831 us; the launch traced here: 821 us
  Pallas kernels  346 us (42%)
  waiting for transfers between devices  233 us (28%)
  matrix products  98.4 us (12%)
  local copies, waits for them, and re-layouts  63.7 us (8%)
  other arithmetic  47.5 us (6%)
  starting transfers between devices  30.2 us (4%)
    pallas_call x1, Pallas kernels, finish(): pl.pallas_call(functools.partial(finish_kernel, plane), out_shape=(jax.Sh...  178 us
    pallas_call x1, Pallas kernels, gather_start(): pl.pallas_call(functools.partial(gather_kernel, plane), out_shape=(jax.Sh...  168 us
    ppermute x18, waiting for transfers between devices, cross(): return lax.ppermute(x, 'dp', [(d, d ^ bit) for d in range(self.count)])  148 us
    ppermute x12, waiting for transfers between devices, step(): return lax.ppermute(x, 'dp', [(d, (d + shift) % n) for d in range(n)])  84.6 us
    dot_general x5, matrix products, matmul(): return jnp.dot(left, right, preferred_element_type=F32)  37.6 us
    dot_general x5, matrix products, t_matmul(): lax.dot_general(left, right, (((0,), (0,)), ((), ())), preferred_element_...  28.2 us
    dot_general x5, matrix products, matmul_t(): lax.dot_general(left, right, (((1,), (1,)), ((), ())), preferred_element_...  27.3 us
    ppermute x18, starting transfers between devices, cross(): return lax.ppermute(x, 'dp', [(d, d ^ bit) for d in range(self.count)])  18 us
  transfers between devices with their start and end apart: 39, of which 17 were waited for; matrix products, arithmetic and copies ran while one was open for 13% of the time, Pallas kernels for 20%

profile of v2, /device:TPU:2, one launch (start us, length us, event | category | flops | bytes accessed | tf_op | source)
XLA Modules:
  0.0 820.7 jit_solution(12010557489278114633)
XLA Ops:
  9.8 168.0 %shard_map.203 = (bf16[2048,3072]{1,0:T(8,128)(2,1)}, bf16[512,3072]{1,0:T(8,128)(2,1)}, bf16[448,2048]{1,0:T(8,128)(2,1)}) custom-call(bf16[128,1024]{1,0:T(8,128)(2,1)} %wq.1, bf16[128,512]{1,0:T(8,128)(2,1)} %wk.1, bf16[128,512]{1,0:T(8,128)(2,1)} %wv.1, bf16[128,1024]{1,0:T(8,128)(2,1)} %bitcast.206, bf16[128,4096]{1,0:T(8,128)(2,1)} %wg.1, ...), custom_call_target="tpu_custom_call" | custom-call | tf_op jit(solution)/shard_map/pallas_call | solution.py:274
  182.2 5.1 fusion.16
  187.3 4.3 fusion.20
  205.5 3.8 fusion.12
  217.3 6.2 broadcast_in_dim.106
  231.7 8.5 %collective-permute-done.4 = bf16[256,1024]{1,0:T(8,128)(2,1)S(1)} collective-permute-done((bf16[256,1024]{1,0:T(8,128)(2,1)S(1)}, bf16[256,1024]{1,0:T(8,128)(2,1)S(1)}, u32[]{:S(2)}, u32[]{:S(2)}) %collective-permute-start.4) | collective-permute-done | bytes 524320 | tf_op jit(solution)/shard_map/ppermute | solution.py:66
  244.8 4.2 collective-permute-done.6
  252.6 30.4 %collective-permute-done.9 = bf16[2,128,3072]{2,1,0:T(8,128)(2,1)S(1)} collective-permute-done((bf16[2,128,3072]{2,1,0:T(8,128)(2,1)S(1)}, bf16[2,128,3072]{2,1,0:T(8,128)(2,1)S(1)}, u32[]{:S(2)}, u32[]{:S(2)}) %collective-permute-start.9) | collective-permute-done | bytes 1572896 | tf_op jit(solution)/shard_map/ppermute | solution.py:69
  287.8 8.4 %collective-permute-done.15 = bf16[256,1024]{1,0:T(8,128)(2,1)S(1)} collective-permute-done((bf16[256,1024]{1,0:T(8,128)(2,1)S(1)}, bf16[256,1024]{1,0:T(8,128)(2,1)S(1)}, u32[]{:S(2)}, u32[]{:S(2)}) %collective-permute-start.15) | collective-permute-done | bytes 524320 | tf_op jit(solution)/shard_map/ppermute | solution.py:66
  296.4 4.2 broadcast_select_fusion.3
  300.5 15.8 %collective-permute-done.8 = bf16[2,128,3072]{2,1,0:T(8,128)(2,1)S(1)} collective-permute-done((bf16[2,128,3072]{2,1,0:T(8,128)(2,1)}, bf16[2,128,3072]{2,1,0:T(8,128)(2,1)S(1)}, u32[]{:S(2)}, u32[]{:S(2)}) %collective-permute-start.8) | collective-permute-done | bytes 1572896 | tf_op jit(solution)/shard_map/ppermute | solution.py:69
  316.9 6.1 collective-permute-done.10
  323.2 31.8 %collective-permute-done.11 = bf16[2,128,3072]{2,1,0:T(8,128)(2,1)S(1)} collective-permute-done((bf16[2,128,3072]{2,1,0:T(8,128)(2,1)S(1)}, bf16[2,128,3072]{2,1,0:T(8,128)(2,1)S(1)}, u32[]{:S(2)}, u32[]{:S(2)}) %collective-permute-start.11) | collective-permute-done | bytes 1572896 | tf_op jit(solution)/shard_map/ppermute | solution.py:69
  357.8 13.1 %fusion.3 = f32[1024,2048]{0,1:T(8,128)} fusion(bf16[2048,3072]{1,0:T(8,128)(2,1)S(1)} %bitcast.183, bf16[1024,1024]{1,0:T(8,128)(2,1)} %get-tuple-element.103, bf16[1024,1024]{1,0:T(8,128)(2,1)} %get-tuple-element.102), kind=kOutput, calls=%fused_computation.4 | convolution fusion | flops 8598323200 | bytes 20971520 | tf_op jit(solution)/shard_map/dot_general | solution.py:23
  370.9 10.7 %multiply_convert_fusion.2 = (bf16[1024,1024]{0,1:T(8,128)(2,1)}, bf16[1024,1024]{0,1:T(8,128)(2,1)}, bf16[1024,1024]{0,1:T(8,128)(2,1)}) fusion(f32[1024,2048]{0,1:T(8,128)} %fusion.3, bf16[2048,3072]{1,0:T(8,128)(2,1)S(1)} %bitcast.184, bf16[1024,1024]{1,0:T(8,128)(2,1)} %get-tuple-element.105, bf16[1024,1024]{1,0:T(8,128)(2,1)S(1)} %copy-done.13), kind=kOutput, calls=%fused_computation.17 | convolution fusion | flops 4319084544 | bytes 23068672 | tf_op jit(solution)/shard_map/dot_general | solution.py:23
  381.7 4.8 pad_maximum_fusion.2
  386.5 11.5 %fusion.1 = f32[1024,2048]{1,0:T(8,128)} fusion(bf16[2048,3072]{1,0:T(8,128)(2,1)S(1)} %bitcast.185, bf16[1024,1024]{0,1:T(8,128)(2,1)S(1)} %copy-done.16, bf16[1024,1024]{0,1:T(8,128)(2,1)S(1)} %copy-done.15), kind=kOutput, calls=%fused_computation.2 | convolution fusion | flops 8598323200 | bytes 20971520 | tf_op jit(solution)/shard_map/dot_general | solution.py:27
  397.9 8.6 %fusion.6 = f32[1024,2048]{1,0:T(8,128)} fusion(bf16[1024,1024]{0,1:T(8,128)(2,1)} %get-tuple-element.24, bf16[2048,3072]{1,0:T(8,128)(2,1)S(1)} %bitcast.186), kind=kOutput, calls=%fused_computation.24 | convolution fusion | flops 4294967296 | bytes 14680064 | tf_op jit(solution)/shard_map/dot_general | solution.py:27
  406.6 4.9 convolution_convert_fusion.4
  411.5 4.0 dynamic-slice_convert_fusion
  415.5 11.9 %convolution_convert_fusion = bf16[2048,2048]{1,0:T(8,128)(2,1)S(1)} fusion(bf16[1024,2048]{0,1:T(8,128)(2,1)S(1)} %copy-done.5, bf16[1024,1024]{1,0:T(8,128)(2,1)} %get-tuple-element.103, bf16[1024,1024]{1,0:T(8,128)(2,1)} %get-tuple-element.102), kind=kOutput, calls=%fused_computation.1 | convolution fusion | flops 8602517504 | bytes 16777216 | tf_op jit(solution)/shard_map/dot_general | solution.py:31
  434.7 9.0 %collective-permute-done.34 = bf16[2,128,1024]{2,1,0:T(8,128)(2,1)S(1)} collective-permute-done((bf16[2,128,1024]{2,1,0:T(8,128)(2,1)S(1)}, bf16[2,128,1024]{2,1,0:T(8,128)(2,1)S(1)}, u32[]{:S(2)}, u32[]{:S(2)}) %collective-permute-start.34) | collective-permute-done | bytes 524320 | tf_op jit(solution)/shard_map/ppermute | solution.py:69
  446.2 8.7 %collective-permute-done.33 = bf16[2,128,1024]{2,1,0:T(8,128)(2,1)S(1)} collective-permute-done((bf16[2,128,1024]{2,1,0:T(8,128)(2,1)S(1)}, bf16[2,128,1024]{2,1,0:T(8,128)(2,1)S(1)}, u32[]{:S(2)}, u32[]{:S(2)}) %collective-permute-start.33) | collective-permute-done | bytes 524320 | tf_op jit(solution)/shard_map/ppermute | solution.py:69
  457.4 10.6 %collective-permute-done.35 = bf16[2,128,1024]{2,1,0:T(8,128)(2,1)S(1)} collective-permute-done((bf16[2,128,1024]{2,1,0:T(8,128)(2,1)S(1)}, bf16[2,128,1024]{2,1,0:T(8,128)(2,1)S(1)}, u32[]{:S(2)}, u32[]{:S(2)}) %collective-permute-start.35) | collective-permute-done | bytes 524320 | tf_op jit(solution)/shard_map/ppermute | solution.py:69
  470.5 18.1 %collective-permute-done.38 = bf16[2,128,1024]{2,1,0:T(8,128)(2,1)S(1)} collective-permute-done((bf16[2,128,1024]{2,1,0:T(8,128)(2,1)S(1)}, bf16[2,128,1024]{2,1,0:T(8,128)(2,1)S(1)}, u32[]{:S(2)}, u32[]{:S(2)}) %collective-permute-start.38) | collective-permute-done | bytes 524320 | tf_op jit(solution)/shard_map/ppermute | solution.py:69
  500.0 13.0 %collective-permute-done.31 = bf16[2,128,2048]{2,1,0:T(8,128)(2,1)S(1)} collective-permute-done((bf16[2,128,2048]{2,1,0:T(8,128)(2,1)S(1)}, bf16[2,128,2048]{2,1,0:T(8,128)(2,1)S(1)}, u32[]{:S(2)}, u32[]{:S(2)}) %collective-permute-start.31) | collective-permute-done | bytes 1048608 | tf_op jit(solution)/shard_map/ppermute | solution.py:69
  520.1 24.9 %collective-permute-done.23 = bf16[256,1024]{1,0:T(8,128)(2,1)} collective-permute-done((bf16[256,1024]{1,0:T(8,128)(2,1)}, bf16[256,1024]{1,0:T(8,128)(2,1)}, u32[]{:S(2)}, u32[]{:S(2)}) %collective-permute-start.23) | collective-permute-done | bytes 524320 | tf_op jit(solution)/shard_map/ppermute | solution.py:66
  552.9 11.8 %collective-permute-done.18 = bf16[256,1024]{1,0:T(8,128)(2,1)S(1)} collective-permute-done((bf16[256,1024]{1,0:T(8,128)(2,1)S(1)}, bf16[256,1024]{1,0:T(8,128)(2,1)S(1)}, u32[]{:S(2)}, u32[]{:S(2)}) %collective-permute-start.18) | collective-permute-done | bytes 524320 | tf_op jit(solution)/shard_map/ppermute | solution.py:66
  564.6 30.3 %collective-permute-done.19 = bf16[256,1024]{1,0:T(8,128)(2,1)S(1)} collective-permute-done((bf16[256,1024]{1,0:T(8,128)(2,1)S(1)}, bf16[256,1024]{1,0:T(8,128)(2,1)S(1)}, u32[]{:S(2)}, u32[]{:S(2)}) %collective-permute-start.19) | collective-permute-done | bytes 524320 | tf_op jit(solution)/shard_map/ppermute | solution.py:66
  600.3 4.4 fusion.37
  622.2 4.5 convolution_convert_fusion.1.gkv
  630.2 178.0 %shard_map.204 = (f32[128,3072]{1,0:T(8,128)}, bf16[3,128,4096]{2,1,0:T(8,128)(2,1)}, bf16[256,1024]{1,0:T(8,128)(2,1)}, f32[8,1024]{1,0:T(8,128)}) custom-call(bf16[2048,1024]{1,0:T(8,128)(2,1)} %convolution_convert_fusion.3.gq, bf16[2048,1024]{1,0:T(8,128)(2,1)} %convolution_convert_fusion.1.gkv, bf16[2048,1024]{1,0:T(8,128)(2,1)} %convolution_convert_fusion.2.go, ...), custom_call_target="tpu_custom_call" | custom-call | tf_op jit(solution)/shard_map/pallas_call | solution.py:580
  (266 shorter events, 139.6 us)
Async XLA Ops:
  1.4 179.7 %collective-permute-start = (bf16[1,1024]{1,0:T(2,128)(2,1)S(1)}, bf16[1,1024]{1,0:T(2,128)(2,1)S(1)}, u32[]{:S(2)}, u32[]{:S(2)}) collective-permute-start(bf16[1,1024]{1,0:T(2,128)(2,1)S(1)} %broadcast_in_dim.100), channel_id=1, source_target_pairs={{0,1},{1,0},{2,3},{3,2},{4,5},{5,4},{6,7},{7,6},{8,9},{9,8},{10,11... | collective-permute-start | bytes 6152 | tf_op jit(solution)/shard_map/ppermute | solution.py:72
  1.4 224.9 %collective-permute-start.2 = (bf16[256,1024]{1,0:T(8,128)(2,1)}, bf16[256,1024]{1,0:T(8,128)(2,1)}, u32[]{:S(2)}, u32[]{:S(2)}) collective-permute-start(bf16[256,1024]{1,0:T(8,128)(2,1)} %param.14), channel_id=1, source_target_pairs={{0,8},{2,10},{4,12},{6,14},{8,16},{10,18},{12,20},{14,22},{16,24},... | collective-permute-start | bytes 1572872 | tf_op jit(solution)/shard_map/ppermute | solution.py:66
  210.5 19.6 %collective-permute-start.1 = (f32[256,1024]{1,0:T(8,128)}, f32[256,1024]{1,0:T(8,128)}, u32[]{:S(2)}, u32[]{:S(2)}) collective-permute-start(f32[256,1024]{1,0:T(8,128)} %constant_dynamic-slice_fusion.1), channel_id=1, source_target_pairs={{0,1},{1,0},{2,3},{3,2},{4,5},{5,4},{6,7},{7,6},{8,9},{9,8},{10,11... | collective-permute-start | bytes 3145736 | tf_op jit(solution)/shard_map/ppermute | solution.py:72
  211.8 37.1 %collective-permute-start.6 = (bf16[2,128,3072]{2,1,0:T(8,128)(2,1)}, bf16[2,128,3072]{2,1,0:T(8,128)(2,1)}, u32[]{:S(2)}, u32[]{:S(2)}) collective-permute-start(bf16[2,128,3072]{2,1,0:T(8,128)(2,1)} %bitcast.10), channel_id=1, source_target_pairs={{0,2},{2,0},{4,6},{6,4},{8,10},{10,8},{12,14},{14,12},{16,18},{18,... | collective-permute-start | bytes 4718600 | tf_op jit(solution)/shard_map/ppermute | solution.py:69
  211.8 40.1 %collective-permute-start.7 = (bf16[2,128,3072]{2,1,0:T(8,128)(2,1)}, bf16[2,128,3072]{2,1,0:T(8,128)(2,1)}, u32[]{:S(2)}, u32[]{:S(2)}) collective-permute-start(bf16[2,128,3072]{2,1,0:T(8,128)(2,1)} %bitcast.10), channel_id=1, source_target_pairs={{0,4},{2,6},{4,0},{6,2},{8,12},{10,14},{12,8},{14,10},{16,20},{18,... | collective-permute-start | bytes 4718600 | tf_op jit(solution)/shard_map/ppermute | solution.py:69
  213.9 15.1 %collective-permute-start.3 = (bf16[256,1024]{1,0:T(8,128)(2,1)S(1)}, bf16[256,1024]{1,0:T(8,128)(2,1)S(1)}, u32[]{:S(2)}, u32[]{:S(2)}) collective-permute-start(bf16[256,1024]{1,0:T(8,128)(2,1)S(1)} %copy-done.17), channel_id=1, source_target_pairs={{0,16},{2,18},{4,20},{6,22},{8,24},{10,26},{12,28},{14,30},{16,0},... | collective-permute-start | bytes 1572872 | tf_op jit(solution)/shard_map/ppermute | solution.py:66
  228.9 54.1 %collective-permute-start.9 = (bf16[2,128,3072]{2,1,0:T(8,128)(2,1)S(1)}, bf16[2,128,3072]{2,1,0:T(8,128)(2,1)S(1)}, u32[]{:S(2)}, u32[]{:S(2)}) collective-permute-start(bf16[2,128,3072]{2,1,0:T(8,128)(2,1)S(1)} %bitcast.195), channel_id=1, source_target_pairs={{0,4},{2,6},{4,0},{6,2},{8,12},{10,14},{12,8},{14,10},{16,20},{18,... | collective-permute-start | bytes 4718600 | tf_op jit(solution)/shard_map/ppermute | solution.py:69
  241.0 55.4 %collective-permute-start.5 = (bf16[1024,1024]{1,0:T(8,128)(2,1)}, bf16[1024,1024]{1,0:T(8,128)(2,1)S(1)}, u32[]{:S(2)}, u32[]{:S(2)}) collective-permute-start(bf16[1024,1024]{1,0:T(8,128)(2,1)} %constant_dynamic-update-slice_fusion), channel_id=1, source_target_pairs={{0,1},{1,0},{2,3},{3,2},{4,5},{5,4},{6,7},{7,6},{8,9},{9,8},{10,11... | collective-permute-start | bytes 6291464 | tf_op jit(solution)/shard_map/ppermute | solution.py:72
  241.2 44.5 %collective-permute-start.13 = (bf16[256,1024]{1,0:T(8,128)(2,1)S(1)}, bf16[256,1024]{1,0:T(8,128)(2,1)S(1)}, u32[]{:S(2)}, u32[]{:S(2)}) collective-permute-start(bf16[256,1024]{1,0:T(8,128)(2,1)S(1)} %multiply_convert_fusion.3), channel_id=1, source_target_pairs={{0,8},{2,10},{4,12},{6,14},{8,16},{10,18},{12,20},{14,22},{16,24},... | collective-permute-start | bytes 1572872 | tf_op jit(solution)/shard_map/ppermute | solution.py:66
  248.9 67.3 %collective-permute-start.8 = (bf16[2,128,3072]{2,1,0:T(8,128)(2,1)}, bf16[2,128,3072]{2,1,0:T(8,128)(2,1)S(1)}, u32[]{:S(2)}, u32[]{:S(2)}) collective-permute-start(bf16[2,128,3072]{2,1,0:T(8,128)(2,1)} %collective-permute-done.6), channel_id=1, source_target_pairs={{0,4},{2,6},{4,0},{6,2},{8,12},{10,14},{12,8},{14,10},{16,20},{18,... | collective-permute-start | bytes 4718600 | tf_op jit(solution)/shard_map/ppermute | solution.py:69
  251.9 35.8 %collective-permute-start.14 = (bf16[256,1024]{1,0:T(8,128)(2,1)S(1)}, bf16[256,1024]{1,0:T(8,128)(2,1)S(1)}, u32[]{:S(2)}, u32[]{:S(2)}) collective-permute-start(bf16[256,1024]{1,0:T(8,128)(2,1)S(1)} %multiply_convert_fusion.3), channel_id=1, source_target_pairs={{0,16},{2,18},{4,20},{6,22},{8,24},{10,26},{12,28},{14,30},{16,0},... | collective-permute-start | bytes 1572872 | tf_op jit(solution)/shard_map/ppermute | solution.py:66
  285.7 37.3 %collective-permute-start.10 = (bf16[2,128,3072]{2,1,0:T(8,128)(2,1)S(1)}, bf16[2,128,3072]{2,1,0:T(8,128)(2,1)S(1)}, u32[]{:S(2)}, u32[]{:S(2)}) collective-permute-start(bf16[2,128,3072]{2,1,0:T(8,128)(2,1)S(1)} %bitcast.196), channel_id=1, source_target_pairs={{0,2},{2,0},{4,6},{6,4},{8,10},{10,8},{12,14},{14,12},{16,18},{18,... | collective-permute-start | bytes 4718600 | tf_op jit(solution)/shard_map/ppermute | solution.py:69
  287.7 67.3 %collective-permute-start.11 = (bf16[2,128,3072]{2,1,0:T(8,128)(2,1)S(1)}, bf16[2,128,3072]{2,1,0:T(8,128)(2,1)S(1)}, u32[]{:S(2)}, u32[]{:S(2)}) collective-permute-start(bf16[2,128,3072]{2,1,0:T(8,128)(2,1)S(1)} %collective-permute-done.9), channel_id=1, source_target_pairs={{0,2},{2,0},{4,6},{6,4},{8,10},{10,8},{12,14},{14,12},{16,18},{18,... | collective-permute-start | bytes 4718600 | tf_op jit(solution)/shard_map/ppermute | solution.py:69
  296.3 58.9 %collective-permute-start.16 = (bf16[1024,1024]{1,0:T(8,128)(2,1)S(1)}, bf16[1024,1024]{1,0:T(8,128)(2,1)S(1)}, u32[]{:S(2)}, u32[]{:S(2)}) collective-permute-start(bf16[1024,1024]{1,0:T(8,128)(2,1)S(1)} %pad_maximum_fusion.7), channel_id=1, source_target_pairs={{0,1},{1,0},{2,3},{3,2},{4,5},{5,4},{6,7},{7,6},{8,9},{9,8},{10,11... | collective-permute-start | bytes 6291464 | tf_op jit(solution)/shard_map/ppermute | solution.py:72
  415.5 77.1 %collective-permute-start.21 = (bf16[1024,1024]{1,0:T(8,128)(2,1)}, bf16[1024,1024]{1,0:T(8,128)(2,1)S(1)}, u32[]{:S(2)}, u32[]{:S(2)}) collective-permute-start(bf16[1024,1024]{1,0:T(8,128)(2,1)} %dynamic-slice_convert_fusion), channel_id=1, source_target_pairs={{0,1},{1,0},{2,3},{3,2},{4,5},{5,4},{6,7},{7,6},{8,9},{9,8},{10,11... | collective-permute-start | bytes 6291464 | tf_op jit(solution)/shard_map/ppermute | solution.py:72
  432.2 22.6 %collective-permute-start.33 = (bf16[2,128,1024]{2,1,0:T(8,128)(2,1)S(1)}, bf16[2,128,1024]{2,1,0:T(8,128)(2,1)S(1)}, u32[]{:S(2)}, u32[]{:S(2)}) collective-permute-start(bf16[2,128,1024]{2,1,0:T(8,128)(2,1)S(1)} %get-tuple-element.108), channel_id=1, source_target_pairs={{0,2},{2,0},{4,6},{6,4},{8,10},{10,8},{12,14},{14,12},{16,18},{18,... | collective-permute-start | bytes 1572872 | tf_op jit(solution)/shard_map/ppermute | solution.py:69
  434.0 57.1 %collective-permute-start.28 = (bf16[2,128,2048]{2,1,0:T(8,128)(2,1)S(1)}, bf16[2,128,2048]{2,1,0:T(8,128)(2,1)S(1)}, u32[]{:S(2)}, u32[]{:S(2)}) collective-permute-start(bf16[2,128,2048]{2,1,0:T(8,128)(2,1)S(1)} %get-tuple-element.97), channel_id=1, source_target_pairs={{0,2},{2,0},{4,6},{6,4},{8,10},{10,8},{12,14},{14,12},{16,18},{18,... | collective-permute-start | bytes 3145736 | tf_op jit(solution)/shard_map/ppermute | solution.py:69
  443.7 25.5 %collective-permute-start.36 = (bf16[2,128,1024]{2,1,0:T(8,128)(2,1)S(1)}, bf16[2,128,1024]{2,1,0:T(8,128)(2,1)S(1)}, u32[]{:S(2)}, u32[]{:S(2)}) collective-permute-start(bf16[2,128,1024]{2,1,0:T(8,128)(2,1)S(1)} %get-tuple-element.110), channel_id=1, source_target_pairs={{0,4},{2,6},{4,0},{6,2},{8,12},{10,14},{12,8},{14,10},{16,20},{18,... | collective-permute-start | bytes 1572872 | tf_op jit(solution)/shard_map/ppermute | solution.py:69
  445.3 22.8 %collective-permute-start.35 = (bf16[2,128,1024]{2,1,0:T(8,128)(2,1)S(1)}, bf16[2,128,1024]{2,1,0:T(8,128)(2,1)S(1)}, u32[]{:S(2)}, u32[]{:S(2)}) collective-permute-start(bf16[2,128,1024]{2,1,0:T(8,128)(2,1)S(1)} %fusion.54), channel_id=1, source_target_pairs={{0,4},{2,6},{4,0},{6,2},{8,12},{10,14},{12,8},{14,10},{16,20},{18,... | collective-permute-start | bytes 1572872 | tf_op jit(solution)/shard_map/ppermute | solution.py:69
  454.9 33.7 %collective-permute-start.38 = (bf16[2,128,1024]{2,1,0:T(8,128)(2,1)S(1)}, bf16[2,128,1024]{2,1,0:T(8,128)(2,1)S(1)}, u32[]{:S(2)}, u32[]{:S(2)}) collective-permute-start(bf16[2,128,1024]{2,1,0:T(8,128)(2,1)S(1)} %fusion.51), channel_id=1, source_target_pairs={{0,2},{2,0},{4,6},{6,4},{8,10},{10,8},{12,14},{14,12},{16,18},{18,... | collective-permute-start | bytes 1572872 | tf_op jit(solution)/shard_map/ppermute | solution.py:69
  468.1 47.1 %collective-permute-start.17 = (bf16[1024,1024]{1,0:T(8,128)(2,1)S(1)}, bf16[1024,1024]{1,0:T(8,128)(2,1)}, u32[]{:S(2)}, u32[]{:S(2)}) collective-permute-start(bf16[1024,1024]{1,0:T(8,128)(2,1)S(1)} %dynamic-slice_convert_fusion.1), channel_id=1, source_target_pairs={{0,1},{1,0},{2,3},{3,2},{4,5},{5,4},{6,7},{7,6},{8,9},{9,8},{10,11... | collective-permute-start | bytes 6291464 | tf_op jit(solution)/shard_map/ppermute | solution.py:72
  469.1 79.8 %collective-permute-start.27 = (bf16[2,128,2048]{2,1,0:T(8,128)(2,1)}, bf16[2,128,2048]{2,1,0:T(8,128)(2,1)}, u32[]{:S(2)}, u32[]{:S(2)}) collective-permute-start(bf16[2,128,2048]{2,1,0:T(8,128)(2,1)} %get-tuple-element.96), channel_id=1, source_target_pairs={{0,2},{2,0},{4,6},{6,4},{8,10},{10,8},{12,14},{14,12},{16,18},{18,... | collective-permute-start | bytes 3145736 | tf_op jit(solution)/shard_map/ppermute | solution.py:69
  488.6 24.4 %collective-permute-start.31 = (bf16[2,128,2048]{2,1,0:T(8,128)(2,1)S(1)}, bf16[2,128,2048]{2,1,0:T(8,128)(2,1)S(1)}, u32[]{:S(2)}, u32[]{:S(2)}) collective-permute-start(bf16[2,128,2048]{2,1,0:T(8,128)(2,1)S(1)} %get-tuple-element.99), channel_id=1, source_target_pairs={{0,4},{2,6},{4,0},{6,2},{8,12},{10,14},{12,8},{14,10},{16,20},{18,... | collective-permute-start | bytes 3145736 | tf_op jit(solution)/shard_map/ppermute | solution.py:69
  496.8 22.5 %collective-permute-start.22 = (bf16[256,1024]{1,0:T(8,128)(2,1)}, bf16[256,1024]{1,0:T(8,128)(2,1)}, u32[]{:S(2)}, u32[]{:S(2)}) collective-permute-start(bf16[256,1024]{1,0:T(8,128)(2,1)} %get-tuple-element.112), channel_id=1, source_target_pairs={{0,24},{2,26},{4,28},{6,30},{8,0},{10,2},{12,4},{14,6},{16,8},{18,... | collective-permute-start | bytes 1572872 | tf_op jit(solution)/shard_map/ppermute | solution.py:66
  497.6 47.4 %collective-permute-start.23 = (bf16[256,1024]{1,0:T(8,128)(2,1)}, bf16[256,1024]{1,0:T(8,128)(2,1)}, u32[]{:S(2)}, u32[]{:S(2)}) collective-permute-start(bf16[256,1024]{1,0:T(8,128)(2,1)} %get-tuple-element.114), channel_id=1, source_target_pairs={{0,16},{2,18},{4,20},{6,22},{8,24},{10,26},{12,28},{14,30},{16,0},... | collective-permute-start | bytes 1572872 | tf_op jit(solution)/shard_map/ppermute | solution.py:66
  513.0 32.5 %collective-permute-start.24 = (bf16[256,1024]{1,0:T(8,128)(2,1)}, bf16[256,1024]{1,0:T(8,128)(2,1)S(1)}, u32[]{:S(2)}, u32[]{:S(2)}) collective-permute-start(bf16[256,1024]{1,0:T(8,128)(2,1)} %get-tuple-element.113), channel_id=1, source_target_pairs={{0,8},{2,10},{4,12},{6,14},{8,16},{10,18},{12,20},{14,22},{16,24},... | collective-permute-start | bytes 1572872 | tf_op jit(solution)/shard_map/ppermute | solution.py:66
  515.2 33.9 %collective-permute-start.29 = (bf16[2,128,2048]{2,1,0:T(8,128)(2,1)}, bf16[2,128,2048]{2,1,0:T(8,128)(2,1)S(1)}, u32[]{:S(2)}, u32[]{:S(2)}) collective-permute-start(bf16[2,128,2048]{2,1,0:T(8,128)(2,1)} %fusion.30), channel_id=1, source_target_pairs={{0,4},{2,6},{4,0},{6,2},{8,12},{10,14},{12,8},{14,10},{16,20},{18,... | collective-permute-start | bytes 3145736 | tf_op jit(solution)/shard_map/ppermute | solution.py:69
  519.4 77.5 %collective-permute-start.30 = (bf16[2,128,2048]{2,1,0:T(8,128)(2,1)}, bf16[2,128,2048]{2,1,0:T(8,128)(2,1)S(1)}, u32[]{:S(2)}, u32[]{:S(2)}) collective-permute-start(bf16[2,128,2048]{2,1,0:T(8,128)(2,1)} %get-tuple-element.98), channel_id=1, source_target_pairs={{0,4},{2,6},{4,0},{6,2},{8,12},{10,14},{12,8},{14,10},{16,20},{18,... | collective-permute-start | bytes 3145736 | tf_op jit(solution)/shard_map/ppermute | solution.py:69
  544.9 51.9 %collective-permute-start.32 = (bf16[2,128,2048]{2,1,0:T(8,128)(2,1)S(1)}, bf16[2,128,2048]{2,1,0:T(8,128)(2,1)S(1)}, u32[]{:S(2)}, u32[]{:S(2)}) collective-permute-start(bf16[2,128,2048]{2,1,0:T(8,128)(2,1)S(1)} %fusion.27), channel_id=1, source_target_pairs={{0,2},{2,0},{4,6},{6,4},{8,10},{10,8},{12,14},{14,12},{16,18},{18,... | collective-permute-start | bytes 3145736 | tf_op jit(solution)/shard_map/ppermute | solution.py:69
  549.0 15.7 %collective-permute-start.18 = (bf16[256,1024]{1,0:T(8,128)(2,1)S(1)}, bf16[256,1024]{1,0:T(8,128)(2,1)S(1)}, u32[]{:S(2)}, u32[]{:S(2)}) collective-permute-start(bf16[256,1024]{1,0:T(8,128)(2,1)S(1)} %get-tuple-element.115), channel_id=1, source_target_pairs={{0,24},{2,26},{4,28},{6,30},{8,0},{10,2},{12,4},{14,6},{16,8},{18,... | collective-permute-start | bytes 1572872 | tf_op jit(solution)/shard_map/ppermute | solution.py:66
  549.0 45.9 %collective-permute-start.19 = (bf16[256,1024]{1,0:T(8,128)(2,1)S(1)}, bf16[256,1024]{1,0:T(8,128)(2,1)S(1)}, u32[]{:S(2)}, u32[]{:S(2)}) collective-permute-start(bf16[256,1024]{1,0:T(8,128)(2,1)S(1)} %get-tuple-element.117), channel_id=1, source_target_pairs={{0,16},{2,18},{4,20},{6,22},{8,24},{10,26},{12,28},{14,30},{16,0},... | collective-permute-start | bytes 1572872 | tf_op jit(solution)/shard_map/ppermute | solution.py:66
  550.0 45.0 %collective-permute-start.20 = (bf16[256,1024]{1,0:T(8,128)(2,1)S(1)}, bf16[256,1024]{1,0:T(8,128)(2,1)S(1)}, u32[]{:S(2)}, u32[]{:S(2)}) collective-permute-start(bf16[256,1024]{1,0:T(8,128)(2,1)S(1)} %get-tuple-element.116), channel_id=1, source_target_pairs={{0,8},{2,10},{4,12},{6,14},{8,16},{10,18},{12,20},{14,22},{16,24},... | collective-permute-start | bytes 1572872 | tf_op jit(solution)/shard_map/ppermute | solution.py:66
  (52 other events, 477.5 us)

commit v3 on v2

--- a/solution.py
+++ b/solution.py
@@ -110,8 +110,10 @@
     return place
 
 
-def gather_kernel(plane, wq, wk, wv, wo, wg, wu, wd, tok, attn, ffn, ext,
-                  own_sem, zs, zr, ps, pr, fs, fr, ts, tr):
+def forward_kernel(plane, wq, wk, wv, wo, wg, wu, wd, tok, cot, gain, gain_two, cos, sin, bias,
+                   attn_out, ffn, normed_line, cot_line, normed, rms, q_rot, k_rot, values, attended, mixed, rms_two,
+                   attn, ext, gains, out_send, out_recv, square, square_in, normed_two,
+                   own_sem, zs, zr, ps, pr, fs, fr, qs, qr, ts, tr, ns, nr, cs, cr, es, er):
     rows, tok_rows, width = wq.shape[0], tok.shape[0], tok.shape[1]
     count = plane * LINE
     halo = ext.shape[0] - tok_rows
@@ -134,25 +136,34 @@
             device_id=(peer, core), device_id_type=MESH,
         )
 
+    def across(src, dst, j):
+        return remote(src, dst, es.at[j], er.at[j], device, 1 - half)
+
     mine = pl.ds(pl.multiple_of(device * rows, rows), rows)
     own, at = [], 0
+
+    def keep(src, dst):
+        own.append(pltpu.make_async_copy(src, dst, own_sem.at[len(own)]))
+
     for block in (wq, wk, wv, wo):
         wide = block.shape[1]
-        own.append(pltpu.make_async_copy(block, attn.at[mine, pl.ds(at, wide)], own_sem.at[len(own)]))
+        keep(block, attn.at[mine, pl.ds(at, wide)])
         at += wide
-    from_line = pl.ds(pl.multiple_of(line * rows, rows), rows)
 
     def hidden(block, member):
         return block.at[:, pl.ds(pl.multiple_of(member * chunk, chunk), chunk)]
 
     for j, block in enumerate((wg, wu, wd)):
-        own.append(
-            pltpu.make_async_copy(
-                hidden(block, line), ffn.at[from_line, pl.ds(j * chunk, chunk)], own_sem.at[len(own)]
-            )
-        )
+        keep(hidden(block, line), ffn.at[mine, pl.ds(j * chunk, chunk)])
     features = pl.ds(pl.multiple_of(half * width, width), width)
-    own.append(pltpu.make_async_copy(tok, ext.at[pl.ds(halo, tok_rows), features], own_sem.at[len(own)]))
+    others = pl.ds(pl.multiple_of((1 - half) * width, width), width)
+    keep(tok, ext.at[pl.ds(halo, tok_rows), features])
+
+    def line_rows(member):
+        return pl.ds(pl.multiple_of(member * tok_rows, tok_rows), tok_rows)
+
+    keep(cot, cot_line.at[line_rows(line), features])
+    keep(gain, gains.at[:, features])
     for copy in own:
         copy.start()
     first = pltpu.make_async_copy(
@@ -160,13 +171,13 @@
     )
     pl.semaphore_wait(barrier, len(greet) + 1)
 
-    tok_cross = remote(tok, ext.at[pl.ds(halo, tok_rows), features], ts.at[0], tr.at[0], device, 1 - half)
+    tok_cross = across(tok, ext.at[pl.ds(halo, tok_rows), features], 0)
+    gain_cross = across(gain, gains.at[:, features], 1)
     tok_next = remote(
-        tok.at[pl.ds(tok_rows - halo, halo)], ext.at[pl.ds(0, halo), features], ts.at[1], tr.at[1], device + 1
+        tok.at[pl.ds(tok_rows - halo, halo)], ext.at[pl.ds(0, halo), features], ts.at[0], tr.at[0], device + 1
     )
-    tok_relay = remote(
-        ext.at[pl.ds(0, halo), features], ext.at[pl.ds(0, halo), features], ts.at[2], tr.at[2], device, 1 - half
-    )
+    tok_relay = across(ext.at[pl.ds(0, halo), features], ext.at[pl.ds(0, halo), features], 2)
+    cot_cross = across(cot, cot_line.at[line_rows(line), features], 3)
     for copy in own[:4]:
         copy.wait()
 
@@ -182,32 +193,50 @@
             keys += [key | bit for key in keys]
         return keys
 
-    def plane_copy(origin, turn, key, bit):
-        block = attn.at[
+    def plane_copy(whole, sent, got, origin, turn, key, bit):
+        block = whole.at[
             pl.ds(pl.multiple_of((origin * plane + flip(place, key)) * rows + turn * part, part), part)
         ]
-        sems = [s.at[origin, turn, key | bit] for s in (ps, pr)]
+        sems = [s.at[origin, turn, key | bit] for s in (sent, got)]
         return remote(block, block, *sems, line * plane + flip(place, bit))
 
-    def spread(origin, stage):
+    def spread(which, origin, stage):
         for turn in range(2):
             order = bits[turn:] + bits[:turn]
             if stage:
                 for key in keys_after(turn, stage - 1):
-                    plane_copy(origin, turn, key, order[stage - 1]).wait_recv()
+                    plane_copy(*which, origin, turn, key, order[stage - 1]).wait_recv()
             if stage < len(bits):
                 for key in keys_after(turn, stage):
-                    plane_copy(origin, turn, key, order[stage]).start()
+                    plane_copy(*which, origin, turn, key, order[stage]).start()
+
+    def spread_sent(which):
+        for origin in range(LINE):
+            for turn in range(2):
+                for stage, bit in enumerate(bits[turn:] + bits[:turn]):
+                    for key in keys_after(turn, stage):
+                        plane_copy(*which, origin, turn, key, bit).wait_send()
+
+    attn_plane, ffn_plane = (attn, ps, pr), (ffn, qs, qr)
+
+    def member(k):
+        return lax.rem(line + k, LINE)
 
     def ffn_copies(k):
-        member = lax.rem(line + k, LINE)
         return [
             remote(
-                hidden(block, member), ffn.at[from_line, pl.ds(j * chunk, chunk)],
-                fs.at[k - 1, j], fr.at[k - 1, j], member * plane + place,
+                hidden(block, member(k)), ffn.at[mine, pl.ds(j * chunk, chunk)],
+                fs.at[k - 1, j], fr.at[k - 1, j], member(k) * plane + place,
             )
             for j, block in enumerate((wg, wu, wd))
         ]
+
+    def line_send(src, whole, sent, got, k):
+        return remote(src, whole.at[line_rows(line), features], sent.at[k - 1], got.at[k - 1], member(k) * plane + place)
+
+    def line_relay(whole, j, k):
+        block = whole.at[line_rows(member(LINE - k)), features]
+        return across(block, block, j + k - 1)
 
     slots = [(line, None, None)]
     for d in range(1, LINE):
@@ -226,78 +255,205 @@
             pl.when(line < LINE - 1)(lambda: line_copy(origin, 1).start())
         if step in (None, -1):
             pl.when(line > 0)(lambda: line_copy(origin, -1).start())
-        spread(origin, 0)
+        spread(attn_plane, origin, 0)
+
+    step = 16
+
+    def block_rows(i, start=0):
+        return pl.ds(pl.multiple_of(start + i * step, step), step)
+
+    def norm_one(start):
+        def body(i, carry):
+            at = block_rows(i, start)
+            x = ext[at].astype(F32)
+            r = lax.rsqrt(jnp.mean(x * x, axis=1, keepdims=True) + EPSILON)
+            normed[at] = (x * r * gains[:1]).astype(BF16)
+            if start:
+                rms[block_rows(i)] = r
+            return carry
+
+        lax.fori_loop(0, (tok_rows if start else halo) // step, body, 0)
 
     pl.when(device < count - 1)(lambda: tok_next.start())
     for j in range(len(slots) + len(bits)):
         if j < len(slots):
-            origin, condition, step = slots[j]
-            guarded(condition, functools.partial(arrive, origin, step))
+            origin, condition, direction = slots[j]
+            guarded(condition, functools.partial(arrive, origin, direction))
         if j == 0:
             tok_cross.start()
-        if j in (2, 4, 6):
-            for copy in ffn_copies((1, 3, 2)[j // 2 - 1]):
-                copy.start()
+            gain_cross.start()
+        if j == len(slots) - 1:
+            for k in (1, 3, 2):
+                for copy in ffn_copies(k):
+                    copy.start()
+            cot_cross.start()
+            for k in range(1, LINE):
+                line_send(cot, cot_line, cs, cr, k).start()
         for stage in range(1, len(bits) + 1):
             if 0 <= j - stage < len(slots):
-                origin, condition, step = slots[j - stage]
-                guarded(condition, functools.partial(spread, origin, stage))
+                origin, condition, direction = slots[j - stage]
+                if j == len(slots) + len(bits) - 1 and stage == len(bits):
+                    for copy in own[4:7]:
+                        copy.wait()
+                    spread(ffn_plane, line, 0)
+                guarded(condition, functools.partial(spread, attn_plane, origin, stage))
         if j == 1:
             pl.when(device == 0)(lambda: first.start())
             pl.when(device == 0)(lambda: first.wait())
             pl.when(device > 0)(lambda: tok_next.wait_recv())
             tok_relay.start()
+        if j == 3:
+            tok_cross.wait()
+            gain_cross.wait()
+            tok_relay.wait()
+            for copy in own[7:]:
+                copy.wait()
+            norm_one(0)
+            norm_one(halo)
+
+    kept = pltpu.make_async_copy(attn, attn_out, own_sem.at[len(own) + 1])
+    kept.start()
+
+    arrivals = (0, 1, 3, 2)
+
+    def ffn_arrive(k):
+        for copy in ffn_copies(k):
+            copy.wait_recv()
+        spread(ffn_plane, member(LINE - k), 0)
+
+    q_width, k_width = wq.shape[1], wk.shape[1]
+    kv_local, repeats = k_width // HD, q_width // k_width
+
+    def turn_by(x, start, size):
+        turned = jnp.concatenate([-x[:, HD // 2 :], x[:, : HD // 2]], axis=1)
+        return (x * cos[pl.ds(start, size)] + turned * sin[pl.ds(start, size)]).astype(BF16)
+
+    whole_rows = normed.shape[0]
+    for j in range(kv_local):
+        at = pl.ds(j * HD, HD)
+        key_block = matmul(normed[...], attn[:, pl.ds(q_width + j * HD, HD)])
+        k_rot[:, at] = turn_by(key_block, 0, whole_rows)
+        values[:, at] = matmul(normed[...], attn[:, pl.ds(q_width + k_width + j * HD, HD)]).astype(BF16)
+        if j == 0:
+            ffn_arrive(1)
+            ffn_arrive(3)
+        for r in range(repeats):
+            head = pl.ds((j * repeats + r) * HD, HD)
+            query = matmul(normed[pl.ds(halo, tok_rows)], attn[:, head])
+            q_rot[:, head] = turn_by(query, halo, tok_rows)
+            scores = matmul_t(q_rot[:, head], k_rot[:, at]) * HD ** (-0.5) + bias[...]
+            expo = jnp.exp(scores - jnp.max(scores, axis=1, keepdims=True))
+            probs = expo / jnp.sum(expo, axis=1, keepdims=True)
+            attended[:, head] = matmul(probs.astype(BF16), values[:, at]).astype(BF16)
+        if j == 0:
+            ffn_arrive(2)
+            for stage in range(1, len(bits)):
+                spread(ffn_plane, line, stage)
+
+    out_at = pl.ds(q_width + 2 * k_width, q_width)
+    tiles = width // 256
+    for tile in range(tiles):
+        block = attn[pl.ds(pl.multiple_of((1 - half) * width + tile * 256, 256), 256), out_at]
+        out_send[:, pl.ds(tile * 256, 256)] = matmul_t(attended[...], block)
+    out_cross = across(out_send, out_recv, 4)
+    out_cross.start()
+    for tile in range(tiles):
+        block = attn[pl.ds(pl.multiple_of(half * width + tile * 256, 256), 256), out_at]
+        mixed[:, pl.ds(tile * 256, 256)] = matmul_t(attended[...], block)
+    for stage in range(1, len(bits)):
+        spread(ffn_plane, member(LINE - 1), stage)
+    out_cross.wait()
+
+    def mix(i, carry):
+        at = block_rows(i)
+        value = ext[block_rows(i, halo), features].astype(F32) + (mixed[at] + out_recv[at])
+        mixed[at] = value
+        square[at] = jnp.broadcast_to(jnp.sum(value * value, axis=1, keepdims=True), (step, square.shape[1]))
+        return carry
+
+    lax.fori_loop(0, tok_rows // step, mix, 0)
+    square_cross = across(square, square_in, 5)
+    square_cross.start()
+    square_cross.wait()
+
+    def norm_two(i, carry):
+        at = block_rows(i)
+        r = lax.rsqrt((square[at] + square_in[at])[:, :1] / (2 * width) + EPSILON)
+        rms_two[at] = r
+        normed_two[at] = (mixed[at] * r * gain_two[...]).astype(BF16)
+        return carry
+
+    lax.fori_loop(0, tok_rows // step, norm_two, 0)
+    normed_own = pltpu.make_async_copy(
+        normed_two, normed_line.at[line_rows(line), features], own_sem.at[len(own) + 2]
+    )
+    normed_own.start()
+    for k in range(1, LINE):
+        line_send(normed_two, normed_line, ns, nr, k).start()
+    normed_cross = across(normed_two, normed_line.at[line_rows(line), features], 6)
+    normed_cross.start()
+
+    for k in range(1, LINE):
+        line_send(cot, cot_line, cs, cr, k).wait_recv()
+        line_relay(cot_line, 7, k).start()
+    for k in arrivals[2:]:
+        for stage in range(1, len(bits)):
+            spread(ffn_plane, member(LINE - k), stage)
+    for k in range(1, LINE):
+        line_send(normed_two, normed_line, ns, nr, k).wait_recv()
+        line_relay(normed_line, 7 + LINE - 1, k).start()
+    for k in arrivals:
+        spread(ffn_plane, member(LINE - k), len(bits))
 
     for origin in range(LINE):
         pl.when((origin <= line) & (line < LINE - 1))(lambda o=origin: line_copy(o, 1).wait_send())
         pl.when((origin >= line) & (line > 0))(lambda o=origin: line_copy(o, -1).wait_send())
-        for turn in range(2):
-            order = bits[turn:] + bits[:turn]
-            for stage, bit in enumerate(order):
-                for key in keys_after(turn, stage):
-                    plane_copy(origin, turn, key, bit).wait_send()
+    spread_sent(attn_plane)
+    spread_sent(ffn_plane)
     for k in range(1, LINE):
         for copy in ffn_copies(k):
-            copy.wait()
+            copy.wait_send()
+        line_send(cot, cot_line, cs, cr, k).wait_send()
+        line_send(normed_two, normed_line, ns, nr, k).wait_send()
+        line_relay(cot_line, 7, k).wait()
+        line_relay(normed_line, 7 + LINE - 1, k).wait()
     pl.when(device < count - 1)(lambda: tok_next.wait_send())
-    tok_cross.wait()
-    tok_relay.wait()
-    for copy in own[4:]:
-        copy.wait()
-
-
-def gather_start(plane, tokens, wq, wk, wv, wo, wg, wu, wd):
-    rows = wq.shape[0]
+    cot_cross.wait()
+    normed_cross.wait()
+    normed_own.wait()
+    kept.wait()
+
+
+def forward(plane, wq, wk, wv, wo, wg, wu, wd, tokens, cotangent, gain, gain_two, cos, sin, bias):
+    rows, (count, half_width) = wq.shape[0], tokens.shape
     chunk = wd.shape[1] // LINE
     columns = sum(w.shape[1] for w in (wq, wk, wv, wo))
-    dma = pltpu.SemaphoreType.DMA
+    width, whole, ext = 2 * half_width, LINE * plane * rows, HALO + count
+    dma, vmem, shape = pltpu.SemaphoreType.DMA, pltpu.VMEM, jax.ShapeDtypeStruct
+    inside = pl.BlockSpec(memory_space=pltpu.VMEM)
+    pairs = [(LINE, 2, plane)] * 2 + [(LINE - 1, 3)] * 2 + [(LINE, 2, plane)] * 2
+    pairs += [(1,)] * 2 + [(LINE - 1,)] * 4 + [(7 + 2 * (LINE - 1),)] * 2
     return pl.pallas_call(
-        functools.partial(gather_kernel, plane),
+        functools.partial(forward_kernel, plane),
         out_shape=(
-            jax.ShapeDtypeStruct((LINE * plane * rows, columns), BF16),
-            jax.ShapeDtypeStruct((LINE * rows, 3 * chunk), BF16),
-            jax.ShapeDtypeStruct((HALO + tokens.shape[0], 2 * tokens.shape[1]), BF16),
+            shape((whole, columns), BF16), shape((whole, 3 * chunk), BF16),
+            shape((LINE * count, width), BF16), shape((LINE * count, width), BF16),
+            shape((ext, width), BF16), shape((count, 1), F32), shape((count, wq.shape[1]), BF16),
+            shape((ext, wk.shape[1]), BF16), shape((ext, wk.shape[1]), BF16), shape((count, wq.shape[1]), BF16),
+            shape((count, half_width), F32), shape((count, 1), F32),
         ),
-        in_specs=[ANY] * 8,
-        out_specs=[ANY] * 3,
+        in_specs=[ANY] * 9 + [inside] * 5,
+        out_specs=[ANY] * 4 + [inside] * 8,
         scratch_shapes=[
-            dma((9,)), dma((2, LINE)), dma((LINE,)), dma((LINE, 2, plane)), dma((LINE, 2, plane)),
-            dma((LINE - 1, 3)), dma((LINE - 1, 3)), dma((3,)), dma((3,)),
+            vmem((whole, columns), BF16), vmem((ext, width), BF16), vmem((8, width), F32),
+            vmem((count, half_width), F32), vmem((count, half_width), F32), vmem((count, 128), F32),
+            vmem((count, 128), F32), vmem((count, half_width), BF16),
+            dma((14,)), dma((2, LINE)), dma((LINE,)), *[dma(p) for p in pairs],
         ],
-        compiler_params=pltpu.CompilerParams(collective_id=1, has_side_effects=True),
-    )(wq, wk, wv, wo, wg, wu, wd, tokens)
-
-
-def spread_plane(links, own, rows):
-    columns = own.shape[1]
-    own = own.reshape(LINE, rows, columns)
-    whole = jnp.zeros((LINE, links.plane, rows, columns), BF16)
-    for turn in range(2):
-        for key, part in links.spread(own[2 * turn : 2 * turn + 2], turn).items():
-            whole = lax.dynamic_update_slice(
-                whole, part[:, None], (2 * turn, flip(links.place, key), 0, 0)
-            )
-    return whole.reshape(-1, columns)
+        compiler_params=pltpu.CompilerParams(
+            collective_id=1, has_side_effects=True, vmem_limit_bytes=60 * 2**20
+        ),
+    )(wq, wk, wv, wo, wg, wu, wd, tokens, cotangent, gain, gain_two, cos, sin, bias)
 
 
 def fold_plan(bits, turn):
@@ -640,75 +796,52 @@
     ff_half = w_gate.shape[1]
     chunk = ff_half // LINE
 
-    attn_all, ffn_own, tokens_ext = gather_start(
-        links.plane, tokens, w_query, w_key, w_value, w_output.T, w_gate, w_up, w_down.T
-    )
-    ffn_all = spread_plane(links, ffn_own, rows)
-    w_gate_up, w_down_t = ffn_all[:, : 2 * chunk], ffn_all[:, 2 * chunk :]
-
-    def line_gather(x):
-        return jnp.concatenate([x] + [links.step(x, k) for k in range(1, LINE)], axis=0)
-
-    def line_sum(x):
-        parts = x.reshape(LINE, count, half_width)
-        total = parts[0].astype(F32)
-        for k in range(1, LINE):
-            total += links.step(parts[k].astype(BF16), LINE - k).astype(F32)
-        return total
-
     n = links.count
-    tokens_ext = tokens_ext.astype(F32)
-    cot_line = links.both(line_gather(cotangent))
-
+    ext = HALO + count
+    q_width, k_width = w_query.shape[1], w_key.shape[1]
+    kv_local, repeats = k_width // HD, q_width // k_width
     seq_ids = jnp.arange(lengths.shape[0])
     in_start = jnp.sum(jnp.where(seq_ids[None, :] < seq_ids[:, None], lengths[None, :], 0), axis=1)
-    row_ids = links.index * count - HALO + jnp.arange(HALO + count)
+    row_ids = links.index * count - HALO + jnp.arange(ext)
     seq_of_row = jnp.sum((row_ids[:, None] >= in_start[None, :]).astype(jnp.int32), axis=1) - 1
     chosen = seq_of_row[:, None] == seq_ids[None, :]
     positions = row_ids - jnp.sum(jnp.where(chosen, in_start[None, :], 0), axis=1)
     cosine, sine = rotary_tables(positions)
-    cos_k, sin_k = cosine[:, None, :], sine[:, None, :]
-    cos_q, sin_q = cosine[HALO:, None, None, :], sine[HALO:, None, None, :]
-
-    gain_one = links.both(attn_gain[None, :]).astype(F32)
+    allowed = (seq_of_row[HALO:, None] == seq_of_row[None, :]) & (
+        row_ids[HALO:, None] >= row_ids[None, :]
+    )
+    bias = jnp.where(allowed, 0.0, -1e30).astype(F32)
+    gain_mine = attn_gain.astype(F32)[None, :]
     gain_two = ffn_gain.astype(F32)[None, :]
-    rms_one = lax.rsqrt(jnp.mean(tokens_ext * tokens_ext, axis=-1, keepdims=True) + EPSILON)
-    normed_attn = (tokens_ext * rms_one * gain_one).astype(BF16)
-
-    q_width, k_width = w_query.shape[1], w_key.shape[1]
-    kv_local = k_width // HD
-    repeats = q_width // k_width
-    ext = HALO + count
+    (
+        attn_all, ffn_all, normed_ffn, cot_line, normed_attn, rms_mine, queries_rot, keys_rot, values,
+        attended, mixed, rms_two,
+    ) = forward(
+        links.plane, w_query, w_key, w_value, w_output.T, w_gate, w_up, w_down.T, tokens, cotangent,
+        jnp.broadcast_to(gain_mine, (8, half_width)), gain_two, cosine, sine, bias,
+    )
+    w_gate_up, w_down_t = ffn_all[:, : 2 * chunk], ffn_all[:, 2 * chunk :]
     w_q = attn_all[:, :q_width]
     w_kv = attn_all[:, q_width : q_width + 2 * k_width]
     w_out_t = attn_all[:, q_width + 2 * k_width :]
-    queries = matmul(normed_attn[HALO:], w_q).reshape(count, kv_local, repeats, HD)
-    keys_values = matmul(normed_attn, w_kv)
-    keys = keys_values[:, :k_width].reshape(ext, kv_local, HD)
-    values = keys_values[:, k_width:].astype(BF16).reshape(ext, kv_local, HD)
-    queries_rot = rotate(queries, cos_q, sin_q).astype(BF16)
-    keys_rot = rotate(keys, cos_k, sin_k).astype(BF16)
-    allowed = (seq_of_row[HALO:, None] == seq_of_row[None, :]) & (
-        row_ids[HALO:, None] >= row_ids[None, :]
-    )
-    scores = jnp.einsum("qgrd,kgd->grqk", queries_rot, keys_rot, preferred_element_type=F32)
-    scores = jnp.where(allowed[None, None], scores * HD ** (-0.5), -1e30)
-    highest = jnp.max(scores, axis=-1, keepdims=True)
-    expo = jnp.exp(scores - highest)
-    probs = expo / jnp.sum(expo, axis=-1, keepdims=True)
-    probs_low = probs.astype(BF16)
-    attended = jnp.einsum("grqk,kgd->qgrd", probs_low, values, preferred_element_type=F32)
-    attended = attended.astype(BF16).reshape(count, q_width)
-    out_mine, out_theirs = links.halves(matmul_t(attended, w_out_t))
-    tokens_half = tokens.astype(F32)
-    mixed = tokens_half + (out_mine + links.swap(out_theirs))
+    cos_k, sin_k = cosine[:, None, :], sine[:, None, :]
+    cos_q, sin_q = cosine[HALO:, None, None, :], sine[HALO:, None, None, :]
+    queries_rot = queries_rot.reshape(count, kv_local, repeats, HD)
+    keys_rot = keys_rot.reshape(ext, kv_local, HD)
+    values = values.reshape(ext, kv_local, HD)
+
+    def line_sum(x):
+        def of(k):
+            return lax.dynamic_slice_in_dim(x, (links.line + k) % LINE * count, count, 0)
+
+        total = of(0).astype(F32)
+        for k in range(1, LINE):
+            total += links.step(of(k).astype(BF16), k).astype(F32)
+        return total
 
     def row_sum(x):
         total = jnp.sum(x, axis=-1)[None, :]
         return (total + links.swap(total)).reshape(count, 1)
-
-    rms_two = lax.rsqrt(row_sum(mixed * mixed) / width + EPSILON)
-    normed_ffn = links.both(line_gather((mixed * rms_two * gain_two).astype(BF16)))
 
     gate_up = matmul(normed_ffn, w_gate_up)
     gate, upward = gate_up[:, :chunk], gate_up[:, chunk:]
@@ -741,6 +874,11 @@
 
     attn_out_grad = links.both(mixed_grad.astype(BF16))
     out_local = t_matmul(attn_out_grad, attended)
+    scores = jnp.einsum("qgrd,kgd->grqk", queries_rot, keys_rot, preferred_element_type=F32)
+    scores = jnp.where(allowed[None, None], scores * HD ** (-0.5), -1e30)
+    expo = jnp.exp(scores - jnp.max(scores, axis=-1, keepdims=True))
+    probs = expo / jnp.sum(expo, axis=-1, keepdims=True)
+    probs_low = probs.astype(BF16)
     attended_grad = matmul(attn_out_grad, w_out_t).astype(BF16)
     attended_grad = attended_grad.reshape(count, kv_local, repeats, HD)
     values_grad = jnp.einsum("grqk,qgrd->kgd", probs_low, attended_grad, preferred_element_type=F32)
@@ -771,8 +909,8 @@
         grad_theirs.astype(BF16),
         mixed_grad,
         tokens,
-        rms_one[HALO:],
-        attn_gain.astype(F32)[None, :],
+        rms_mine,
+        gain_mine,
         ffn_gain_local[None, :],
     )
     ffn_grads = ffn_bf16.astype(F32)

time: 831 us -> 770 us (0.927)
  waiting for transfers between devices: 233 us -> 95.1 us
  Pallas kernels: 346 us -> 455 us
  other arithmetic: 47.5 us -> 35.4 us
    ppermute x18 -> x12, waiting for transfers between devices: 148 us -> 21.9 us  [cross(): return lax.ppermute(x, 'dp', [(d, d ^ bit) for d in range(self.count)])]
    pallas_call x1, Pallas kernels: 168 us -> 277 us  [forward(): pl.pallas_call(functools.partial(forward_kernel, plane), out_shape=(shape...]
    ppermute x12 -> x6, waiting for transfers between devices: 84.6 us -> 73.2 us  [step(): return lax.ppermute(x, 'dp', [(d, (d + shift) % n) for d in range(n)])]
    dynamic_update_slice x8 -> x0, local copies, waits for them, and re-layouts: 9.09 us -> none  [spread_plane(): lax.dynamic_update_slice(whole, part[:, None], (2 * turn, flip(links.plac...]
    dot_general x5 -> x3, matrix products: 37.6 us -> 30.6 us  [matmul(): return jnp.dot(left, right, preferred_element_type=F32)]
    ppermute x18 -> x12, starting transfers between devices: 18 us -> 14.4 us  [cross(): return lax.ppermute(x, 'dp', [(d, d ^ bit) for d in range(self.count)])]
    dot_general x5 -> x4, matrix products: 27.3 us -> 24 us  [matmul_t(): lax.dot_general(left, right, (((1,), (1,)), ((), ())), preferred_element_...]
  transfers between devices with their start and end apart: 39 -> 22, of which waited for: 17 -> 7; matrix products, arithmetic and copies ran while one was open for 13% -> 11% of each run, Pallas kernels for 20% -> 0%
where the time goes in v3:
time: 770 us; the launch traced here: 763 us
  Pallas kernels  455 us (59%)
  waiting for transfers between devices  95.1 us (12%)
  matrix products  90.9 us (12%)
  local copies, waits for them, and re-layouts  57.3 us (7%)
  other arithmetic  35.4 us (5%)
  starting transfers between devices  27.8 us (4%)
    pallas_call x1, Pallas kernels, forward(): pl.pallas_call(functools.partial(forward_kernel, plane), out_shape=(shape...  277 us
    pallas_call x1, Pallas kernels, finish(): pl.pallas_call(functools.partial(finish_kernel, plane), out_shape=(jax.Sh...  179 us
    ppermute x6, waiting for transfers between devices, step(): return lax.ppermute(x, 'dp', [(d, (d + shift) % n) for d in range(n)])  73.2 us
    dot_general x3, matrix products, matmul(): return jnp.dot(left, right, preferred_element_type=F32)  30.6 us
    dot_general x5, matrix products, t_matmul(): lax.dot_general(left, right, (((0,), (0,)), ((), ())), preferred_element_...  30.3 us
    dot_general x4, matrix products, matmul_t(): lax.dot_general(left, right, (((1,), (1,)), ((), ())), preferred_element_...  24 us
    ppermute x12, waiting for transfers between devices, cross(): return lax.ppermute(x, 'dp', [(d, d ^ bit) for d in range(self.count)])  21.9 us
  transfers between devices with their start and end apart: 22, of which 7 were waited for; matrix products, arithmetic and copies ran while one was open for 11% of the time, Pallas kernels for 0%

profile of v3, /device:TPU:2, one launch (start us, length us, event | category | flops | bytes accessed | tf_op | source)
XLA Modules:
  0.0 763.3 jit_solution(15705522472233012644)
XLA Ops:
  3.6 2.3 copy.66
  7.2 2.5 broadcast_multiply_fusion.3
  11.3 276.5 %shard_map.203 = (bf16[2048,3072]{1,0:T(8,128)(2,1)}, bf16[2048,3072]{1,0:T(8,128)(2,1)}, bf16[1024,2048]{1,0:T(8,128)(2,1)}, bf16[1024,2048]{1,0:T(8,128)(2,1)}...) custom-call(bf16[128,1024]{1,0:T(8,128)(2,1)} %wq.1, ...), custom_call_target="tpu_custom_call" | custom-call | tf_op jit(solution)/shard_map/pallas_call | solution.py:436
  287.9 15.3 %fusion.3 = f32[1024,2048]{0,1:T(8,128)} fusion(bf16[1024,2048]{1,0:T(8,128)(2,1)} %get-tuple-element.33, bf16[2048,3072]{1,0:T(8,128)(2,1)} %get-tuple-element.32), kind=kOutput, calls=%fused_computation.4 | convolution fusion | flops 8589934592 | bytes 20971520 | tf_op jit(solution)/shard_map/dot_general | solution.py:23
  303.2 10.9 %multiply_convert_fusion.2 = (bf16[1024,1024]{0,1:T(8,128)(2,1)S(1)}, bf16[1024,1024]{0,1:T(8,128)(2,1)S(1)}, bf16[1024,1024]{0,1:T(8,128)(2,1)}) fusion(f32[1024,2048]{0,1:T(8,128)} %fusion.3, bf16[1024,2048]{1,0:T(8,128)(2,1)} %get-tuple-element.31, bf16[2048,3072]{1,0:T(8,128)(2,1)S(1)} %copy-done.22), kind=kOutput, calls=%fused_computation.19 | convolution fusion | flops 4310695936 | bytes 23068672 | tf_op jit(solution)/shard_map/dot_general | solution.py:23
  314.1 11.2 %fusion.1 = f32[1024,2048]{1,0:T(8,128)} fusion(bf16[2048,3072]{1,0:T(8,128)(2,1)S(1)} %copy-done.22, bf16[1024,1024]{0,1:T(8,128)(2,1)S(1)} %get-tuple-element.88, bf16[1024,1024]{0,1:T(8,128)(2,1)S(1)} %get-tuple-element.87), kind=kOutput, calls=%fused_computation.2 | convolution fusion | flops 8598323200 | bytes 20971520 | tf_op jit(solution)/shard_map/dot_general | solution.py:27
  325.3 2.5 pad_maximum_fusion
  327.8 4.0 dynamic-slice_convert_fusion
  331.7 7.0 convolution_convert_fusion.4
  342.8 2.5 collective-permute-start.20
  348.4 12.2 %convolution_convert_fusion = bf16[2048,2048]{1,0:T(8,128)(2,1)S(1)} fusion(bf16[1024,2048]{1,0:T(8,128)(2,1)} %get-tuple-element.33, bf16[1024,2048]{0,1:T(8,128)(2,1)} %pad_maximum_fusion), kind=kOutput, calls=%fused_computation.1 | convolution fusion | flops 8594128896 | bytes 16777216 | tf_op jit(solution)/shard_map/dot_general | solution.py:31
  360.6 2.3 fusion.75
  366.6 9.4 %fusion.12 = f32[1024,2048]{1,0:T(8,128)} fusion(bf16[1024,1024]{0,1:T(8,128)(2,1)S(1)} %copy-done.25, bf16[2048,3072]{1,0:T(8,128)(2,1)} %get-tuple-element.32), kind=kOutput, calls=%fused_computation.26 | convolution fusion | flops 4294967296 | bytes 14680064 | tf_op jit(solution)/shard_map/dot_general | solution.py:27
  379.6 2.9 fusion.81
  382.5 3.2 dynamic-slice_bitcast_fusion.3
  389.9 3.8 dynamic-slice_convert_fusion.1
  409.0 16.6 %collective-permute-done.11 = bf16[2,128,2048]{2,1,0:T(8,128)(2,1)} collective-permute-done((bf16[2,128,2048]{2,1,0:T(8,128)(2,1)}, bf16[2,128,2048]{2,1,0:T(8,128)(2,1)}, u32[]{:S(2)}, u32[]{:S(2)}) %collective-permute-start.11) | collective-permute-done | bytes 1048608 | tf_op jit(solution)/shard_map/ppermute | solution.py:69
  429.4 3.7 convert_add_fusion
  433.4 3.3 collective-permute-done.16
  436.7 4.7 collective-permute-start.7
  443.4 5.3 collective-permute-start.5
  449.0 2.8 convert_add_fusion.1
  455.8 28.7 %collective-permute-done.6 = bf16[256,1024]{1,0:T(8,128)(2,1)S(1)} collective-permute-done((bf16[256,1024]{1,0:T(8,128)(2,1)S(1)}, bf16[256,1024]{1,0:T(8,128)(2,1)S(1)}, u32[]{:S(2)}, u32[]{:S(2)}) %collective-permute-start.6) | collective-permute-done | bytes 524320 | tf_op jit(solution)/shard_map/ppermute | solution.py:66
  492.5 10.3 %collective-permute-done.3 = bf16[256,1024]{1,0:T(8,128)(2,1)S(1)} collective-permute-done((bf16[256,1024]{1,0:T(8,128)(2,1)S(1)}, bf16[256,1024]{1,0:T(8,128)(2,1)S(1)}, u32[]{:S(2)}, u32[]{:S(2)}) %collective-permute-start.3) | collective-permute-done | bytes 524320 | tf_op jit(solution)/shard_map/ppermute | solution.py:66
  502.9 32.1 %collective-permute-done.2 = bf16[256,1024]{1,0:T(8,128)(2,1)S(1)} collective-permute-done((bf16[256,1024]{1,0:T(8,128)(2,1)S(1)}, bf16[256,1024]{1,0:T(8,128)(2,1)S(1)}, u32[]{:S(2)}, u32[]{:S(2)}) %collective-permute-start.2) | collective-permute-done | bytes 524320 | tf_op jit(solution)/shard_map/ppermute | solution.py:66
  540.4 4.4 fusion.28
  553.7 3.3 convolution_convert_fusion.3.gq
  558.4 4.4 convolution_convert_fusion.1.gkv
  567.5 3.4 convolution_convert_fusion.2.go
  570.8 178.7 %shard_map.204 = (f32[128,3072]{1,0:T(8,128)}, bf16[3,128,4096]{2,1,0:T(8,128)(2,1)}, bf16[256,1024]{1,0:T(8,128)(2,1)}, f32[8,1024]{1,0:T(8,128)}) custom-call(bf16[2048,1024]{1,0:T(8,128)(2,1)} %convolution_convert_fusion.3.gq, bf16[2048,1024]{1,0:T(8,128)(2,1)} %convolution_convert_fusion.1.gkv, bf16[2048,1024]{1,0:T(8,128)(2,1)} %convolution_convert_fusion.2.go, ...), custom_call_target="tpu_custom_call" | custom-call | tf_op jit(solution)/shard_map/pallas_call | solution.py:736
  749.6 2.4 slice_bitcast_fusion.3
  758.0 2.4 slice_bitcast_fusion
  (169 shorter events, 86.6 us)
Async XLA Ops:
  0.6 10.1 %copy-start.21 = (bf16[1024]{0:T(1024)(128)(2,1)S(1)}, bf16[1024]{0:T(1024)(128)(2,1)}, u32[]{:S(2)}) copy-start(bf16[1024]{0:T(1024)(128)(2,1)} %param.16) | copy-start | bytes 6148
  287.9 15.3 %copy-start.22 = (bf16[2048,3072]{1,0:T(8,128)(2,1)S(1)}, bf16[2048,3072]{1,0:T(8,128)(2,1)}, u32[]{:S(2)}) copy-start(bf16[2048,3072]{1,0:T(8,128)(2,1)} %get-tuple-element.32) | copy-start | bytes 37748740
  331.7 97.6 %collective-permute-start.4 = (bf16[1024,1024]{1,0:T(8,128)(2,1)}, bf16[1024,1024]{1,0:T(8,128)(2,1)}, u32[]{:S(2)}, u32[]{:S(2)}) collective-permute-start(bf16[1024,1024]{1,0:T(8,128)(2,1)} %dynamic-slice_convert_fusion), channel_id=1, source_target_pairs={{0,1},{1,0},{2,3},{3,2},{4,5},{5,4},{6,7},{7,6},{8,9},{9,8},{10,11... | collective-permute-start | bytes 6291464 | tf_op jit(solution)/shard_map/ppermute | solution.py:72
  342.8 43.0 %collective-permute-start.20 = (bf16[2,128,1024]{2,1,0:T(8,128)(2,1)}, bf16[2,128,1024]{2,1,0:T(8,128)(2,1)}, u32[]{:S(2)}, u32[]{:S(2)}) collective-permute-start(bf16[2,128,1024]{2,1,0:T(8,128)(2,1)} %get-tuple-element.110), channel_id=1, source_target_pairs={{0,4},{2,6},{4,0},{6,2},{8,12},{10,14},{12,8},{14,10},{16,20},{18,... | collective-permute-start | bytes 1572872 | tf_op jit(solution)/shard_map/ppermute | solution.py:69
  345.3 48.5 %collective-permute-start.19 = (bf16[2,128,1024]{2,1,0:T(8,128)(2,1)}, bf16[2,128,1024]{2,1,0:T(8,128)(2,1)}, u32[]{:S(2)}, u32[]{:S(2)}) collective-permute-start(bf16[2,128,1024]{2,1,0:T(8,128)(2,1)} %get-tuple-element.109), channel_id=1, source_target_pairs={{0,4},{2,6},{4,0},{6,2},{8,12},{10,14},{12,8},{14,10},{16,20},{18,... | collective-permute-start | bytes 1572872 | tf_op jit(solution)/shard_map/ppermute | solution.py:69
  346.4 47.4 %collective-permute-start.17 = (bf16[2,128,1024]{2,1,0:T(8,128)(2,1)}, bf16[2,128,1024]{2,1,0:T(8,128)(2,1)}, u32[]{:S(2)}, u32[]{:S(2)}) collective-permute-start(bf16[2,128,1024]{2,1,0:T(8,128)(2,1)} %get-tuple-element.108), channel_id=1, source_target_pairs={{0,2},{2,0},{4,6},{6,4},{8,10},{10,8},{12,14},{14,12},{16,18},{18,... | collective-permute-start | bytes 1572872 | tf_op jit(solution)/shard_map/ppermute | solution.py:69
  366.6 40.4 %collective-permute-start.14 = (bf16[2,128,2048]{2,1,0:T(8,128)(2,1)}, bf16[2,128,2048]{2,1,0:T(8,128)(2,1)}, u32[]{:S(2)}, u32[]{:S(2)}) collective-permute-start(bf16[2,128,2048]{2,1,0:T(8,128)(2,1)} %get-tuple-element.98), channel_id=1, source_target_pairs={{0,4},{2,6},{4,0},{6,2},{8,12},{10,14},{12,8},{14,10},{16,20},{18,... | collective-permute-start | bytes 3145736 | tf_op jit(solution)/shard_map/ppermute | solution.py:69
  382.5 11.4 %copy-start.4 = (f32[448,256]{1,0:T(8,128)S(1)}, f32[448,256]{1,0:T(8,128)}, u32[]{:S(2)}) copy-start(f32[448,256]{1,0:T(8,128)} %get-tuple-element.124.sin) | copy-start | bytes 1376260
  382.5 11.4 %copy-start.5 = (f32[448,256]{1,0:T(8,128)S(1)}, f32[448,256]{1,0:T(8,128)}, u32[]{:S(2)}) copy-start(f32[448,256]{1,0:T(8,128)} %get-tuple-element.125.cos) | copy-start | bytes 1376260
  387.9 15.3 %collective-permute-start.21 = (bf16[2,128,1024]{2,1,0:T(8,128)(2,1)}, bf16[2,128,1024]{2,1,0:T(8,128)(2,1)}, u32[]{:S(2)}, u32[]{:S(2)}) collective-permute-start(bf16[2,128,1024]{2,1,0:T(8,128)(2,1)} %fusion.34), channel_id=1, source_target_pairs={{0,2},{2,0},{4,6},{6,4},{8,10},{10,8},{12,14},{14,12},{16,18},{18,... | collective-permute-start | bytes 1572872 | tf_op jit(solution)/shard_map/ppermute | solution.py:69
  393.8 49.6 %collective-permute-start = (bf16[1024,1024]{1,0:T(8,128)(2,1)}, bf16[1024,1024]{1,0:T(8,128)(2,1)}, u32[]{:S(2)}, u32[]{:S(2)}) collective-permute-start(bf16[1024,1024]{1,0:T(8,128)(2,1)} %dynamic-slice_convert_fusion.1), channel_id=1, source_target_pairs={{0,1},{1,0},{2,3},{3,2},{4,5},{5,4},{6,7},{7,6},{8,9},{9,8},{10,11... | collective-permute-start | bytes 6291464 | tf_op jit(solution)/shard_map/ppermute | solution.py:72
  393.8 31.8 %collective-permute-start.11 = (bf16[2,128,2048]{2,1,0:T(8,128)(2,1)}, bf16[2,128,2048]{2,1,0:T(8,128)(2,1)}, u32[]{:S(2)}, u32[]{:S(2)}) collective-permute-start(bf16[2,128,2048]{2,1,0:T(8,128)(2,1)} %get-tuple-element.96), channel_id=1, source_target_pairs={{0,2},{2,0},{4,6},{6,4},{8,10},{10,8},{12,14},{14,12},{16,18},{18,... | collective-permute-start | bytes 3145736 | tf_op jit(solution)/shard_map/ppermute | solution.py:69
  401.8 25.7 %copy-start = (bf16[1024,2048]{1,0:T(8,128)(2,1)S(1)}, bf16[1024,2048]{1,0:T(8,128)(2,1)}, u32[]{:S(2)}) copy-start(bf16[1024,2048]{1,0:T(8,128)(2,1)} %get-tuple-element.89) | copy-start | bytes 12582916
  403.2 33.4 %collective-permute-start.16 = (bf16[2,128,1024]{2,1,0:T(8,128)(2,1)}, bf16[2,128,1024]{2,1,0:T(8,128)(2,1)S(1)}, u32[]{:S(2)}, u32[]{:S(2)}) collective-permute-start(bf16[2,128,1024]{2,1,0:T(8,128)(2,1)} %get-tuple-element.107), channel_id=1, source_target_pairs={{0,2},{2,0},{4,6},{6,4},{8,10},{10,8},{12,14},{14,12},{16,18},{18,... | collective-permute-start | bytes 1572872 | tf_op jit(solution)/shard_map/ppermute | solution.py:69
  406.9 80.4 %collective-permute-start.13 = (bf16[2,128,2048]{2,1,0:T(8,128)(2,1)}, bf16[2,128,2048]{2,1,0:T(8,128)(2,1)S(1)}, u32[]{:S(2)}, u32[]{:S(2)}) collective-permute-start(bf16[2,128,2048]{2,1,0:T(8,128)(2,1)} %get-tuple-element.97), channel_id=1, source_target_pairs={{0,4},{2,6},{4,0},{6,2},{8,12},{10,14},{12,8},{14,10},{16,20},{18,... | collective-permute-start | bytes 3145736 | tf_op jit(solution)/shard_map/ppermute | solution.py:69
  425.5 17.9 %collective-permute-start.18 = (bf16[2,128,1024]{2,1,0:T(8,128)(2,1)S(1)}, bf16[2,128,1024]{2,1,0:T(8,128)(2,1)S(1)}, u32[]{:S(2)}, u32[]{:S(2)}) collective-permute-start(bf16[2,128,1024]{2,1,0:T(8,128)(2,1)S(1)} %fusion.37), channel_id=1, source_target_pairs={{0,4},{2,6},{4,0},{6,2},{8,12},{10,14},{12,8},{14,10},{16,20},{18,... | collective-permute-start | bytes 1572872 | tf_op jit(solution)/shard_map/ppermute | solution.py:69
  427.6 21.4 %slice-start = ((s8[8388608]{0:T(1024)(128)(4,1)}), s8[4194304]{0:T(1024)(128)(4,1)S(1)}, s32[]{:S(2)}) async-start(s8[8388608]{0:T(1024)(128)(4,1)} %bitcast.145), calls=%async_computation | async-start | bytes 8388608
  429.3 19.6 %slice-start.1 = ((s8[8388608]{0:T(1024)(128)(4,1)}), s8[4194304]{0:T(1024)(128)(4,1)S(1)}, s32[]{:S(2)}) async-start(s8[8388608]{0:T(1024)(128)(4,1)} %bitcast.145), calls=%async_computation.1 | async-start | bytes 8388608
  429.4 58.0 %collective-permute-start.15 = (bf16[2,128,2048]{2,1,0:T(8,128)(2,1)S(1)}, bf16[2,128,2048]{2,1,0:T(8,128)(2,1)S(1)}, u32[]{:S(2)}, u32[]{:S(2)}) collective-permute-start(bf16[2,128,2048]{2,1,0:T(8,128)(2,1)S(1)} %fusion.18), channel_id=1, source_target_pairs={{0,2},{2,0},{4,6},{6,4},{8,10},{10,8},{12,14},{14,12},{16,18},{18,... | collective-permute-start | bytes 3145736 | tf_op jit(solution)/shard_map/ppermute | solution.py:69
  436.7 17.1 %collective-permute-start.7 = (bf16[256,1024]{1,0:T(8,128)(2,1)S(1)}, bf16[256,1024]{1,0:T(8,128)(2,1)S(1)}, u32[]{:S(2)}, u32[]{:S(2)}) collective-permute-start(bf16[256,1024]{1,0:T(8,128)(2,1)S(1)} %get-tuple-element.102), channel_id=1, source_target_pairs={{0,24},{2,26},{4,28},{6,30},{8,0},{10,2},{12,4},{14,6},{16,8},{18,... | collective-permute-start | bytes 1572872 | tf_op jit(solution)/shard_map/ppermute | solution.py:66
  443.4 41.1 %collective-permute-start.6 = (bf16[256,1024]{1,0:T(8,128)(2,1)S(1)}, bf16[256,1024]{1,0:T(8,128)(2,1)S(1)}, u32[]{:S(2)}, u32[]{:S(2)}) collective-permute-start(bf16[256,1024]{1,0:T(8,128)(2,1)S(1)} %get-tuple-element.103), channel_id=1, source_target_pairs={{0,16},{2,18},{4,20},{6,22},{8,24},{10,26},{12,28},{14,30},{16,0},... | collective-permute-start | bytes 1572872 | tf_op jit(solution)/shard_map/ppermute | solution.py:66
  443.4 42.5 %collective-permute-start.5 = (bf16[256,1024]{1,0:T(8,128)(2,1)S(1)}, bf16[256,1024]{1,0:T(8,128)(2,1)S(1)}, u32[]{:S(2)}, u32[]{:S(2)}) collective-permute-start(bf16[256,1024]{1,0:T(8,128)(2,1)S(1)} %get-tuple-element.101), channel_id=1, source_target_pairs={{0,8},{2,10},{4,12},{6,14},{8,16},{10,18},{12,20},{14,22},{16,24},... | collective-permute-start | bytes 1572872 | tf_op jit(solution)/shard_map/ppermute | solution.py:66
  449.0 36.9 %copy-start.2 = (f32[256,1024]{1,0:T(8,128)S(1)}, f32[256,1024]{1,0:T(8,128)}, u32[]{:S(2)}) copy-start(f32[256,1024]{1,0:T(8,128)} %get-tuple-element.30) | copy-start | bytes 3145732
  449.0 36.9 %copy-start.20 = (f32[1024]{0:T(1024)S(1)}, f32[1024]{0:T(1024)}, u32[]{:S(2)}) copy-start(f32[1024]{0:T(1024)} %convert_element_type.231) | copy-start | bytes 12292
  453.8 83.1 %collective-permute-start.10 = (bf16[2,128,2048]{2,1,0:T(8,128)(2,1)S(1)}, bf16[2,128,2048]{2,1,0:T(8,128)(2,1)S(1)}, u32[]{:S(2)}, u32[]{:S(2)}) collective-permute-start(bf16[2,128,2048]{2,1,0:T(8,128)(2,1)S(1)} %copy-done.11), channel_id=1, source_target_pairs={{0,2},{2,0},{4,6},{6,4},{8,10},{10,8},{12,14},{14,12},{16,18},{18,... | collective-permute-start | bytes 3145736 | tf_op jit(solution)/shard_map/ppermute | solution.py:69
  484.5 52.4 %collective-permute-start.12 = (bf16[2,128,2048]{2,1,0:T(8,128)(2,1)S(1)}, bf16[2,128,2048]{2,1,0:T(8,128)(2,1)S(1)}, u32[]{:S(2)}, u32[]{:S(2)}) collective-permute-start(bf16[2,128,2048]{2,1,0:T(8,128)(2,1)S(1)} %fusion.21), channel_id=1, source_target_pairs={{0,4},{2,6},{4,0},{6,2},{8,12},{10,14},{12,8},{14,10},{16,20},{18,... | collective-permute-start | bytes 3145736 | tf_op jit(solution)/shard_map/ppermute | solution.py:69
  487.1 48.0 %copy-start.6 = (bf16[256,1024]{1,0:T(8,128)(2,1)S(1)}, bf16[256,1024]{1,0:T(8,128)(2,1)}, u32[]{:S(2)}) copy-start(bf16[256,1024]{1,0:T(8,128)(2,1)} %cot.1) | copy-start | bytes 1572868
  487.1 1.8 collective-permute-start.8
  487.3 15.6 %collective-permute-start.3 = (bf16[256,1024]{1,0:T(8,128)(2,1)S(1)}, bf16[256,1024]{1,0:T(8,128)(2,1)S(1)}, u32[]{:S(2)}, u32[]{:S(2)}) collective-permute-start(bf16[256,1024]{1,0:T(8,128)(2,1)S(1)} %get-tuple-element.105), channel_id=1, source_target_pairs={{0,24},{2,26},{4,28},{6,30},{8,0},{10,2},{12,4},{14,6},{16,8},{18,... | collective-permute-start | bytes 1572872 | tf_op jit(solution)/shard_map/ppermute | solution.py:66
  487.4 47.6 %collective-permute-start.2 = (bf16[256,1024]{1,0:T(8,128)(2,1)S(1)}, bf16[256,1024]{1,0:T(8,128)(2,1)S(1)}, u32[]{:S(2)}, u32[]{:S(2)}) collective-permute-start(bf16[256,1024]{1,0:T(8,128)(2,1)S(1)} %get-tuple-element.106), channel_id=1, source_target_pairs={{0,16},{2,18},{4,20},{6,22},{8,24},{10,26},{12,28},{14,30},{16,0},... | collective-permute-start | bytes 1572872 | tf_op jit(solution)/shard_map/ppermute | solution.py:66
  488.8 46.2 %collective-permute-start.1 = (bf16[256,1024]{1,0:T(8,128)(2,1)S(1)}, bf16[256,1024]{1,0:T(8,128)(2,1)S(1)}, u32[]{:S(2)}, u32[]{:S(2)}) collective-permute-start(bf16[256,1024]{1,0:T(8,128)(2,1)S(1)} %get-tuple-element.104), channel_id=1, source_target_pairs={{0,8},{2,10},{4,12},{6,14},{8,16},{10,18},{12,20},{14,22},{16,24},... | collective-permute-start | bytes 1572872 | tf_op jit(solution)/shard_map/ppermute | solution.py:66
  536.9 2.5 collective-permute-start.9
  (21 other events, 60.0 us)
